TPU v7x, 32 devices: a whole 2x2x4 slice. The times are simulated.
32 devices in a mesh: group: 2 (over y), head: 4 (over z), cache: 4 (over x, core).
Axes of the slice: x: 2, y: 2, z: 4, core: 2. Of those that a mesh axis runs over, the one named last changes fastest.
Arguments:
- queries: bfloat16 [512, 4096], P(('group', 'head')), parts along dimension 0, may hold values from -8 to 8
- keys: bfloat16 [256, 128, 4096], P(('group', 'cache'), None, 'head'), parts along dimension 0, may hold values from -8 to 8
- values: bfloat16 [256, 128, 4096], P(('group', 'cache'), None, 'head'), parts along dimension 0, may hold values from -6 to 6
- page_lists: int32 [8, 32], P(('group', 'cache')), parts along dimension 0, may hold values from 0 to 31, as said below
- page_counts: int32 [8], P(('group', 'cache')), parts along dimension 0, may hold values from 1 to 32, as said below
Outputs:
- attended: float32 [512, 4096], P(('group', 'head', 'cache')), parts along dimension 0
- log_sums: float32 [512, 32], P(('group', 'head', 'cache')), parts along dimension 0
There are 2 independent parts, one for each index of `group`. A program takes and returns all parts, laid end to end along the dimension named above; each array names one. Nothing has to cross between parts.
Inputs may be any that keep to these rules, and one draw needn't show every extreme that they name: `page_lists`: row c holds 32 distinct page ids of owner c's pool; only its first page_counts[c] entries are attended. `page_counts`: some owner lists exactly 32 pages in every draw.
All inputs are finite; a program needn't handle non-finite values.
Results may differ from a plain program's by a relative error of at most 0.00038.
Values may be sent and summed in bfloat16 or wider, within the bound.
No kernel may reach another device: no remote copies, remote signals or barrier semaphores. Data moves between devices by JAX's collectives and lax.ppermute only.
A program may use at most 64 MiB of HBM per device.

v0:
```python
import math

import jax
import jax.numpy as jnp
from jax import lax
from jax.sharding import PartitionSpec as P

HEADS = 32
DH = 128
PAGE = 128


lowest = -1e30


def combined_all(value, axis, join):
    pieces = jax.tree.map(lambda part: lax.all_gather(part, axis), value)
    head = jax.tree.map(lambda part: part[0], pieces)
    tail = jax.tree.map(lambda part: part[1:], pieces)
    so_far, _ = lax.scan(lambda so_far, share: (join(so_far, share), None), head, tail)
    return so_far


def join_states(first, second):
    best_first, total_first, accum_first = first
    best_second, total_second, accum_second = second
    top = jnp.maximum(best_first, best_second)
    keep_first = jnp.exp(best_first - top)
    keep_second = jnp.exp(best_second - top)
    total = total_first * keep_first + total_second * keep_second
    accum = accum_first * keep_first[..., None] + accum_second * keep_second[..., None]
    return (top, total, accum)


def on_device(queries, keys, values, page_lists, page_counts):
    n_head = lax.axis_size("head")
    n_cache = lax.axis_size("cache")
    tok_local = queries.shape[0]
    local_heads = keys.shape[2] // DH
    all_tok = tok_local * n_head
    share = all_tok // (n_head * n_cache)
    score_scale = 1.0 / math.sqrt(DH)
    moved = lax.all_to_all(
        queries.reshape(tok_local, n_head, local_heads * DH),
        "head",
        split_axis=1,
        concat_axis=0,
        tiled=True,
    )
    query_heads = moved.reshape(all_tok, local_heads, DH)
    pool_keys = keys.reshape(keys.shape[0], PAGE, local_heads, DH)
    pool_values = values.reshape(values.shape[0], PAGE, local_heads, DH)
    listed = page_lists[0]
    count = page_counts[0]
    blocks = (count + 3) // 4

    def visit_block(block, state):
        best, total, accum = state
        first = block * 4
        page_ids = lax.dynamic_slice_in_dim(listed, first, 4)
        usable = first + jnp.arange(4, dtype=jnp.int32) < count
        key_block = pool_keys[page_ids]
        value_block = pool_values[page_ids]
        scores = (
            jnp.einsum("thd,pkhd->thpk", query_heads, key_block, preferred_element_type=jnp.float32)
            * score_scale
        )
        page_max = jnp.max(scores, axis=-1)
        weights = jnp.exp(scores - page_max[..., None]).astype(jnp.bfloat16)
        page_sum = jnp.sum(weights, axis=-1, dtype=jnp.float32)
        page_out = jnp.einsum(
            "thpk,pkhd->thpd", weights, value_block, preferred_element_type=jnp.float32
        )
        used_max = jnp.where(usable[None, None, :], page_max, lowest)
        running = jnp.maximum(best, jnp.max(used_max, axis=-1))
        fresh = jnp.exp(used_max - running[..., None])
        keep = jnp.exp(best - running)
        total = total * keep + jnp.sum(fresh * page_sum, axis=-1)
        accum = accum * keep[..., None] + jnp.sum(fresh[..., None] * page_out, axis=2)
        return (running, total, accum)

    start = (
        jnp.full((all_tok, local_heads), lowest, jnp.float32),
        jnp.zeros((all_tok, local_heads), jnp.float32),
        jnp.zeros((all_tok, local_heads, DH), jnp.float32),
    )
    best, total, accum = lax.fori_loop(0, blocks, visit_block, start)
    position = lax.axis_index("cache")
    best, total, accum = combined_all((best, total, accum), "cache", join_states)
    result = accum / total[..., None]
    logged = best + jnp.log(total)
    result = lax.dynamic_index_in_dim(
        result.reshape(n_head, n_cache, share, local_heads, DH), position, 1, keepdims=False
    )
    logged = lax.dynamic_index_in_dim(
        logged.reshape(n_head, n_cache, share, local_heads), position, 1, keepdims=False
    )
    result, logged = (
        lax.all_to_all(result, "head", split_axis=0, concat_axis=2, tiled=True),
        lax.all_to_all(logged, "head", split_axis=0, concat_axis=2, tiled=True),
    )
    return (result.reshape(share, HEADS * DH), logged.reshape(share, HEADS))


def solution(mesh):
    in_specs = (
        P(("group", "head"), None),
        P(("group", "cache"), None, "head"),
        P(("group", "cache"), None, "head"),
        P(("group", "cache"), None),
        P(("group", "cache")),
    )
    out_specs = (P(("group", "head", "cache"), None), P(("group", "head", "cache"), None))
    return jax.shard_map(
        on_device, mesh=mesh, in_specs=in_specs, out_specs=out_specs, check_vma=False
    )
```

profile of v0, /device:TPU:0, one launch (start us, length us, event | category | flops | bytes accessed | tf_op | source)
XLA Modules:
  0.0 244.6 jit_solution(14165468163173509033)
XLA Ops:
  7.2 1.9 copy.70
  9.0 6.3 %all-to-all-start = ((bf16[64,4,1024]{2,0,1:T(8,128)(2,1)}), bf16[64,4,1024]{2,0,1:T(8,128)(2,1)S(1)}, u32[]{:S(2)}, u32[]{:S(2)}) async-start(bf16[64,4,1024]{2,0,1:T(8,128)(2,1)} %bitcast.86), calls=%async_computation | async-start | bytes 1048576 | tf_op jit(solution)/shard_map/all_to_all | solution.py:43
  16.0 8.8 %copy.57 = bf16[512,8,8,128]{3,2,1,0:T(8,128)(2,1)} copy(bf16[512,8,8,128]{3,1,2,0:T(8,128)(2,1)} %bitcast.107) | data formatting | bytes 16777216
  24.8 8.8 %copy.59 = bf16[512,8,8,128]{3,2,1,0:T(8,128)(2,1)} copy(bf16[512,8,8,128]{3,1,2,0:T(8,128)(2,1)} %bitcast.108) | data formatting | bytes 16777216
  33.6 0.1 copy.58
  33.7 0.1 copy.46
  33.8 0.1 broadcast_in_dim.35
  33.9 16.7 %while.28 = (s32[]{:T(128)}, f32[256,8]{0,1:T(8,128)S(1)}, f32[256,8]{0,1:T(8,128)S(1)}, f32[256,8,128]{0,2,1:T(8,128)S(1)}, s32[]{:T(128)}, /*index=5*/s32[]{:T...) while((s32[]{:T(128)}, f32[256,8]{0,1:T(8,128)S(1)}, ...), condition=%wide.region_6.7_spmd, body=%wide.region_0.6_spmd.sunk | while | flops 549753856 | bytes 40792384 | solution.py:87
  33.9 0.1 compare_select_fusion.2
  34.0 4.1 %gather_fusion = bf16[4,128,8,128]{3,2,1,0:T(8,128)(2,1)S(1)} fusion(bf16[32,128,8,128]{3,2,1,0:T(8,128)(2,1)} %get-tuple-element.342, s32[1024]{0:T(1024)S(1)} %pad_clamp_fusion.2), kind=kCustom, calls=%fused_computation.clone.1 | custom fusion | bytes 2097168 | tf_op jit(solution)/shard_map/while/body/gather | solution.py:62
  38.1 0.7 bitcast_reduce_fusion.2
  38.9 1.9 copy-done
  40.8 0.8 convert_reduce_fusion.2
  41.6 0.7 add_compare_fusion.2
  42.3 0.1 select_reduce_fusion.2
  42.4 0.1 multiply_reduce_fusion.2
  42.5 4.1 %gather_fusion.1 = bf16[4,128,8,128]{3,2,1,0:T(8,128)(2,1)S(1)} fusion(bf16[32,128,8,128]{3,2,1,0:T(8,128)(2,1)} %get-tuple-element.344, s32[1024]{0:T(1024)S(1)} %pad_clamp_fusion.2), kind=kCustom, calls=%fused_computation.1.clone.1 | custom fusion | bytes 2097168 | tf_op jit(solution)/shard_map/while/body/gather | solution.py:63
  46.7 3.5 %fusion.21 = f32[256,8,128]{0,2,1:T(8,128)S(1)} fusion(f32[256,8,4]{0,2,1:T(4,128)S(1)} %get-tuple-element.294, bf16[4,128,8,128]{3,2,1,0:T(8,128)(2,1)S(1)} %gather_fusion.1, f32[8,4,128,256]{3,2,1,0:T(8,128)} %copy-done, f32[256,8,4]{0,2,1:T(4,128)S(1)} %get-tuple-element.290), kind=kOutput, calls=%fused_computation.11.clone.1 | convolution fusion | flops 273416192 | bytes 6356992 | tf_op jit(solution)/shard_map/while/body/thpk,pkhd->thpd/dot_general | solution.py:71
  50.1 0.4 multiply_add_fusion.5
  50.6 1.3 copy.47
  51.9 120.3 %all-gather = f32[1024,8]{0,1:T(8,128)S(1)} all-gather(f32[256,8]{0,1:T(8,128)S(1)} %get-tuple-element.96), channel_id=2, replica_groups=mesh['group'=2,'head'=4,'cache'=4] {'cache'}, dimensions={0}, use_global_device_ids=true | all-gather | bytes 40960 | tf_op jit(solution)/shard_map/all_gather | solution.py:17
  172.2 5.2 %all-gather.1 = f32[1024,8]{0,1:T(8,128)S(1)} all-gather(f32[256,8]{0,1:T(8,128)S(1)} %get-tuple-element.97), channel_id=3, replica_groups=mesh['group'=2,'head'=4,'cache'=4] {'cache'}, dimensions={0}, use_global_device_ids=true | all-gather | bytes 40960 | tf_op jit(solution)/shard_map/all_gather | solution.py:17
  177.4 26.6 %all-gather.5.cloned.1.call-done = f32[1024,8,128]{2,1,0:T(8,128)} async-done(((f32[256,8,128]{2,1,0:T(8,128)}), f32[1024,8,128]{2,1,0:T(8,128)}) %all-gather.5.cloned.1.call-update) | async-done | bytes 4194320 | tf_op jit(solution)/shard_map/all_gather | solution.py:17
  204.0 3.9 %slice.39 = f32[768,8,128]{2,1,0:T(8,128)} slice(f32[1024,8,128]{2,1,0:T(8,128)} %all-gather.5.cloned.1.call-done), slice={[256:1024], [0:8], [0:128]} | slice | bytes 6291456 | tf_op jit(solution)/shard_map/slice | solution.py:19
  207.8 6.6 %while.29 = (s32[]{:T(128)}, f32[256,8]{0,1:T(8,128)S(1)}, f32[256,8]{0,1:T(8,128)S(1)}, f32[256,8,128]{2,1,0:T(8,128)S(1)}, f32[3,256,8]{1,2,0:T(8,128)S(1)}, /...) while((s32[]{:T(128)}, f32[256,8]{0,1:T(8,128)S(1)}, f32[256,8]{0,1:T(8,128)S(1)}, ...), condition=%wide.region_8.9_spmd, body=%wide.region_7.8_spmd.sunk | while | flops 798722 | bytes 3260517 | solution.py:20
  207.9 0.1 copy.78
  208.0 0.1 copy.79
  208.1 1.9 fusion.23
  210.1 0.1 copy.78
  210.2 0.1 copy.79
  210.3 1.9 fusion.23
  212.3 0.1 copy.78
  212.4 0.1 copy.79
  212.5 1.9 fusion.23
  214.4 0.1 copy.48
  214.6 0.1 reshape.53
  214.7 0.7 reshape.86
  215.4 4.6 %all-to-all-start.2 = ((f32[4,1,128]{2,1,0:T(1,128)}), f32[4,1,128]{2,1,0:T(1,128)S(1)}, u32[]{:S(2)}, u32[]{:S(2)}) async-start(f32[4,1,128]{2,1,0:T(1,128)} %reshape.86), calls=%async_computation.2 | async-start | bytes 4096 | tf_op jit(solution)/shard_map/all_to_all | solution.py:100
  220.0 0.3 broadcast_divide_fusion
  220.3 0.7 dynamic-slice_bitcast_fusion
  221.1 4.4 %all-to-all-done.2 = f32[4,1,128]{2,1,0:T(1,128)S(1)} async-done(((f32[4,1,128]{2,1,0:T(1,128)}), f32[4,1,128]{2,1,0:T(1,128)S(1)}, u32[]{:S(2)}, u32[]{:S(2)}) %all-to-all-start.2) | async-done | bytes 2080 | tf_op jit(solution)/shard_map/all_to_all | solution.py:100
  225.5 3.4 %all-to-all-start.1 = ((f32[4,16,8,128]{3,2,1,0:T(8,128)}), f32[4,16,8,128]{3,2,1,0:T(8,128)S(1)}, u32[]{:S(2)}, u32[]{:S(2)}) async-start(f32[4,16,8,128]{3,2,1,0:T(8,128)} %dynamic-slice_bitcast_fusion), calls=%async_computation.1 | async-start | bytes 524288 | tf_op jit(solution)/shard_map/all_to_all | solution.py:99
  228.9 0.5 broadcast.51
  229.4 0.7 reduce
  230.0 0.1 reshape.87
  230.1 0.7 copy.52
  230.8 6.2 %all-to-all-done.1 = f32[4,16,8,128]{3,2,1,0:T(8,128)S(1)} async-done(((f32[4,16,8,128]{3,2,1,0:T(8,128)}), f32[4,16,8,128]{3,2,1,0:T(8,128)S(1)}, u32[]{:S(2)}, u32[]{:S(2)}) %all-to-all-start.1) | async-done | bytes 262176 | tf_op jit(solution)/shard_map/all_to_all | solution.py:99
  237.0 0.8 reshape.52
  (26 shorter events, 0.2 us)
Async XLA Ops:
  9.0 24.5 %all-to-all-start = ((bf16[64,4,1024]{2,0,1:T(8,128)(2,1)}), bf16[64,4,1024]{2,0,1:T(8,128)(2,1)S(1)}, u32[]{:S(2)}, u32[]{:S(2)}) async-start(bf16[64,4,1024]{2,0,1:T(8,128)(2,1)} %bitcast.86), calls=%async_computation | async-start | bytes 1048576 | tf_op jit(solution)/shard_map/all_to_all | solution.py:43
  15.3 188.6 %all-gather.5.cloned.1.call-start = ((), (), s32[]{:S(2)}) async-start(), calls=%async_computation.3 | async-start | bytes 5242880 | tf_op jit(solution)/shard_map/all_gather | solution.py:17
  24.8 9.1 %copy-start.1 = (s32[1,32]{1,0:T(1,128)S(1)}, s32[1,32]{1,0:T(1,128)}, u32[]{:S(2)}) copy-start(s32[1,32]{1,0:T(1,128)} %param.12) | copy-start | bytes 388
  38.8 1.9 copy-start
  204.0 3.9 %slice-start = ((f32[1024,8,128]{2,1,0:T(8,128)}), f32[256,8,128]{2,1,0:T(8,128)S(1)}, s32[]{:S(2)}) async-start(f32[1024,8,128]{2,1,0:T(8,128)} %all-gather.5.cloned.1.call-done), calls=%async_computation.4 | async-start | bytes 2097152 | tf_op jit(solution)/shard_map/slice | solution.py:18
  215.4 10.1 %all-to-all-start.2 = ((f32[4,1,128]{2,1,0:T(1,128)}), f32[4,1,128]{2,1,0:T(1,128)S(1)}, u32[]{:S(2)}, u32[]{:S(2)}) async-start(f32[4,1,128]{2,1,0:T(1,128)} %reshape.86), calls=%async_computation.2 | async-start | bytes 4096 | tf_op jit(solution)/shard_map/all_to_all | solution.py:100
  225.5 11.6 %all-to-all-start.1 = ((f32[4,16,8,128]{3,2,1,0:T(8,128)}), f32[4,16,8,128]{3,2,1,0:T(8,128)S(1)}, u32[]{:S(2)}, u32[]{:S(2)}) async-start(f32[4,16,8,128]{3,2,1,0:T(8,128)} %dynamic-slice_bitcast_fusion), calls=%async_computation.1 | async-start | bytes 524288 | tf_op jit(solution)/shard_map/all_to_all | solution.py:99
Sparse Core Ops, SparseCore 0:
  52.0 151.9 all-gather.4
where the time goes:
time: 246 us; the launch traced here: 245 us
  blocking collectives  125 us (51%)
  local copies, waits for them, and re-layouts  39.5 us (16%)
  waiting for transfers between devices  37.2 us (15%)
  between operations  14.8 us (6%)
  starting transfers between devices  14.3 us (6%)
  other arithmetic  8.95 us (4%)
  matrix products  4.2 us (2%)
    all_gather x2, blocking collectives, combined_all(): pieces = jax.tree.map(lambda part: lax.all_gather(part, axis), value)  125 us
    all_gather x1, waiting for transfers between devices, combined_all(): pieces = jax.tree.map(lambda part: lax.all_gather(part, axis), value)  26.6 us
    unnamed x8, local copies, waits for them, and re-layouts  19.1 us
    all_to_all x1, starting transfers between devices, on_device(): lax.all_to_all(queries.reshape(tok_local, n_head, local_heads * DH), 'hea...  6.32 us
    all_to_all x1, waiting for transfers between devices, on_device(): lax.all_to_all(result, 'head', split_axis=0, concat_axis=2, tiled=True)  6.2 us
    add x3, other arithmetic, join_states(): accum_first * keep_first[..., None] + accum_second * keep_second[..., None]  5.68 us
  transfers between devices with their start and end apart: 4, of which 3 were waited for; matrix products, arithmetic and copies ran while one was open for 8% of the time, Pallas kernels for 0%

commit v1 on v0

v1 whole, which is shorter than its diff:
```python
import functools
import math

import jax
import jax.numpy as jnp
from jax import lax
from jax.experimental import pallas as pl
from jax.experimental.pallas import tpu as pltpu
from jax.sharding import PartitionSpec as P

HEADS = 32
DH = 128
PAGE = 128
LANES = 128
TOK_TILE = 256
VMEM_LIMIT = 50 * 2**20

lowest = -1e30
to_log2 = math.log2(math.e) / math.sqrt(DH)


def attend_kernel(n_parts, *refs):
    count_ref, listed_ref = refs[:2]
    q_refs = refs[2 : 2 + n_parts]
    k_hbm, v_hbm, keep_ref, send_ref = refs[2 + n_parts : 6 + n_parts]
    q_turned, k_pool, v_pool, stats, k_sem, v_sem = refs[6 + n_parts :]
    heads, pool = k_pool.shape[:2]
    all_tok = q_turned.shape[2]
    tile = min(all_tok, TOK_TILE)
    tiles = all_tok // tile
    half = keep_ref.shape[0]
    count = count_ref[0]
    ahead = min(heads, 2)

    def copies(h):
        columns = pl.ds(pl.multiple_of(h * DH, DH), DH)
        return (
            pltpu.make_async_copy(k_hbm.at[:, :, columns], k_pool.at[h], k_sem.at[h]),
            pltpu.make_async_copy(v_hbm.at[:, :, columns], v_pool.at[h], v_sem.at[h]),
        )

    for h in range(ahead):
        for copy in copies(h):
            copy.start()
    row = 0
    for q_ref in q_refs:
        rows = q_ref.shape[0]
        for h in range(heads):
            q_turned[h, :, row : row + rows] = q_ref[:, h * DH : (h + 1) * DH].T
        row += rows
    stats[...] = jnp.zeros_like(stats)
    ones = jnp.ones((8, PAGE), jnp.bfloat16)

    def unit(u, carry):
        h, t = u // tiles, lax.rem(u, tiles)

        @pl.when(t == 0)
        def _():
            for copy in copies(h):
                copy.wait()

            @pl.when(h + ahead < heads)
            def _():
                for copy in copies(h + ahead):
                    copy.start()

        start = pl.multiple_of(t * tile, tile)
        columns = pl.ds(start, tile)
        q_tile = q_turned[h, :, columns]
        scores, tops = [], []
        for i in range(pool):
            s = jnp.dot(k_pool[h, listed_ref[0, i]], q_tile, preferred_element_type=jnp.float32)
            scores.append(s)
            tops.append(jnp.max(s, axis=0, keepdims=True))
        used = [jnp.where(i < count, tops[i], lowest) for i in range(pool)]
        best = functools.reduce(jnp.maximum, used)
        total, accum = 0.0, 0.0
        for i in range(pool):
            weights = jnp.exp2((scores[i] - tops[i]) * to_log2).astype(jnp.bfloat16)
            turned = v_pool[h, listed_ref[0, i]].T
            page_out = jnp.dot(
                jnp.concatenate([turned, ones], axis=0),
                weights,
                preferred_element_type=jnp.float32,
            )
            fresh = jnp.exp2((used[i] - best) * to_log2)
            total = total + fresh * page_out[DH : DH + 1]
            accum = accum + fresh * page_out[:DH]
        out = (accum / total).T
        stats[pl.ds(h, 1), columns] = best * to_log2 + jnp.log2(total)
        lanes = pl.ds(pl.multiple_of(h * DH, DH), DH)
        if tiles == 1:
            keep_ref[:, lanes] = out[:half]
            send_ref[:, lanes] = out[half:]
        else:

            @pl.when(start < half)
            def _():
                keep_ref[columns, lanes] = out

            @pl.when(start >= half)
            def _():
                send_ref[pl.ds(pl.multiple_of(start - half, tile), tile), lanes] = out

        return carry

    lax.fori_loop(0, heads * tiles, unit, 0)
    for t in range(tiles):
        turned = stats[:, t * tile : (t + 1) * tile].T
        for r in range(0, tile, 8):
            row = t * tile + r
            ref = keep_ref if row < half else send_ref
            row = row if row < half else row - half
            ref[row : row + 8, heads * DH :] = turned[r : r + 8]


def attend(q_parts, keys, values, page_lists, page_counts):
    all_tok = sum(part.shape[0] for part in q_parts)
    pool = keys.shape[0]
    heads = keys.shape[2] // DH
    in_vmem = pl.BlockSpec(memory_space=pltpu.VMEM)
    in_smem = pl.BlockSpec(memory_space=pltpu.SMEM)
    anywhere = pl.BlockSpec(memory_space=pl.ANY)
    out = jax.ShapeDtypeStruct((all_tok // 2, heads * DH + LANES), jnp.float32)
    return pl.pallas_call(
        functools.partial(attend_kernel, len(q_parts)),
        in_specs=[in_smem, in_smem] + [in_vmem] * len(q_parts) + [anywhere, anywhere],
        out_specs=[in_vmem, in_vmem],
        scratch_shapes=[
            pltpu.VMEM((heads, DH, all_tok), jnp.bfloat16),
            pltpu.VMEM((heads, pool, PAGE, DH), jnp.bfloat16),
            pltpu.VMEM((heads, pool, PAGE, DH), jnp.bfloat16),
            pltpu.VMEM((LANES, all_tok), jnp.float32),
            pltpu.SemaphoreType.DMA((heads,)),
            pltpu.SemaphoreType.DMA((heads,)),
        ],
        out_shape=[out, out],
        compiler_params=pltpu.CompilerParams(vmem_limit_bytes=VMEM_LIMIT),
        name="attend",
    )(page_counts, page_lists, *q_parts, keys, values)


def merge_kernel(heads, mine_ref, theirs_ref, *out_refs):
    rows = out_refs[0].shape[0]
    for i, out_ref in enumerate(out_refs):
        part = slice(i * rows, (i + 1) * rows)
        logs = []
        for h in range(heads):
            lanes = slice(h * DH, (h + 1) * DH)
            stat = slice(heads * DH + h, heads * DH + h + 1)
            first, second = mine_ref[part, stat], theirs_ref[part, stat]
            top = jnp.maximum(first, second)
            a, b = jnp.exp2(first - top), jnp.exp2(second - top)
            both = a + b
            out_ref[:, lanes] = (mine_ref[part, lanes] * a + theirs_ref[part, lanes] * b) / both
        first, second = mine_ref[part, heads * DH :], theirs_ref[part, heads * DH :]
        top = jnp.maximum(first, second)
        both = jnp.exp2(first - top) + jnp.exp2(second - top)
        out_ref[:, heads * DH :] = top + jnp.log2(both)


def merge(mine, theirs, heads, n_out):
    out = jax.ShapeDtypeStruct((mine.shape[0] // n_out, mine.shape[1]), jnp.float32)
    return pl.pallas_call(
        functools.partial(merge_kernel, heads),
        out_shape=[out] * n_out,
        compiler_params=pltpu.CompilerParams(vmem_limit_bytes=VMEM_LIMIT),
        name="merge",
    )(mine, theirs)


def across(value, axis, size, bit):
    return lax.ppermute(value, axis, [(i, i ^ bit) for i in range(size)])


def on_device(queries, keys, values, page_lists, page_counts):
    n_head = lax.axis_size("head")
    n_cache = lax.axis_size("cache")
    tok_local = queries.shape[0]
    heads = keys.shape[2] // DH
    share = tok_local // n_cache
    bits = [1 << i for i in range(n_cache.bit_length() - 1)]
    mine = lax.dynamic_slice_in_dim(queries, lax.axis_index("cache") * share, share, 0)
    part = lax.all_to_all(
        mine.reshape(share, n_head, heads * DH), "head", split_axis=1, concat_axis=0, tiled=True
    ).reshape(n_head * share, heads * DH)
    parts = [part]
    for bit in reversed(bits):
        parts = parts + [across(part, "cache", n_cache, bit) for part in parts]
    keep, send = attend(parts, keys, values, page_lists, page_counts)
    for bit in bits:
        theirs = across(send, "cache", n_cache, bit)
        if bit != bits[-1]:
            keep, send = merge(keep, theirs, heads, 2)
        else:
            (keep,) = merge(keep, theirs, heads, 1)
    result = lax.all_to_all(
        keep.reshape(n_head, share, keep.shape[1]), "head", split_axis=0, concat_axis=0, tiled=True
    )
    attended = result[:, :, : heads * DH].transpose(1, 0, 2).reshape(share, HEADS * DH)
    logged = result[:, :, heads * DH : heads * DH + heads].transpose(1, 0, 2)
    return attended, logged.reshape(share, HEADS) * math.log(2.0)


def solution(mesh):
    in_specs = (
        P(("group", "head"), None),
        P(("group", "cache"), None, "head"),
        P(("group", "cache"), None, "head"),
        P(("group", "cache"), None),
        P(("group", "cache")),
    )
    out_specs = (P(("group", "head", "cache"), None), P(("group", "head", "cache"), None))
    return jax.shard_map(
        on_device, mesh=mesh, in_specs=in_specs, out_specs=out_specs, check_vma=False
    )
```

time: 246 us -> 61.5 us (0.25)
  blocking collectives: 125 us -> 23.9 us
  local copies, waits for them, and re-layouts: 39.5 us -> 3.2 us
  waiting for transfers between devices: 37.2 us -> 13.6 us
  Pallas kernels: 0 us -> 16 us
  between operations: 14.8 us -> 1.34 us
  starting transfers between devices: 14.3 us -> 3.27 us
  other arithmetic: 8.95 us -> 0.01 us
  matrix products: 4.2 us -> 0 us
    all_gather x2 -> x0, blocking collectives: 125 us -> none  [combined_all(): pieces = jax.tree.map(lambda part: lax.all_gather(part, axis), value)]
    all_gather x1 -> x0, waiting for transfers between devices: 26.6 us -> none  [combined_all(): pieces = jax.tree.map(lambda part: lax.all_gather(part, axis), value)]
    all_to_all x0 -> x2, blocking collectives: none -> 23.9 us  [the longest x1 12.2 us: on_device(): lax.all_to_all(mine.reshape(share, n_head, heads * DH), 'head', split_axi...]
    unnamed x8 -> x6, local copies, waits for them, and re-layouts: 19.1 us -> 2.38 us
    pallas_call x0 -> x3, Pallas kernels: none -> 16 us  [the longest x1 15.2 us: attend(): pl.pallas_call(functools.partial(attend_kernel, len(q_parts)), in_specs=[...]
    all_to_all x3 -> x0, starting transfers between devices: 14.3 us -> none  [the longest x1 6.32 us: on_device(): lax.all_to_all(queries.reshape(tok_local, n_head, local_heads * DH), 'hea...]
    ppermute x0 -> x5, waiting for transfers between devices: none -> 13.6 us  [across(): return lax.ppermute(value, axis, [(i, i ^ bit) for i in range(size)])]
    all_to_all x3 -> x0, waiting for transfers between devices: 10.6 us -> none  [the longest x1 6.2 us: on_device(): lax.all_to_all(result, 'head', split_axis=0, concat_axis=2, tiled=True)]
  transfers between devices with their start and end apart: 4 -> 5, of which waited for: 3 -> 4; matrix products, arithmetic and copies ran while one was open for 8% -> 0% of each run, Pallas kernels for 0% -> 0%
where the time goes in v1:
time: 61.5 us; the launch traced here: 61.3 us
  blocking collectives  23.9 us (39%)
  Pallas kernels  16 us (26%)
  waiting for transfers between devices  13.6 us (22%)
  starting transfers between devices  3.27 us (5%)
  local copies, waits for them, and re-layouts  3.2 us (5%)
  between operations  1.34 us (2%)
    pallas_call x1, Pallas kernels, attend(): pl.pallas_call(functools.partial(attend_kernel, len(q_parts)), in_specs=[...  15.2 us
    ppermute x5, waiting for transfers between devices, across(): return lax.ppermute(value, axis, [(i, i ^ bit) for i in range(size)])  13.6 us
    all_to_all x1, blocking collectives, on_device(): lax.all_to_all(mine.reshape(share, n_head, heads * DH), 'head', split_axi...  12.2 us
    all_to_all x1, blocking collectives, on_device(): lax.all_to_all(keep.reshape(n_head, share, keep.shape[1]), 'head', split_...  11.7 us
    ppermute x5, starting transfers between devices, across(): return lax.ppermute(value, axis, [(i, i ^ bit) for i in range(size)])  3.27 us
    unnamed x6, local copies, waits for them, and re-layouts  2.38 us
  transfers between devices with their start and end apart: 5, of which 4 were waited for; matrix products, arithmetic and copies ran while one was open for 0% of the time, Pallas kernels for 0%

profile of v1, /device:TPU:0, one launch (start us, length us, event | category | flops | bytes accessed | tf_op | source)
XLA Modules:
  0.0 61.3 jit_solution(514946893282515066)
XLA Ops:
  0.6 0.0 copy-start
  0.6 1.0 %copy-done = bf16[64,4096]{1,0:T(8,128)(2,1)S(1)} copy-done((bf16[64,4096]{1,0:T(8,128)(2,1)S(1)}, bf16[64,4096]{1,0:T(8,128)(2,1)}, u32[]{:S(2)}) %copy-start) | copy-done | bytes 524312
  1.7 12.2 %all_to_all.20 = bf16[16,4,1024]{2,0,1:T(8,128)(2,1)S(1)} all-to-all(bf16[16,4,1024]{2,0,1:T(8,128)(2,1)S(1)} %bitcast.22), channel_id=1, replica_groups=mesh['group'=2,'head'=4,'cache'=4] {'head'}, dimensions={1} | all-to-all | bytes 262144 | tf_op jit(solution)/shard_map/all_to_all | solution.py:184
  13.9 1.5 %collective-permute-start = (bf16[64,1024]{1,0:T(8,128)(2,1)S(1)}, bf16[64,1024]{1,0:T(8,128)(2,1)S(1)}, u32[]{:S(2)}, u32[]{:S(2)}) collective-permute-start(bf16[64,1024]{1,0:T(8,128)(2,1)S(1)} %bitcast.18), channel_id=1, source_target_pairs={{0,2},{1,3},{2,0},{3,1},{4,6},{5,7},{6,4},{7,5},{8,10},{9,11},{10,... | collective-permute-start | bytes 393224 | tf_op jit(solution)/shard_map/ppermute | solution.py:173
  15.4 0.0 collective-permute-start.1
  15.4 3.5 %collective-permute-done.refs_3_ = bf16[64,1024]{1,0:T(8,128)(2,1)S(1)} collective-permute-done((bf16[64,1024]{1,0:T(8,128)(2,1)S(1)}, bf16[64,1024]{1,0:T(8,128)(2,1)S(1)}, u32[]{:S(2)}, u32[]{:S(2)}) %collective-permute-start) | collective-permute-done | bytes 131104 | tf_op jit(solution)/shard_map/ppermute | solution.py:173
  18.9 0.0 collective-permute-start.2
  19.5 0.0 collective-permute-done.1.refs_4_
  19.5 0.7 %collective-permute-done.2.refs_5_ = bf16[64,1024]{1,0:T(8,128)(2,1)S(1)} collective-permute-done((bf16[64,1024]{1,0:T(8,128)(2,1)S(1)}, bf16[64,1024]{1,0:T(8,128)(2,1)S(1)}, u32[]{:S(2)}, u32[]{:S(2)}) %collective-permute-start.2) | collective-permute-done | bytes 131104 | tf_op jit(solution)/shard_map/ppermute | solution.py:173
  20.2 0.0 copy-start.1
  20.2 0.7 %copy-done.1 = s32[1,32]{1,0:T(1,128)S(1)} copy-done((s32[1,32]{1,0:T(1,128)S(1)}, s32[1,32]{1,0:T(1,128)}, u32[]{:S(2)}) %copy-start.1) | copy-done | bytes 152
  20.9 15.2 %attend.1 = (f32[128,1152]{1,0:T(8,128)S(1)}, f32[128,1152]{1,0:T(8,128)S(1)}) custom-call(s32[1]{0:T(128)S(6)} %copy.24.refs_0_, s32[1,32]{1,0:T(1,128)S(1)} %copy-done.1, bf16[64,1024]{1,0:T(8,128)(2,1)S(1)} %bitcast.20, bf16[64,1024]{1,0:T(8,128)(2,1)S(1)} %collective-permute-done.refs_3_, bf16[64,1024]{1,0:T(8,128)(2,1)S(1)} %collective-permute-done.1.refs_4_, ...), custom_call_target="tpu_custom_call" | custom-call | tf_op jit(solution)/shard_map/attend/pallas_call | solution.py:125
  36.1 0.2 collective-permute-start.3
  36.3 1.9 %collective-permute-done.3.theirs_ref = f32[128,1152]{1,0:T(8,128)S(1)} collective-permute-done((f32[128,1152]{1,0:T(8,128)S(1)}, f32[128,1152]{1,0:T(8,128)S(1)}, u32[]{:S(2)}, u32[]{:S(2)}) %collective-permute-start.3) | collective-permute-done | bytes 589856 | tf_op jit(solution)/shard_map/ppermute | solution.py:173
  38.2 0.5 merge.2
  38.7 1.6 %collective-permute-start.4 = (f32[64,1152]{1,0:T(8,128)S(1)}, f32[64,1152]{1,0:T(8,128)S(1)}, u32[]{:S(2)}, u32[]{:S(2)}) collective-permute-start(f32[64,1152]{1,0:T(8,128)S(1)} %get-tuple-element.9), channel_id=1, source_target_pairs={{0,2},{1,3},{2,0},{3,1},{4,6},{5,7},{6,4},{7,5},{8,10},{9,11},{10,... | collective-permute-start | bytes 884744 | tf_op jit(solution)/shard_map/ppermute | solution.py:173
  40.2 7.6 %collective-permute-done.4.theirs_ref = f32[64,1152]{1,0:T(8,128)S(1)} collective-permute-done((f32[64,1152]{1,0:T(8,128)S(1)}, f32[64,1152]{1,0:T(8,128)S(1)}, u32[]{:S(2)}, u32[]{:S(2)}) %collective-permute-start.4) | collective-permute-done | bytes 294944 | tf_op jit(solution)/shard_map/ppermute | solution.py:173
  47.8 0.3 merge.3
  48.1 11.7 %all_to_all.21 = f32[4,16,1152]{2,1,0:T(8,128)S(1)} all-to-all(f32[4,16,1152]{2,1,0:T(8,128)S(1)} %bitcast.17), channel_id=1, replica_groups=mesh['group'=2,'head'=4,'cache'=4] {'head'}, dimensions={0} | all-to-all | bytes 589824 | tf_op jit(solution)/shard_map/all_to_all | solution.py:197
  59.8 0.1 copy.18
  59.9 0.7 %copy.19 = f32[16,32]{1,0:T(8,128)} copy(f32[16,32]{0,1:T(8,128)S(1)} %bitcast.24) | data formatting | bytes 4096
  60.6 0.7 %copy.21 = f32[4,2,8,1024]{3,2,0,1:T(8,128)} copy(f32[4,2,8,1024]{3,2,1,0:T(8,128)S(1)} %slice_bitcast_fusion) | data formatting | bytes 524288 | tf_op jit(solution)/shard_map/reshape | solution.py:200
  (4 shorter events, 0.0 us)
Async XLA Ops:
  0.6 1.0 %copy-start = (bf16[64,4096]{1,0:T(8,128)(2,1)S(1)}, bf16[64,4096]{1,0:T(8,128)(2,1)}, u32[]{:S(2)}) copy-start(bf16[64,4096]{1,0:T(8,128)(2,1)} %param.5) | copy-start | bytes 1572868
  13.9 5.0 %collective-permute-start = (bf16[64,1024]{1,0:T(8,128)(2,1)S(1)}, bf16[64,1024]{1,0:T(8,128)(2,1)S(1)}, u32[]{:S(2)}, u32[]{:S(2)}) collective-permute-start(bf16[64,1024]{1,0:T(8,128)(2,1)S(1)} %bitcast.18), channel_id=1, source_target_pairs={{0,2},{1,3},{2,0},{3,1},{4,6},{5,7},{6,4},{7,5},{8,10},{9,11},{10,... | collective-permute-start | bytes 393224 | tf_op jit(solution)/shard_map/ppermute | solution.py:173
  15.4 4.1 %collective-permute-start.1 = (bf16[64,1024]{1,0:T(8,128)(2,1)S(1)}, bf16[64,1024]{1,0:T(8,128)(2,1)S(1)}, u32[]{:S(2)}, u32[]{:S(2)}) collective-permute-start(bf16[64,1024]{1,0:T(8,128)(2,1)S(1)} %bitcast.19), channel_id=1, source_target_pairs={{0,1},{1,0},{2,3},{3,2},{4,5},{5,4},{6,7},{7,6},{8,9},{9,8},{10,11... | collective-permute-start | bytes 393224 | tf_op jit(solution)/shard_map/ppermute | solution.py:173
  18.9 1.3 %collective-permute-start.2 = (bf16[64,1024]{1,0:T(8,128)(2,1)S(1)}, bf16[64,1024]{1,0:T(8,128)(2,1)S(1)}, u32[]{:S(2)}, u32[]{:S(2)}) collective-permute-start(bf16[64,1024]{1,0:T(8,128)(2,1)S(1)} %collective-permute-done.refs_3_), channel_id=1, source_target_pairs={{0,1},{1,0},{2,3},{3,2},{4,5},{5,4},{6,7},{7,6},{8,9},{9,8},{10,11... | collective-permute-start | bytes 393224 | tf_op jit(solution)/shard_map/ppermute | solution.py:173
  20.2 0.7 %copy-start.1 = (s32[1,32]{1,0:T(1,128)S(1)}, s32[1,32]{1,0:T(1,128)}, u32[]{:S(2)}) copy-start(s32[1,32]{1,0:T(1,128)} %refs_1_.1) | copy-start | bytes 388
  36.1 2.1 %collective-permute-start.3 = (f32[128,1152]{1,0:T(8,128)S(1)}, f32[128,1152]{1,0:T(8,128)S(1)}, u32[]{:S(2)}, u32[]{:S(2)}) collective-permute-start(f32[128,1152]{1,0:T(8,128)S(1)} %get-tuple-element.7), channel_id=1, source_target_pairs={{0,1},{1,0},{2,3},{3,2},{4,5},{5,4},{6,7},{7,6},{8,9},{9,8},{10,11... | collective-permute-start | bytes 1769480 | tf_op jit(solution)/shard_map/ppermute | solution.py:173
  38.7 9.1 %collective-permute-start.4 = (f32[64,1152]{1,0:T(8,128)S(1)}, f32[64,1152]{1,0:T(8,128)S(1)}, u32[]{:S(2)}, u32[]{:S(2)}) collective-permute-start(f32[64,1152]{1,0:T(8,128)S(1)} %get-tuple-element.9), channel_id=1, source_target_pairs={{0,2},{1,3},{2,0},{3,1},{4,6},{5,7},{6,4},{7,5},{8,10},{9,11},{10,... | collective-permute-start | bytes 884744 | tf_op jit(solution)/shard_map/ppermute | solution.py:173

commit v2 on v1

v2 whole, which is shorter than its diff:
```python
import functools
import math

import jax
import jax.numpy as jnp
from jax import lax
from jax.experimental import pallas as pl
from jax.experimental.pallas import tpu as pltpu
from jax.sharding import PartitionSpec as P

HEADS = 32
DH = 128
PAGE = 128
LANES = 128
TOK_TILE = 256
GROUP = 2
MOST_PERMUTES = 8
VMEM_LIMIT = 50 * 2**20

lowest = -1e30
to_log2 = math.log2(math.e) / math.sqrt(DH)


def attend_kernel(n_parts, limits_ref, *refs):
    q_refs = refs[:n_parts]
    k_hbm, v_hbm, keep_ref, send_ref = refs[n_parts : n_parts + 4]
    q_turned, k_pool, v_pool, stats, k_sem, v_sem = refs[n_parts + 4 :]
    heads, pool = k_pool.shape[:2]
    all_tok = q_turned.shape[2]
    tile = min(all_tok, TOK_TILE)
    tiles = all_tok // tile
    half = keep_ref.shape[0]
    ahead = min(heads, 2)

    def copies(h):
        columns = pl.ds(pl.multiple_of(h * DH, DH), DH)
        return (
            pltpu.make_async_copy(k_hbm.at[:, :, columns], k_pool.at[h], k_sem.at[h]),
            pltpu.make_async_copy(v_hbm.at[:, :, columns], v_pool.at[h], v_sem.at[h]),
        )

    for h in range(ahead):
        for copy in copies(h):
            copy.start()
    for h in range(heads):
        rows = [q_ref[:, h * DH : (h + 1) * DH] for q_ref in q_refs]
        q_turned[h] = jnp.concatenate(rows, axis=0).T
    stats[...] = jnp.zeros_like(stats)
    ones = jnp.ones((8, PAGE), jnp.bfloat16)

    def unit(u, carry):
        h, t = u // tiles, lax.rem(u, tiles)

        @pl.when(t == 0)
        def _():
            for copy in copies(h):
                copy.wait()

            @pl.when(h + ahead < heads)
            def _():
                for copy in copies(h + ahead):
                    copy.start()

        start = pl.multiple_of(t * tile, tile)
        columns = pl.ds(start, tile)
        q_tile = q_turned[h, :, columns]
        scores, tops = [], []
        for i in range(0, pool, GROUP):
            block = k_pool[h, i : i + GROUP].reshape(GROUP * PAGE, DH)
            both = jnp.dot(block, q_tile, preferred_element_type=jnp.float32)
            for j in range(GROUP):
                scores.append(both[j * PAGE : (j + 1) * PAGE])
                tops.append(jnp.max(scores[-1], axis=0, keepdims=True))
        used = [jnp.minimum(tops[i], limits_ref[i : i + 1, :]) for i in range(pool)]
        best = functools.reduce(jnp.maximum, used)
        total, accum = 0.0, 0.0
        for i in range(pool):
            weights = jnp.exp2((scores[i] - tops[i]) * to_log2).astype(jnp.bfloat16)
            page_out = jnp.dot(
                jnp.concatenate([v_pool[h, i].T, ones], axis=0),
                weights,
                preferred_element_type=jnp.float32,
            )
            fresh = jnp.exp2((used[i] - best) * to_log2)
            total = total + fresh * page_out[DH : DH + 1]
            accum = accum + fresh * page_out[:DH]
        out = (accum / total).T
        stats[pl.ds(h, 1), columns] = best * to_log2 + jnp.log2(total)
        lanes = pl.ds(pl.multiple_of(h * DH, DH), DH)
        if tiles == 1:
            keep_ref[:, lanes] = out[:half]
            send_ref[:, lanes] = out[half:]
        else:

            @pl.when(start < half)
            def _():
                keep_ref[columns, lanes] = out

            @pl.when(start >= half)
            def _():
                send_ref[pl.ds(pl.multiple_of(start - half, tile), tile), lanes] = out

        return carry

    lax.fori_loop(0, heads * tiles, unit, 0)
    for t in range(tiles):
        turned = stats[:, t * tile : (t + 1) * tile].T
        for r in range(0, tile, 8):
            row = t * tile + r
            ref = keep_ref if row < half else send_ref
            row = row if row < half else row - half
            ref[row : row + 8, heads * DH :] = turned[r : r + 8]


def attend(q_parts, keys, values, limits):
    all_tok = sum(part.shape[0] for part in q_parts)
    pool = keys.shape[0]
    heads = keys.shape[2] // DH
    in_vmem = pl.BlockSpec(memory_space=pltpu.VMEM)
    anywhere = pl.BlockSpec(memory_space=pl.ANY)
    out = jax.ShapeDtypeStruct((all_tok // 2, heads * DH + LANES), jnp.float32)
    return pl.pallas_call(
        functools.partial(attend_kernel, len(q_parts)),
        in_specs=[in_vmem] * (1 + len(q_parts)) + [anywhere, anywhere],
        out_specs=[in_vmem, in_vmem],
        scratch_shapes=[
            pltpu.VMEM((heads, DH, all_tok), jnp.bfloat16),
            pltpu.VMEM((heads, pool, PAGE, DH), jnp.bfloat16),
            pltpu.VMEM((heads, pool, PAGE, DH), jnp.bfloat16),
            pltpu.VMEM((LANES, all_tok), jnp.float32),
            pltpu.SemaphoreType.DMA((heads,)),
            pltpu.SemaphoreType.DMA((heads,)),
        ],
        out_shape=[out, out],
        compiler_params=pltpu.CompilerParams(vmem_limit_bytes=VMEM_LIMIT),
        name="attend",
    )(limits, *q_parts, keys, values)


def rounded(x):
    return jnp.where(x < 0, x - 0.5, x + 0.5).astype(jnp.int32)


def encode(outs, logs, out_ref):
    heads = len(outs)
    where = (slice(None),) * (len(out_ref.shape) - 1)
    powers = []
    for h, out in enumerate(outs):
        largest = jnp.max(jnp.abs(out), axis=-1, keepdims=True)
        power = jnp.ceil(jnp.log2(jnp.maximum(largest, 2.0**-100)))
        powers.append(power)
        out_ref[where + (slice(h * DH, (h + 1) * DH),)] = rounded(
            out * (jnp.exp2(-power) * 32767.0)
        ).astype(jnp.int16)
    fixed = rounded(logs * 2.0**19)
    high = lax.shift_right_arithmetic(fixed, 16)
    low = lax.bitwise_and(fixed, 65535) - 32768
    pad = jnp.zeros(logs.shape[:-1] + (LANES - 3 * heads,), jnp.int32)
    stat = jnp.concatenate(
        [high[..., :heads], low[..., :heads]] + [p.astype(jnp.int32) for p in powers] + [pad], axis=-1
    )
    out_ref[where + (slice(heads * DH, heads * DH + LANES),)] = stat.astype(jnp.int16)


def decode(heads, ref):
    where = (slice(None),) * (len(ref.shape) - 1)
    stat = ref[where + (slice(heads * DH, heads * DH + LANES),)].astype(jnp.int32)
    fixed = lax.shift_left(stat[..., :heads], 16) + (stat[..., heads : 2 * heads] + 32768)
    logs = fixed.astype(jnp.float32) * 2.0**-19
    steps = jnp.exp2(stat[..., 2 * heads : 3 * heads].astype(jnp.float32)) * (1.0 / 32767.0)
    outs = []
    for h in range(heads):
        coded = ref[where + (slice(h * DH, (h + 1) * DH),)].astype(jnp.int32).astype(jnp.float32)
        outs.append(coded * steps[..., h : h + 1])
    return outs, logs


def plain(heads, ref):
    where = (slice(None),) * (len(ref.shape) - 1)
    outs = [ref[where + (slice(h * DH, (h + 1) * DH),)] for h in range(heads)]
    return outs, ref[where + (slice(heads * DH, heads * DH + heads),)]


def merge_kernel(heads, last, mine_ref, theirs_ref, *out_refs):
    mine, mine_logs = plain(heads, mine_ref)
    theirs, their_logs = (decode if theirs_ref.dtype == jnp.int16 else plain)(heads, theirs_ref)
    top = jnp.maximum(mine_logs, their_logs)
    first, second = jnp.exp2(mine_logs - top), jnp.exp2(their_logs - top)
    both = first + second
    first, second, logs = first / both, second / both, top + jnp.log2(both)
    outs = [
        mine[h] * first[..., h : h + 1] + theirs[h] * second[..., h : h + 1] for h in range(heads)
    ]
    if last:
        if len(out_refs) == 1:
            encode(outs, logs, out_refs[0])
        else:
            for block, out_ref in enumerate(out_refs):
                encode([out[block] for out in outs], logs[block], out_ref)
    else:
        keep_ref, send_ref = out_refs
        half = keep_ref.shape[1]
        for h in range(heads):
            keep_ref[:, :, h * DH : (h + 1) * DH] = outs[h][:, :half]
        pad = jnp.zeros(logs.shape[:-1] + (LANES - heads,), jnp.float32)
        keep_ref[:, :, heads * DH :] = jnp.concatenate([logs, pad], axis=-1)[:, :half]
        encode([out[:, half:] for out in outs], logs[:, half:], send_ref)


def merge(mine, theirs, heads, out_shapes, last):
    return pl.pallas_call(
        functools.partial(merge_kernel, heads, last),
        out_shape=out_shapes,
        compiler_params=pltpu.CompilerParams(vmem_limit_bytes=VMEM_LIMIT),
        name="merge",
    )(mine, theirs)


def place_kernel(heads, axis, *refs):
    part_refs, (out_ref, logs_ref) = refs[:-2], refs[-2:]
    here = lax.axis_index(axis) if len(part_refs) > 1 else 0
    pieces = []
    if len(part_refs) > 1:
        for k, part_ref in enumerate(part_refs):
            outs, logs = decode(heads, part_ref)
            at = lax.bitwise_xor(here, k)
            out_ref[:, pl.ds(pl.multiple_of(at * heads * DH, DH), heads * DH)] = jnp.concatenate(
                outs, axis=-1
            )
            pieces.append((at, logs))
        columns = []
        for z in range(len(part_refs)):
            columns.append(sum(jnp.where(at == z, logs, 0.0) for at, logs in pieces))
    else:
        outs, logs = decode(heads, part_refs[0])
        for z in range(logs.shape[0]):
            for h in range(heads):
                first = (z * heads + h) * DH
                out_ref[:, first : first + DH] = outs[h][z]
        columns = [logs[z] for z in range(logs.shape[0])]
    logs_ref[...] = jnp.concatenate(columns, axis=-1) * math.log(2.0)


def place(parts, heads, axis, share):
    return pl.pallas_call(
        functools.partial(place_kernel, heads, axis),
        out_shape=[
            jax.ShapeDtypeStruct((share, HEADS * DH), jnp.float32),
            jax.ShapeDtypeStruct((share, HEADS), jnp.float32),
        ],
        compiler_params=pltpu.CompilerParams(vmem_limit_bytes=VMEM_LIMIT),
        name="place",
    )(*parts)


def across(value, axis, size, bit):
    return lax.ppermute(value, axis, [(i, i ^ bit) for i in range(size)])


def page_limits(page_lists, page_counts, pool, width):
    slots = jnp.arange(page_lists.shape[1], dtype=jnp.int32)
    pages = jnp.arange(pool, dtype=jnp.int32)
    live = jnp.any(
        (page_lists[0][None, :] == pages[:, None]) & (slots < page_counts[0])[None, :], axis=1
    )
    return jnp.broadcast_to(jnp.where(live, -lowest, lowest)[:, None], (pool, width))


def on_device(queries, keys, values, page_lists, page_counts):
    n_head = lax.axis_size("head")
    n_cache = lax.axis_size("cache")
    heads = keys.shape[2] // DH
    share = queries.shape[0] // n_cache
    bits = [1 << i for i in range(n_cache.bit_length() - 1)]
    direct = n_head <= MOST_PERMUTES
    head_at, cache_at = lax.axis_index("head"), lax.axis_index("cache")
    order = [0]
    for bit in reversed(bits):
        order = order + [share_at ^ bit for share_at in order]
    shares = queries.reshape(n_cache, share, n_head, heads * DH)

    def pick(names):
        return jnp.concatenate(
            [lax.dynamic_index_in_dim(shares, cache_at ^ name, 0, keepdims=False) for name in names]
        )

    same = pick(order[: n_cache // 2])
    rows = same.shape[0]

    def for_head(part, k):
        return lax.dynamic_index_in_dim(part, head_at ^ k, 1, keepdims=False)

    if direct:
        parts = [across(for_head(same, k), "head", n_head, k) for k in range(1, n_head)]
        swapped = [across(part, "cache", n_cache, 1) for part in parts]
        other = pick(order[n_cache // 2 :])
        q_parts = [for_head(same, 0)] + parts + [for_head(other, 0)] + swapped
    else:
        moved = lax.all_to_all(same, "head", split_axis=1, concat_axis=0, tiled=True)
        moved = moved.reshape(n_head * rows, heads * DH)
        q_parts = [moved, across(moved, "cache", n_cache, 1)]
    all_tok = n_head * queries.shape[0]
    limits = page_limits(page_lists, page_counts, keys.shape[0], min(all_tok, TOK_TILE))
    keep, send = attend(q_parts, keys, values, limits)
    width = keep.shape[1]
    keep = keep.reshape(n_head, rows, width)
    send = send.reshape(n_head, rows, width)
    for bit in bits:
        theirs = across(send, "cache", n_cache, bit)
        if bit != bits[-1]:
            half = keep.shape[1] // 2
            shapes = [
                jax.ShapeDtypeStruct((n_head, half, width), jnp.float32),
                jax.ShapeDtypeStruct((n_head, half, width), jnp.int16),
            ]
            keep, send = merge(keep, theirs, heads, shapes, False)
        elif direct:
            shapes = [jax.ShapeDtypeStruct((share, width), jnp.int16)] * n_head
            blocks = merge(keep, theirs, heads, shapes, True)
            parts = [blocks[0]] + [across(blocks[k], "head", n_head, k) for k in range(1, n_head)]
        else:
            shapes = [jax.ShapeDtypeStruct((n_head, share, width), jnp.int16)]
            (blocks,) = merge(keep, theirs, heads, shapes, True)
            parts = [lax.all_to_all(blocks, "head", split_axis=0, concat_axis=0, tiled=True)]
    return tuple(place(parts, heads, "head", share))


def solution(mesh):
    in_specs = (
        P(("group", "head"), None),
        P(("group", "cache"), None, "head"),
        P(("group", "cache"), None, "head"),
        P(("group", "cache"), None),
        P(("group", "cache")),
    )
    out_specs = (P(("group", "head", "cache"), None), P(("group", "head", "cache"), None))
    return jax.shard_map(
        on_device, mesh=mesh, in_specs=in_specs, out_specs=out_specs, check_vma=False
    )
```

time: 61.5 us -> 47.5 us (0.77)
  blocking collectives: 23.9 us -> 0 us
  starting transfers between devices: 3.27 us -> 12 us
  waiting for transfers between devices: 13.6 us -> 15 us
  local copies, waits for them, and re-layouts: 3.2 us -> 1.91 us
  other arithmetic: 0.01 us -> 0.82 us
    all_to_all x2 -> x0, blocking collectives: 23.9 us -> none  [the longest x1 12.2 us: on_device(): lax.all_to_all(mine.reshape(share, n_head, heads * DH), 'head', split_axi...]
    ppermute x5 -> x11, starting transfers between devices: 3.27 us -> 12 us  [across(): return lax.ppermute(value, axis, [(i, i ^ bit) for i in range(size)])]
    unnamed x6 -> x0, local copies, waits for them, and re-layouts: 2.38 us -> none
    ppermute x5 -> x11, waiting for transfers between devices: 13.6 us -> 15 us  [across(): return lax.ppermute(value, axis, [(i, i ^ bit) for i in range(size)])]
    pallas_call x2 -> x3, Pallas kernels: 0.79 us -> 2.03 us  [the longest x2 1.09 us: merge(): pl.pallas_call(functools.partial(merge_kernel, heads, last), out_shape=ou...]
    pallas_call x1, Pallas kernels: 15.2 us -> 14.1 us  [attend(): pl.pallas_call(functools.partial(attend_kernel, len(q_parts)), in_specs=[...]
    reduce_or x0 -> x1, other arithmetic: none -> 0.77 us  [page_limits(): jnp.any((page_lists[0][None, :] == pages[:, None]) & (slots < page_counts...]
    reshape x2 -> x1, local copies, waits for them, and re-layouts: 0.73 us -> 1.43 us  [on_device(): shares = queries.reshape(n_cache, share, n_head, heads * DH)]
  transfers between devices with their start and end apart: 5 -> 11, of which waited for: 4 -> 9; matrix products, arithmetic and copies ran while one was open for 0% -> 2% of each run, Pallas kernels for 0% -> 0%
where the time goes in v2:
time: 47.5 us; the launch traced here: 47.4 us
  Pallas kernels  16.2 us (34%)
  waiting for transfers between devices  15 us (32%)
  starting transfers between devices  12 us (25%)
  local copies, waits for them, and re-layouts  1.91 us (4%)
  between operations  1.43 us (3%)
  other arithmetic  0.82 us (2%)
    ppermute x11, waiting for transfers between devices, across(): return lax.ppermute(value, axis, [(i, i ^ bit) for i in range(size)])  15 us
    pallas_call x1, Pallas kernels, attend(): pl.pallas_call(functools.partial(attend_kernel, len(q_parts)), in_specs=[...  14.1 us
    ppermute x11, starting transfers between devices, across(): return lax.ppermute(value, axis, [(i, i ^ bit) for i in range(size)])  12 us
    reshape x1, local copies, waits for them, and re-layouts, on_device(): shares = queries.reshape(n_cache, share, n_head, heads * DH)  1.43 us
    pallas_call x2, Pallas kernels, merge(): pl.pallas_call(functools.partial(merge_kernel, heads, last), out_shape=ou...  1.09 us
  transfers between devices with their start and end apart: 11, of which 9 were waited for; matrix products, arithmetic and copies ran while one was open for 2% of the time, Pallas kernels for 0%

profile of v2, /device:TPU:0, one launch (start us, length us, event | category | flops | bytes accessed | tf_op | source)
XLA Modules:
  0.0 47.4 jit_solution(17407383155155840361)
XLA Ops:
  0.7 1.4 %reshape.20 = bf16[4,16,4,1024]{3,2,1,0:T(4,128)(2,1)S(1)} reshape(bf16[64,4096]{1,0:T(8,128)(2,1)} %param.5) | data formatting | bytes 1048576 | tf_op jit(solution)/shard_map/reshape | solution.py:280
  2.1 0.2 constant_dynamic-slice_fusion
  2.4 0.1 copy_bitcast_fusion.2
  2.5 5.1 %collective-permute-start.2 = (bf16[32,1024]{1,0:T(8,128)(2,1)S(1)}, bf16[32,1024]{1,0:T(8,128)(2,1)S(1)}, u32[]{:S(2)}, u32[]{:S(2)}) collective-permute-start(bf16[32,1024]{1,0:T(8,128)(2,1)S(1)} %get-tuple-element.22), channel_id=1, source_target_pairs={{0,12},{4,8},{8,4},{12,0},{1,13},{5,9},{9,5},{13,1},{2,14},{6,10},... | collective-permute-start | bytes 196616 | tf_op jit(solution)/shard_map/ppermute | solution.py:257
  7.6 0.0 collective-permute-start
  7.6 0.6 %collective-permute-start.1 = (bf16[32,1024]{1,0:T(8,128)(2,1)S(1)}, bf16[32,1024]{1,0:T(8,128)(2,1)S(1)}, u32[]{:S(2)}, u32[]{:S(2)}) collective-permute-start(bf16[32,1024]{1,0:T(8,128)(2,1)S(1)} %get-tuple-element.25), channel_id=1, source_target_pairs={{0,8},{4,12},{8,0},{12,4},{1,9},{5,13},{9,1},{13,5},{2,10},{6,14},... | collective-permute-start | bytes 196616 | tf_op jit(solution)/shard_map/ppermute | solution.py:257
  8.9 0.8 %fusion.11 = pred[32]{0:T(512)(128)(4,1)S(1)} fusion(s32[32]{0:T(128)} %bitcast.25, pred[32]{0:T(512)(128)(4,1)S(1)} %iota_compare_fusion.1), kind=kLoop, calls=%fused_computation.26 | loop fusion | flops 3040 | bytes 192 | tf_op jit(solution)/shard_map/reduce_or | solution.py:263
  9.7 0.1 copy_bitcast_fusion
  9.8 0.7 %collective-permute-done.2.refs_3_ = bf16[32,1024]{1,0:T(8,128)(2,1)S(1)} collective-permute-done((bf16[32,1024]{1,0:T(8,128)(2,1)S(1)}, bf16[32,1024]{1,0:T(8,128)(2,1)S(1)}, u32[]{:S(2)}, u32[]{:S(2)}) %collective-permute-start.2) | collective-permute-done | bytes 65568 | tf_op jit(solution)/shard_map/ppermute | solution.py:257
  10.5 0.0 collective-permute-start.5
  10.5 1.8 %collective-permute-done.refs_1_ = bf16[32,1024]{1,0:T(8,128)(2,1)S(1)} collective-permute-done((bf16[32,1024]{1,0:T(8,128)(2,1)S(1)}, bf16[32,1024]{1,0:T(8,128)(2,1)S(1)}, u32[]{:S(2)}, u32[]{:S(2)}) %collective-permute-start) | collective-permute-done | bytes 65568 | tf_op jit(solution)/shard_map/ppermute | solution.py:257
  12.3 0.0 collective-permute-start.3
  12.3 1.0 %collective-permute-done.1.refs_2_ = bf16[32,1024]{1,0:T(8,128)(2,1)S(1)} collective-permute-done((bf16[32,1024]{1,0:T(8,128)(2,1)S(1)}, bf16[32,1024]{1,0:T(8,128)(2,1)S(1)}, u32[]{:S(2)}, u32[]{:S(2)}) %collective-permute-start.1) | collective-permute-done | bytes 65568 | tf_op jit(solution)/shard_map/ppermute | solution.py:257
  13.2 0.0 collective-permute-start.4
  13.3 0.0 collective-permute-done.5.refs_7_
  13.3 0.3 collective-permute-done.3.refs_5_
  13.5 1.0 %collective-permute-done.4.refs_6_ = bf16[32,1024]{1,0:T(8,128)(2,1)S(1)} collective-permute-done((bf16[32,1024]{1,0:T(8,128)(2,1)S(1)}, bf16[32,1024]{1,0:T(8,128)(2,1)S(1)}, u32[]{:S(2)}, u32[]{:S(2)}) %collective-permute-start.4) | collective-permute-done | bytes 65568 | tf_op jit(solution)/shard_map/ppermute | solution.py:257
  14.5 0.1 broadcast_in_dim.18.limits_ref
  14.6 14.1 %attend.1 = (f32[128,1152]{1,0:T(8,128)S(1)}, f32[128,1152]{1,0:T(8,128)S(1)}) custom-call(f32[32,256]{1,0:T(8,128)S(1)} %broadcast_in_dim.18.limits_ref, bf16[32,1024]{1,0:T(8,128)(2,1)S(1)} %get-tuple-element.23.refs_0_, bf16[32,1024]{1,0:T(8,128)(2,1)S(1)} %collective-permute-done.refs_1_, bf16[32,1024]{1,0:T(8,128)(2,1)S(1)} %collective-permute-done.1.refs_2_, ...), custom_call_target="tpu_custom_call" | custom-call | tf_op jit(solution)/shard_map/attend/pallas_call | solution.py:122
  28.7 0.2 collective-permute-start.6
  28.9 1.8 %collective-permute-done.6.theirs_ref = f32[4,32,1152]{2,1,0:T(8,128)S(1)} collective-permute-done((f32[4,32,1152]{2,1,0:T(8,128)S(1)}, f32[4,32,1152]{2,1,0:T(8,128)S(1)}, u32[]{:S(2)}, u32[]{:S(2)}) %collective-permute-start.6) | collective-permute-done | bytes 589856 | tf_op jit(solution)/shard_map/ppermute | solution.py:257
  30.8 0.6 %merge.2 = (f32[4,16,1152]{2,1,0:T(8,128)S(1)}, s16[4,16,1152]{2,1,0:T(8,128)(2,1)S(1)}) custom-call(f32[4,32,1152]{2,1,0:T(8,128)S(1)} %bitcast.23, f32[4,32,1152]{2,1,0:T(8,128)S(1)} %collective-permute-done.6.theirs_ref), custom_call_target="tpu_custom_call" | custom-call | tf_op jit(solution)/shard_map/merge/pallas_call | solution.py:211
  31.4 1.6 %collective-permute-start.7 = (s16[4,16,1152]{2,1,0:T(8,128)(2,1)S(1)}, s16[4,16,1152]{2,1,0:T(8,128)(2,1)S(1)}, u32[]{:S(2)}, u32[]{:S(2)}) collective-permute-start(s16[4,16,1152]{2,1,0:T(8,128)(2,1)S(1)} %get-tuple-element.13), channel_id=1, source_target_pairs={{0,2},{1,3},{2,0},{3,1},{4,6},{5,7},{6,4},{7,5},{8,10},{9,11},{10,... | collective-permute-start | bytes 442376 | tf_op jit(solution)/shard_map/ppermute | solution.py:257
  32.9 4.4 %collective-permute-done.7.theirs_ref = s16[4,16,1152]{2,1,0:T(8,128)(2,1)S(1)} collective-permute-done((s16[4,16,1152]{2,1,0:T(8,128)(2,1)S(1)}, s16[4,16,1152]{2,1,0:T(8,128)(2,1)S(1)}, u32[]{:S(2)}, u32[]{:S(2)}) %collective-permute-start.7) | collective-permute-done | bytes 147488 | tf_op jit(solution)/shard_map/ppermute | solution.py:257
  37.3 0.5 %merge.3 = (s16[16,1152]{1,0:T(8,128)(2,1)S(1)}, s16[16,1152]{1,0:T(8,128)(2,1)S(1)}, s16[16,1152]{1,0:T(8,128)(2,1)S(1)}, s16[16,1152]{1,0:T(8,128)(2,1)S(1)}) custom-call(f32[4,16,1152]{2,1,0:T(8,128)S(1)} %get-tuple-element.12.mine_ref, s16[4,16,1152]{2,1,0:T(8,128)(2,1)S(1)} %collective-permute-done.7.theirs_ref), custom_call_target="tpu_custom_call" | custom-call | tf_op jit(solution)/shard_map/merge/pallas_call | solution.py:211
  37.9 1.6 %collective-permute-start.8 = (s16[16,1152]{1,0:T(8,128)(2,1)S(1)}, s16[16,1152]{1,0:T(8,128)(2,1)S(1)}, u32[]{:S(2)}, u32[]{:S(2)}) collective-permute-start(s16[16,1152]{1,0:T(8,128)(2,1)S(1)} %get-tuple-element.15), channel_id=1, source_target_pairs={{0,4},{4,0},{8,12},{12,8},{1,5},{5,1},{9,13},{13,9},{2,6},{6,2},{1... | collective-permute-start | bytes 110600 | tf_op jit(solution)/shard_map/ppermute | solution.py:257
  39.5 1.2 %collective-permute-start.9 = (s16[16,1152]{1,0:T(8,128)(2,1)S(1)}, s16[16,1152]{1,0:T(8,128)(2,1)S(1)}, u32[]{:S(2)}, u32[]{:S(2)}) collective-permute-start(s16[16,1152]{1,0:T(8,128)(2,1)S(1)} %get-tuple-element.16), channel_id=1, source_target_pairs={{0,8},{4,12},{8,0},{12,4},{1,9},{5,13},{9,1},{13,5},{2,10},{6,14},... | collective-permute-start | bytes 110600 | tf_op jit(solution)/shard_map/ppermute | solution.py:257
  40.7 1.7 %collective-permute-start.10 = (s16[16,1152]{1,0:T(8,128)(2,1)S(1)}, s16[16,1152]{1,0:T(8,128)(2,1)S(1)}, u32[]{:S(2)}, u32[]{:S(2)}) collective-permute-start(s16[16,1152]{1,0:T(8,128)(2,1)S(1)} %get-tuple-element.17), channel_id=1, source_target_pairs={{0,12},{4,8},{8,4},{12,0},{1,13},{5,9},{9,5},{13,1},{2,14},{6,10},... | collective-permute-start | bytes 110600 | tf_op jit(solution)/shard_map/ppermute | solution.py:257
  42.3 0.0 collective-permute-done.8.refs_1_
  42.3 2.7 %collective-permute-done.9.refs_2_ = s16[16,1152]{1,0:T(8,128)(2,1)S(1)} collective-permute-done((s16[16,1152]{1,0:T(8,128)(2,1)S(1)}, s16[16,1152]{1,0:T(8,128)(2,1)S(1)}, u32[]{:S(2)}, u32[]{:S(2)}) %collective-permute-start.9) | collective-permute-done | bytes 36896 | tf_op jit(solution)/shard_map/ppermute | solution.py:257
  45.0 1.4 %collective-permute-done.10.refs_3_ = s16[16,1152]{1,0:T(8,128)(2,1)S(1)} collective-permute-done((s16[16,1152]{1,0:T(8,128)(2,1)S(1)}, s16[16,1152]{1,0:T(8,128)(2,1)S(1)}, u32[]{:S(2)}, u32[]{:S(2)}) %collective-permute-start.10) | collective-permute-done | bytes 36896 | tf_op jit(solution)/shard_map/ppermute | solution.py:257
  46.4 0.9 %place.1 = (f32[16,4096]{1,0:T(8,128)}, f32[16,32]{1,0:T(8,128)}) custom-call(s16[16,1152]{1,0:T(8,128)(2,1)S(1)} %get-tuple-element.14.refs_0_, s16[16,1152]{1,0:T(8,128)(2,1)S(1)} %collective-permute-done.8.refs_1_, s16[16,1152]{1,0:T(8,128)(2,1)S(1)} %collective-permute-done.9.refs_2_, s16[16,1152]{1,0:T(8,128)(2,1)S(1)} %collective-permute-done.10.refs_3_), custom_call_target="tpu_custom_call" | custom-call | tf_op jit(solution)/shard_map/place/pallas_call | solution.py:245
  (4 shorter events, 0.0 us)
Async XLA Ops:
  2.5 8.0 %collective-permute-start.2 = (bf16[32,1024]{1,0:T(8,128)(2,1)S(1)}, bf16[32,1024]{1,0:T(8,128)(2,1)S(1)}, u32[]{:S(2)}, u32[]{:S(2)}) collective-permute-start(bf16[32,1024]{1,0:T(8,128)(2,1)S(1)} %get-tuple-element.22), channel_id=1, source_target_pairs={{0,12},{4,8},{8,4},{12,0},{1,13},{5,9},{9,5},{13,1},{2,14},{6,10},... | collective-permute-start | bytes 196616 | tf_op jit(solution)/shard_map/ppermute | solution.py:257
  7.6 4.7 %collective-permute-start = (bf16[32,1024]{1,0:T(8,128)(2,1)S(1)}, bf16[32,1024]{1,0:T(8,128)(2,1)S(1)}, u32[]{:S(2)}, u32[]{:S(2)}) collective-permute-start(bf16[32,1024]{1,0:T(8,128)(2,1)S(1)} %get-tuple-element.24), channel_id=1, source_target_pairs={{0,4},{4,0},{8,12},{12,8},{1,5},{5,1},{9,13},{13,9},{2,6},{6,2},{1... | collective-permute-start | bytes 196616 | tf_op jit(solution)/shard_map/ppermute | solution.py:257
  7.6 5.6 %collective-permute-start.1 = (bf16[32,1024]{1,0:T(8,128)(2,1)S(1)}, bf16[32,1024]{1,0:T(8,128)(2,1)S(1)}, u32[]{:S(2)}, u32[]{:S(2)}) collective-permute-start(bf16[32,1024]{1,0:T(8,128)(2,1)S(1)} %get-tuple-element.25), channel_id=1, source_target_pairs={{0,8},{4,12},{8,0},{12,4},{1,9},{5,13},{9,1},{13,5},{2,10},{6,14},... | collective-permute-start | bytes 196616 | tf_op jit(solution)/shard_map/ppermute | solution.py:257
  10.5 2.8 %collective-permute-start.5 = (bf16[32,1024]{1,0:T(8,128)(2,1)S(1)}, bf16[32,1024]{1,0:T(8,128)(2,1)S(1)}, u32[]{:S(2)}, u32[]{:S(2)}) collective-permute-start(bf16[32,1024]{1,0:T(8,128)(2,1)S(1)} %collective-permute-done.2.refs_3_), channel_id=1, source_target_pairs={{0,1},{1,0},{2,3},{3,2},{4,5},{5,4},{6,7},{7,6},{8,9},{9,8},{10,11... | collective-permute-start | bytes 196616 | tf_op jit(solution)/shard_map/ppermute | solution.py:257
  12.3 1.3 %collective-permute-start.3 = (bf16[32,1024]{1,0:T(8,128)(2,1)S(1)}, bf16[32,1024]{1,0:T(8,128)(2,1)S(1)}, u32[]{:S(2)}, u32[]{:S(2)}) collective-permute-start(bf16[32,1024]{1,0:T(8,128)(2,1)S(1)} %collective-permute-done.refs_1_), channel_id=1, source_target_pairs={{0,1},{1,0},{2,3},{3,2},{4,5},{5,4},{6,7},{7,6},{8,9},{9,8},{10,11... | collective-permute-start | bytes 196616 | tf_op jit(solution)/shard_map/ppermute | solution.py:257
  13.2 1.3 %collective-permute-start.4 = (bf16[32,1024]{1,0:T(8,128)(2,1)S(1)}, bf16[32,1024]{1,0:T(8,128)(2,1)S(1)}, u32[]{:S(2)}, u32[]{:S(2)}) collective-permute-start(bf16[32,1024]{1,0:T(8,128)(2,1)S(1)} %collective-permute-done.1.refs_2_), channel_id=1, source_target_pairs={{0,1},{1,0},{2,3},{3,2},{4,5},{5,4},{6,7},{7,6},{8,9},{9,8},{10,11... | collective-permute-start | bytes 196616 | tf_op jit(solution)/shard_map/ppermute | solution.py:257
  28.7 2.1 %collective-permute-start.6 = (f32[4,32,1152]{2,1,0:T(8,128)S(1)}, f32[4,32,1152]{2,1,0:T(8,128)S(1)}, u32[]{:S(2)}, u32[]{:S(2)}) collective-permute-start(f32[4,32,1152]{2,1,0:T(8,128)S(1)} %bitcast.24), channel_id=1, source_target_pairs={{0,1},{1,0},{2,3},{3,2},{4,5},{5,4},{6,7},{7,6},{8,9},{9,8},{10,11... | collective-permute-start | bytes 1769480 | tf_op jit(solution)/shard_map/ppermute | solution.py:257
  31.4 6.0 %collective-permute-start.7 = (s16[4,16,1152]{2,1,0:T(8,128)(2,1)S(1)}, s16[4,16,1152]{2,1,0:T(8,128)(2,1)S(1)}, u32[]{:S(2)}, u32[]{:S(2)}) collective-permute-start(s16[4,16,1152]{2,1,0:T(8,128)(2,1)S(1)} %get-tuple-element.13), channel_id=1, source_target_pairs={{0,2},{1,3},{2,0},{3,1},{4,6},{5,7},{6,4},{7,5},{8,10},{9,11},{10,... | collective-permute-start | bytes 442376 | tf_op jit(solution)/shard_map/ppermute | solution.py:257
  37.9 4.5 %collective-permute-start.8 = (s16[16,1152]{1,0:T(8,128)(2,1)S(1)}, s16[16,1152]{1,0:T(8,128)(2,1)S(1)}, u32[]{:S(2)}, u32[]{:S(2)}) collective-permute-start(s16[16,1152]{1,0:T(8,128)(2,1)S(1)} %get-tuple-element.15), channel_id=1, source_target_pairs={{0,4},{4,0},{8,12},{12,8},{1,5},{5,1},{9,13},{13,9},{2,6},{6,2},{1... | collective-permute-start | bytes 110600 | tf_op jit(solution)/shard_map/ppermute | solution.py:257
  39.5 5.5 %collective-permute-start.9 = (s16[16,1152]{1,0:T(8,128)(2,1)S(1)}, s16[16,1152]{1,0:T(8,128)(2,1)S(1)}, u32[]{:S(2)}, u32[]{:S(2)}) collective-permute-start(s16[16,1152]{1,0:T(8,128)(2,1)S(1)} %get-tuple-element.16), channel_id=1, source_target_pairs={{0,8},{4,12},{8,0},{12,4},{1,9},{5,13},{9,1},{13,5},{2,10},{6,14},... | collective-permute-start | bytes 110600 | tf_op jit(solution)/shard_map/ppermute | solution.py:257
  40.7 5.8 %collective-permute-start.10 = (s16[16,1152]{1,0:T(8,128)(2,1)S(1)}, s16[16,1152]{1,0:T(8,128)(2,1)S(1)}, u32[]{:S(2)}, u32[]{:S(2)}) collective-permute-start(s16[16,1152]{1,0:T(8,128)(2,1)S(1)} %get-tuple-element.17), channel_id=1, source_target_pairs={{0,12},{4,8},{8,4},{12,0},{1,13},{5,9},{9,5},{13,1},{2,14},{6,10},... | collective-permute-start | bytes 110600 | tf_op jit(solution)/shard_map/ppermute | solution.py:257

commit v3 on v2

--- a/solution.py
+++ b/solution.py
@@ -13,7 +13,7 @@
 PAGE = 128
 LANES = 128
 TOK_TILE = 256
-GROUP = 2
+GROUP = 4
 MOST_PERMUTES = 8
 VMEM_LIMIT = 50 * 2**20
 
@@ -21,16 +21,16 @@
 to_log2 = math.log2(math.e) / math.sqrt(DH)
 
 
-def attend_kernel(n_parts, limits_ref, *refs):
+def attend_kernel(n_parts, starts, limits_ref, *refs):
     q_refs = refs[:n_parts]
-    k_hbm, v_hbm, keep_ref, send_ref = refs[n_parts : n_parts + 4]
-    q_turned, k_pool, v_pool, stats, k_sem, v_sem = refs[n_parts + 4 :]
+    k_hbm, v_hbm, k_first, v_first = refs[n_parts : n_parts + 4]
+    out_refs = refs[n_parts + 4 : n_parts + 4 + len(starts)]
+    q_turned, k_pool, v_pool, stats, k_sem, v_sem = refs[n_parts + 4 + len(starts) :]
     heads, pool = k_pool.shape[:2]
     all_tok = q_turned.shape[2]
     tile = min(all_tok, TOK_TILE)
     tiles = all_tok // tile
-    half = keep_ref.shape[0]
-    ahead = min(heads, 2)
+    ahead = min(heads, 3)
 
     def copies(h):
         columns = pl.ds(pl.multiple_of(h * DH, DH), DH)
@@ -39,9 +39,11 @@
             pltpu.make_async_copy(v_hbm.at[:, :, columns], v_pool.at[h], v_sem.at[h]),
         )
 
-    for h in range(ahead):
+    for h in range(1, ahead):
         for copy in copies(h):
             copy.start()
+    k_pool[0] = k_first[...]
+    v_pool[0] = v_first[...]
     for h in range(heads):
         rows = [q_ref[:, h * DH : (h + 1) * DH] for q_ref in q_refs]
         q_turned[h] = jnp.concatenate(rows, axis=0).T
@@ -53,8 +55,10 @@
 
         @pl.when(t == 0)
         def _():
-            for copy in copies(h):
-                copy.wait()
+            @pl.when(h > 0)
+            def _():
+                for copy in copies(h):
+                    copy.wait()
 
             @pl.when(h + ahead < heads)
             def _():
@@ -87,42 +91,44 @@
         out = (accum / total).T
         stats[pl.ds(h, 1), columns] = best * to_log2 + jnp.log2(total)
         lanes = pl.ds(pl.multiple_of(h * DH, DH), DH)
-        if tiles == 1:
-            keep_ref[:, lanes] = out[:half]
-            send_ref[:, lanes] = out[half:]
-        else:
-
-            @pl.when(start < half)
-            def _():
-                keep_ref[columns, lanes] = out
-
-            @pl.when(start >= half)
-            def _():
-                send_ref[pl.ds(pl.multiple_of(start - half, tile), tile), lanes] = out
+        for first, out_ref in zip(starts, out_refs):
+            length = out_ref.shape[0]
+            if tiles == 1:
+                out_ref[:, lanes] = out[first : first + length]
+            else:
+
+                @pl.when((start >= first) & (start < first + length))
+                def _():
+                    out_ref[pl.ds(pl.multiple_of(start - first, tile), tile), lanes] = out
 
         return carry
 
     lax.fori_loop(0, heads * tiles, unit, 0)
     for t in range(tiles):
         turned = stats[:, t * tile : (t + 1) * tile].T
-        for r in range(0, tile, 8):
-            row = t * tile + r
-            ref = keep_ref if row < half else send_ref
-            row = row if row < half else row - half
-            ref[row : row + 8, heads * DH :] = turned[r : r + 8]
-
-
-def attend(q_parts, keys, values, limits):
+        for first, out_ref in zip(starts, out_refs):
+            low = max(first, t * tile)
+            high = min(first + out_ref.shape[0], (t + 1) * tile)
+            if low < high:
+                out_ref[low - first : high - first, heads * DH :] = turned[
+                    low - t * tile : high - t * tile
+                ]
+
+
+def attend(q_parts, keys, values, limits, starts):
     all_tok = sum(part.shape[0] for part in q_parts)
     pool = keys.shape[0]
     heads = keys.shape[2] // DH
     in_vmem = pl.BlockSpec(memory_space=pltpu.VMEM)
     anywhere = pl.BlockSpec(memory_space=pl.ANY)
-    out = jax.ShapeDtypeStruct((all_tok // 2, heads * DH + LANES), jnp.float32)
+    outs = [
+        jax.ShapeDtypeStruct((end - first, heads * DH + LANES), jnp.float32)
+        for first, end in zip(starts, starts[1:] + [all_tok])
+    ]
     return pl.pallas_call(
-        functools.partial(attend_kernel, len(q_parts)),
-        in_specs=[in_vmem] * (1 + len(q_parts)) + [anywhere, anywhere],
-        out_specs=[in_vmem, in_vmem],
+        functools.partial(attend_kernel, len(q_parts), starts),
+        in_specs=[in_vmem] * (1 + len(q_parts)) + [anywhere, anywhere, in_vmem, in_vmem],
+        out_specs=[in_vmem] * len(outs),
         scratch_shapes=[
             pltpu.VMEM((heads, DH, all_tok), jnp.bfloat16),
             pltpu.VMEM((heads, pool, PAGE, DH), jnp.bfloat16),
@@ -131,10 +137,10 @@
             pltpu.SemaphoreType.DMA((heads,)),
             pltpu.SemaphoreType.DMA((heads,)),
         ],
-        out_shape=[out, out],
+        out_shape=outs,
         compiler_params=pltpu.CompilerParams(vmem_limit_bytes=VMEM_LIMIT),
         name="attend",
-    )(limits, *q_parts, keys, values)
+    )(limits, *q_parts, keys, values, keys[:, :, :DH], values[:, :, :DH])
 
 
 def rounded(x):
@@ -277,51 +283,61 @@
     order = [0]
     for bit in reversed(bits):
         order = order + [share_at ^ bit for share_at in order]
-    shares = queries.reshape(n_cache, share, n_head, heads * DH)
-
-    def pick(names):
-        return jnp.concatenate(
-            [lax.dynamic_index_in_dim(shares, cache_at ^ name, 0, keepdims=False) for name in names]
+
+    def pick(names, k):
+        width = heads * DH
+        at = (head_at ^ k) * width
+        pieces = [
+            lax.dynamic_slice(queries, ((cache_at ^ name) * share, at), (share, width))
+            for name in names
+        ]
+        return jnp.concatenate(pieces)
+
+    half = n_cache // 2
+    rows = half * share
+    if direct:
+        parts = [across(pick(order[:half], k), "head", n_head, k) for k in range(1, n_head)]
+        swapped = [across(part, "cache", n_cache, 1) for part in parts]
+        q_parts = [pick(order[:half], 0)] + parts + [pick(order[half:], 0)] + swapped
+    else:
+        shares = queries.reshape(n_cache, share, HEADS * DH)
+        same = jnp.concatenate(
+            [lax.dynamic_index_in_dim(shares, cache_at ^ name, 0, False) for name in order[:half]]
         )
-
-    same = pick(order[: n_cache // 2])
-    rows = same.shape[0]
-
-    def for_head(part, k):
-        return lax.dynamic_index_in_dim(part, head_at ^ k, 1, keepdims=False)
-
-    if direct:
-        parts = [across(for_head(same, k), "head", n_head, k) for k in range(1, n_head)]
-        swapped = [across(part, "cache", n_cache, 1) for part in parts]
-        other = pick(order[n_cache // 2 :])
-        q_parts = [for_head(same, 0)] + parts + [for_head(other, 0)] + swapped
-    else:
-        moved = lax.all_to_all(same, "head", split_axis=1, concat_axis=0, tiled=True)
-        moved = moved.reshape(n_head * rows, heads * DH)
+        moved = lax.all_to_all(
+            same.reshape(rows, n_head, heads * DH), "head", split_axis=1, concat_axis=0, tiled=True
+        ).reshape(n_head * rows, heads * DH)
         q_parts = [moved, across(moved, "cache", n_cache, 1)]
     all_tok = n_head * queries.shape[0]
     limits = page_limits(page_lists, page_counts, keys.shape[0], min(all_tok, TOK_TILE))
-    keep, send = attend(q_parts, keys, values, limits)
-    width = keep.shape[1]
-    keep = keep.reshape(n_head, rows, width)
-    send = send.reshape(n_head, rows, width)
+    groups = [range(n_head // 2), range(n_head // 2, n_head)] if direct else [range(n_head)]
+    starts = [group[0] * rows for group in groups]
+    starts = starts + [n_head * rows + first for first in starts]
+    states = attend(q_parts, keys, values, limits, starts)
+    width = states[0].shape[1]
+    states = [state.reshape(-1, rows, width) for state in states]
+    states = list(zip(states[: len(groups)], states[len(groups) :]))[::-1]
+    groups = groups[::-1]
+    parts = [None] * n_head
     for bit in bits:
-        theirs = across(send, "cache", n_cache, bit)
-        if bit != bits[-1]:
-            half = keep.shape[1] // 2
-            shapes = [
-                jax.ShapeDtypeStruct((n_head, half, width), jnp.float32),
-                jax.ShapeDtypeStruct((n_head, half, width), jnp.int16),
-            ]
-            keep, send = merge(keep, theirs, heads, shapes, False)
-        elif direct:
-            shapes = [jax.ShapeDtypeStruct((share, width), jnp.int16)] * n_head
-            blocks = merge(keep, theirs, heads, shapes, True)
-            parts = [blocks[0]] + [across(blocks[k], "head", n_head, k) for k in range(1, n_head)]
-        else:
-            shapes = [jax.ShapeDtypeStruct((n_head, share, width), jnp.int16)]
-            (blocks,) = merge(keep, theirs, heads, shapes, True)
-            parts = [lax.all_to_all(blocks, "head", split_axis=0, concat_axis=0, tiled=True)]
+        arrived = [across(send, "cache", n_cache, bit) for _, send in states]
+        for g, (keep, _) in enumerate(states):
+            size, length, _ = keep.shape
+            if bit != bits[-1]:
+                shapes = [
+                    jax.ShapeDtypeStruct((size, length // 2, width), jnp.float32),
+                    jax.ShapeDtypeStruct((size, length // 2, width), jnp.int16),
+                ]
+                states[g] = merge(keep, arrived[g], heads, shapes, False)
+            elif direct:
+                shapes = [jax.ShapeDtypeStruct((share, width), jnp.int16)] * size
+                blocks = merge(keep, arrived[g], heads, shapes, True)
+                for k, block in zip(groups[g], blocks):
+                    parts[k] = across(block, "head", n_head, k) if k else block
+            else:
+                shapes = [jax.ShapeDtypeStruct((n_head, share, width), jnp.int16)]
+                (blocks,) = merge(keep, arrived[g], heads, shapes, True)
+                parts = [lax.all_to_all(blocks, "head", split_axis=0, concat_axis=0, tiled=True)]
     return tuple(place(parts, heads, "head", share))
 
 

time: 47.5 us -> 44.6 us (0.939)
  waiting for transfers between devices: 15 us -> 11.9 us
  local copies, waits for them, and re-layouts: 1.91 us -> 3.68 us
  Pallas kernels: 16.2 us -> 14.9 us
    ppermute x11 -> x13, waiting for transfers between devices: 15 us -> 11.9 us  [across(): return lax.ppermute(value, axis, [(i, i ^ bit) for i in range(size)])]
    slice x0 -> x2, local copies, waits for them, and re-layouts: none -> 2.66 us  [the longest x1 1.33 us: attend(): keys[:, :, :DH]]
    pallas_call x1, Pallas kernels: 14.1 us -> 12.6 us  [attend(): pl.pallas_call(functools.partial(attend_kernel, len(q_parts), starts), in...]
    reshape x1 -> x0, local copies, waits for them, and re-layouts: 1.43 us -> none  [on_device(): shares = queries.reshape(n_cache, share, n_head, heads * DH)]
    dynamic_slice x1, local copies, waits for them, and re-layouts: 0.24 us -> 0.95 us  [pick(): lax.dynamic_slice(queries, ((cache_at ^ name) * share, at), (share, width))]
    ppermute x11 -> x13, starting transfers between devices: 12 us -> 11.6 us  [across(): return lax.ppermute(value, axis, [(i, i ^ bit) for i in range(size)])]
    pallas_call x2 -> x4, Pallas kernels: 1.09 us -> 1.4 us  [merge(): pl.pallas_call(functools.partial(merge_kernel, heads, last), out_shape=ou...]
  transfers between devices with their start and end apart: 11 -> 13, of which waited for: 9 -> 8; matrix products, arithmetic and copies ran while one was open for 2% -> 8% of each run, Pallas kernels for 0% -> 3%
where the time goes in v3:
time: 44.6 us; the launch traced here: 44.3 us
  Pallas kernels  14.9 us (33%)
  waiting for transfers between devices  11.9 us (27%)
  starting transfers between devices  11.6 us (26%)
  local copies, waits for them, and re-layouts  3.68 us (8%)
  between operations  1.44 us (3%)
  other arithmetic  0.81 us (2%)
    pallas_call x1, Pallas kernels, attend(): pl.pallas_call(functools.partial(attend_kernel, len(q_parts), starts), in...  12.6 us
    ppermute x13, waiting for transfers between devices, across(): return lax.ppermute(value, axis, [(i, i ^ bit) for i in range(size)])  11.9 us
    ppermute x13, starting transfers between devices, across(): return lax.ppermute(value, axis, [(i, i ^ bit) for i in range(size)])  11.6 us
    pallas_call x4, Pallas kernels, merge(): pl.pallas_call(functools.partial(merge_kernel, heads, last), out_shape=ou...  1.4 us
    slice x1, local copies, waits for them, and re-layouts, attend(): keys[:, :, :DH]  1.33 us
    slice x1, local copies, waits for them, and re-layouts, attend(): values[:, :, :DH]  1.33 us
    dynamic_slice x1, local copies, waits for them, and re-layouts, pick(): lax.dynamic_slice(queries, ((cache_at ^ name) * share, at), (share, width))  0.95 us
    pallas_call x1, Pallas kernels, place(): pl.pallas_call(functools.partial(place_kernel, heads, axis), out_shape=[j...  0.94 us
  transfers between devices with their start and end apart: 13, of which 8 were waited for; matrix products, arithmetic and copies ran while one was open for 8% of the time, Pallas kernels for 3%

profile of v3, /device:TPU:0, one launch (start us, length us, event | category | flops | bytes accessed | tf_op | source)
XLA Modules:
  0.0 44.3 jit_solution(5075005322689063755)
XLA Ops:
  0.7 0.9 %fusion.2 = (bf16[16,1024]{1,0:T(8,128)(2,1)S(1)}, bf16[16,1024]{1,0:T(8,128)(2,1)S(1)}, bf16[16,1024]{1,0:T(8,128)(2,1)S(1)}, bf16[16,1024]{1,0:T(8,128)(2,1)S(...) fusion(bf16[64,4096]{1,0:T(8,128)(2,1)} %param.5, ...), kind=kLoop, calls=%fused_computation.10 | loop fusion | bytes 655392 | tf_op jit(solution)/shard_map/dynamic_slice | solution.py:291
  1.6 3.1 %collective-permute-start = (bf16[32,1024]{1,0:T(8,128)(2,1)S(1)}, bf16[32,1024]{1,0:T(8,128)(2,1)S(1)}, u32[]{:S(2)}, u32[]{:S(2)}) collective-permute-start(bf16[32,1024]{1,0:T(8,128)(2,1)S(1)} %pad_maximum_fusion.1), channel_id=1, source_target_pairs={{0,4},{4,0},{8,12},{12,8},{1,5},{5,1},{9,13},{13,9},{2,6},{6,2},{1... | collective-permute-start | bytes 196616 | tf_op jit(solution)/shard_map/ppermute | solution.py:263
  4.7 2.6 %collective-permute-start.1 = (bf16[32,1024]{1,0:T(8,128)(2,1)S(1)}, bf16[32,1024]{1,0:T(8,128)(2,1)S(1)}, u32[]{:S(2)}, u32[]{:S(2)}) collective-permute-start(bf16[32,1024]{1,0:T(8,128)(2,1)S(1)} %pad_maximum_fusion.2), channel_id=1, source_target_pairs={{0,8},{4,12},{8,0},{12,4},{1,9},{5,13},{9,1},{13,5},{2,10},{6,14},... | collective-permute-start | bytes 196616 | tf_op jit(solution)/shard_map/ppermute | solution.py:263
  7.3 0.0 collective-permute-start.2
  8.0 0.8 %fusion.1 = pred[32]{0:T(512)(128)(4,1)S(1)} fusion(s32[32]{0:T(128)} %bitcast.11, pred[32]{0:T(512)(128)(4,1)S(1)} %iota_compare_fusion.1), kind=kLoop, calls=%fused_computation.7 | loop fusion | flops 3040 | bytes 192 | tf_op jit(solution)/shard_map/reduce_or | solution.py:269
  8.8 1.3 %slice.6.refs_10_ = bf16[32,128,128]{2,1,0:T(8,128)(2,1)S(1)} slice(bf16[32,128,1024]{2,1,0:T(8,128)(2,1)} %refs_8_.1), slice={[0:32], [0:128], [0:128]} | slice | bytes 2097152 | tf_op jit(solution)/shard_map/slice | solution.py:143
  10.1 1.3 %slice.7.refs_11_ = bf16[32,128,128]{2,1,0:T(8,128)(2,1)S(1)} slice(bf16[32,128,1024]{2,1,0:T(8,128)(2,1)} %refs_9_.1), slice={[0:32], [0:128], [0:128]} | slice | bytes 2097152 | tf_op jit(solution)/shard_map/slice | solution.py:143
  11.4 0.0 collective-permute-done.refs_1_
  11.5 0.1 collective-permute-start.3
  11.5 0.5 %collective-permute-done.1.refs_2_ = bf16[32,1024]{1,0:T(8,128)(2,1)S(1)} collective-permute-done((bf16[32,1024]{1,0:T(8,128)(2,1)S(1)}, bf16[32,1024]{1,0:T(8,128)(2,1)S(1)}, u32[]{:S(2)}, u32[]{:S(2)}) %collective-permute-start.1) | collective-permute-done | bytes 65568 | tf_op jit(solution)/shard_map/ppermute | solution.py:263
  12.0 0.0 collective-permute-start.4
  12.0 1.4 %collective-permute-done.2.refs_3_ = bf16[32,1024]{1,0:T(8,128)(2,1)S(1)} collective-permute-done((bf16[32,1024]{1,0:T(8,128)(2,1)S(1)}, bf16[32,1024]{1,0:T(8,128)(2,1)S(1)}, u32[]{:S(2)}, u32[]{:S(2)}) %collective-permute-start.2) | collective-permute-done | bytes 65568 | tf_op jit(solution)/shard_map/ppermute | solution.py:263
  13.4 0.0 collective-permute-start.5
  13.4 0.0 collective-permute-done.3.refs_5_
  13.4 0.0 collective-permute-done.4.refs_6_
  13.4 1.2 %collective-permute-done.5.refs_7_ = bf16[32,1024]{1,0:T(8,128)(2,1)S(1)} collective-permute-done((bf16[32,1024]{1,0:T(8,128)(2,1)S(1)}, bf16[32,1024]{1,0:T(8,128)(2,1)S(1)}, u32[]{:S(2)}, u32[]{:S(2)}) %collective-permute-start.5) | collective-permute-done | bytes 65568 | tf_op jit(solution)/shard_map/ppermute | solution.py:263
  14.7 0.1 broadcast_in_dim.18.limits_ref
  14.7 12.6 %attend.1 = (f32[64,1152]{1,0:T(8,128)S(1)}, f32[64,1152]{1,0:T(8,128)S(1)}, f32[64,1152]{1,0:T(8,128)S(1)}, f32[64,1152]{1,0:T(8,128)S(1)}) custom-call(f32[32,256]{1,0:T(8,128)S(1)} %broadcast_in_dim.18.limits_ref, bf16[32,1024]{1,0:T(8,128)(2,1)S(1)} %get-tuple-element.36.refs_0_, bf16[32,1024]{1,0:T(8,128)(2,1)S(1)} %collective-permute-done.refs_1_, ...), custom_call_target="tpu_custom_call" | custom-call | tf_op jit(solution)/shard_map/attend/pallas_call | solution.py:128
  27.3 0.2 collective-permute-start.6
  27.5 0.3 collective-permute-start.9
  27.9 1.1 %collective-permute-done.6.theirs_ref = f32[2,32,1152]{2,1,0:T(8,128)S(1)} collective-permute-done((f32[2,32,1152]{2,1,0:T(8,128)S(1)}, f32[2,32,1152]{2,1,0:T(8,128)S(1)}, u32[]{:S(2)}, u32[]{:S(2)}) %collective-permute-start.6) | collective-permute-done | bytes 294944 | tf_op jit(solution)/shard_map/ppermute | solution.py:263
  28.9 0.3 merge.4
  29.3 1.6 %collective-permute-start.7 = (s16[2,16,1152]{2,1,0:T(8,128)(2,1)S(1)}, s16[2,16,1152]{2,1,0:T(8,128)(2,1)S(1)}, u32[]{:S(2)}, u32[]{:S(2)}) collective-permute-start(s16[2,16,1152]{2,1,0:T(8,128)(2,1)S(1)} %get-tuple-element.17), channel_id=1, source_target_pairs={{0,2},{1,3},{2,0},{3,1},{4,6},{5,7},{6,4},{7,5},{8,10},{9,11},{10,... | collective-permute-start | bytes 221192 | tf_op jit(solution)/shard_map/ppermute | solution.py:263
  30.8 0.0 collective-permute-done.9.theirs_ref
  30.8 0.3 merge.6
  31.2 0.6 %collective-permute-start.10 = (s16[2,16,1152]{2,1,0:T(8,128)(2,1)S(1)}, s16[2,16,1152]{2,1,0:T(8,128)(2,1)S(1)}, u32[]{:S(2)}, u32[]{:S(2)}) collective-permute-start(s16[2,16,1152]{2,1,0:T(8,128)(2,1)S(1)} %get-tuple-element.23), channel_id=1, source_target_pairs={{0,2},{1,3},{2,0},{3,1},{4,6},{5,7},{6,4},{7,5},{8,10},{9,11},{10,... | collective-permute-start | bytes 221192 | tf_op jit(solution)/shard_map/ppermute | solution.py:263
  31.8 1.9 %collective-permute-done.7.theirs_ref = s16[2,16,1152]{2,1,0:T(8,128)(2,1)S(1)} collective-permute-done((s16[2,16,1152]{2,1,0:T(8,128)(2,1)S(1)}, s16[2,16,1152]{2,1,0:T(8,128)(2,1)S(1)}, u32[]{:S(2)}, u32[]{:S(2)}) %collective-permute-start.7) | collective-permute-done | bytes 73760 | tf_op jit(solution)/shard_map/ppermute | solution.py:263
  33.7 0.4 merge.5
  34.1 0.1 collective-permute-start.8
  34.1 1.4 %collective-permute-done.10.theirs_ref = s16[2,16,1152]{2,1,0:T(8,128)(2,1)S(1)} collective-permute-done((s16[2,16,1152]{2,1,0:T(8,128)(2,1)S(1)}, s16[2,16,1152]{2,1,0:T(8,128)(2,1)S(1)}, u32[]{:S(2)}, u32[]{:S(2)}) %collective-permute-start.10) | collective-permute-done | bytes 73760 | tf_op jit(solution)/shard_map/ppermute | solution.py:263
  35.6 0.4 merge.7
  36.0 1.6 %collective-permute-start.11 = (s16[16,1152]{1,0:T(8,128)(2,1)S(1)}, s16[16,1152]{1,0:T(8,128)(2,1)S(1)}, u32[]{:S(2)}, u32[]{:S(2)}) collective-permute-start(s16[16,1152]{1,0:T(8,128)(2,1)S(1)} %get-tuple-element.24), channel_id=1, source_target_pairs={{0,8},{4,12},{8,0},{12,4},{1,9},{5,13},{9,1},{13,5},{2,10},{6,14},... | collective-permute-start | bytes 110600 | tf_op jit(solution)/shard_map/ppermute | solution.py:263
  37.6 1.4 %collective-permute-start.12 = (s16[16,1152]{1,0:T(8,128)(2,1)S(1)}, s16[16,1152]{1,0:T(8,128)(2,1)S(1)}, u32[]{:S(2)}, u32[]{:S(2)}) collective-permute-start(s16[16,1152]{1,0:T(8,128)(2,1)S(1)} %get-tuple-element.25), channel_id=1, source_target_pairs={{0,12},{4,8},{8,4},{12,0},{1,13},{5,9},{9,5},{13,1},{2,14},{6,10},... | collective-permute-start | bytes 110600 | tf_op jit(solution)/shard_map/ppermute | solution.py:263
  39.0 0.0 collective-permute-done.8.refs_1_
  39.0 2.7 %collective-permute-done.11.refs_2_ = s16[16,1152]{1,0:T(8,128)(2,1)S(1)} collective-permute-done((s16[16,1152]{1,0:T(8,128)(2,1)S(1)}, s16[16,1152]{1,0:T(8,128)(2,1)S(1)}, u32[]{:S(2)}, u32[]{:S(2)}) %collective-permute-start.11) | collective-permute-done | bytes 36896 | tf_op jit(solution)/shard_map/ppermute | solution.py:263
  41.7 1.7 %collective-permute-done.12.refs_3_ = s16[16,1152]{1,0:T(8,128)(2,1)S(1)} collective-permute-done((s16[16,1152]{1,0:T(8,128)(2,1)S(1)}, s16[16,1152]{1,0:T(8,128)(2,1)S(1)}, u32[]{:S(2)}, u32[]{:S(2)}) %collective-permute-start.12) | collective-permute-done | bytes 36896 | tf_op jit(solution)/shard_map/ppermute | solution.py:263
  43.4 0.9 %place.1 = (f32[16,4096]{1,0:T(8,128)}, f32[16,32]{1,0:T(8,128)}) custom-call(s16[16,1152]{1,0:T(8,128)(2,1)S(1)} %get-tuple-element.18.refs_0_, s16[16,1152]{1,0:T(8,128)(2,1)S(1)} %collective-permute-done.8.refs_1_, s16[16,1152]{1,0:T(8,128)(2,1)S(1)} %collective-permute-done.11.refs_2_, s16[16,1152]{1,0:T(8,128)(2,1)S(1)} %collective-permute-done.12.refs_3_), custom_call_target="tpu_custom_call" | custom-call | tf_op jit(solution)/shard_map/place/pallas_call | solution.py:251
  (6 shorter events, 0.0 us)
Async XLA Ops:
  1.6 9.8 %collective-permute-start = (bf16[32,1024]{1,0:T(8,128)(2,1)S(1)}, bf16[32,1024]{1,0:T(8,128)(2,1)S(1)}, u32[]{:S(2)}, u32[]{:S(2)}) collective-permute-start(bf16[32,1024]{1,0:T(8,128)(2,1)S(1)} %pad_maximum_fusion.1), channel_id=1, source_target_pairs={{0,4},{4,0},{8,12},{12,8},{1,5},{5,1},{9,13},{13,9},{2,6},{6,2},{1... | collective-permute-start | bytes 196616 | tf_op jit(solution)/shard_map/ppermute | solution.py:263
  4.7 7.3 %collective-permute-start.1 = (bf16[32,1024]{1,0:T(8,128)(2,1)S(1)}, bf16[32,1024]{1,0:T(8,128)(2,1)S(1)}, u32[]{:S(2)}, u32[]{:S(2)}) collective-permute-start(bf16[32,1024]{1,0:T(8,128)(2,1)S(1)} %pad_maximum_fusion.2), channel_id=1, source_target_pairs={{0,8},{4,12},{8,0},{12,4},{1,9},{5,13},{9,1},{13,5},{2,10},{6,14},... | collective-permute-start | bytes 196616 | tf_op jit(solution)/shard_map/ppermute | solution.py:263
  7.3 6.1 %collective-permute-start.2 = (bf16[32,1024]{1,0:T(8,128)(2,1)S(1)}, bf16[32,1024]{1,0:T(8,128)(2,1)S(1)}, u32[]{:S(2)}, u32[]{:S(2)}) collective-permute-start(bf16[32,1024]{1,0:T(8,128)(2,1)S(1)} %pad_maximum_fusion.3), channel_id=1, source_target_pairs={{0,12},{4,8},{8,4},{12,0},{1,13},{5,9},{9,5},{13,1},{2,14},{6,10},... | collective-permute-start | bytes 196616 | tf_op jit(solution)/shard_map/ppermute | solution.py:263
  11.5 2.0 %collective-permute-start.3 = (bf16[32,1024]{1,0:T(8,128)(2,1)S(1)}, bf16[32,1024]{1,0:T(8,128)(2,1)S(1)}, u32[]{:S(2)}, u32[]{:S(2)}) collective-permute-start(bf16[32,1024]{1,0:T(8,128)(2,1)S(1)} %collective-permute-done.refs_1_), channel_id=1, source_target_pairs={{0,1},{1,0},{2,3},{3,2},{4,5},{5,4},{6,7},{7,6},{8,9},{9,8},{10,11... | collective-permute-start | bytes 196616 | tf_op jit(solution)/shard_map/ppermute | solution.py:263
  12.0 1.4 %collective-permute-start.4 = (bf16[32,1024]{1,0:T(8,128)(2,1)S(1)}, bf16[32,1024]{1,0:T(8,128)(2,1)S(1)}, u32[]{:S(2)}, u32[]{:S(2)}) collective-permute-start(bf16[32,1024]{1,0:T(8,128)(2,1)S(1)} %collective-permute-done.1.refs_2_), channel_id=1, source_target_pairs={{0,1},{1,0},{2,3},{3,2},{4,5},{5,4},{6,7},{7,6},{8,9},{9,8},{10,11... | collective-permute-start | bytes 196616 | tf_op jit(solution)/shard_map/ppermute | solution.py:263
  13.4 1.3 %collective-permute-start.5 = (bf16[32,1024]{1,0:T(8,128)(2,1)S(1)}, bf16[32,1024]{1,0:T(8,128)(2,1)S(1)}, u32[]{:S(2)}, u32[]{:S(2)}) collective-permute-start(bf16[32,1024]{1,0:T(8,128)(2,1)S(1)} %collective-permute-done.2.refs_3_), channel_id=1, source_target_pairs={{0,1},{1,0},{2,3},{3,2},{4,5},{5,4},{6,7},{7,6},{8,9},{9,8},{10,11... | collective-permute-start | bytes 196616 | tf_op jit(solution)/shard_map/ppermute | solution.py:263
  27.3 1.6 %collective-permute-start.6 = (f32[2,32,1152]{2,1,0:T(8,128)S(1)}, f32[2,32,1152]{2,1,0:T(8,128)S(1)}, u32[]{:S(2)}, u32[]{:S(2)}) collective-permute-start(f32[2,32,1152]{2,1,0:T(8,128)S(1)} %bitcast.10), channel_id=1, source_target_pairs={{0,1},{1,0},{2,3},{3,2},{4,5},{5,4},{6,7},{7,6},{8,9},{9,8},{10,11... | collective-permute-start | bytes 884744 | tf_op jit(solution)/shard_map/ppermute | solution.py:263
  27.5 3.3 %collective-permute-start.9 = (f32[2,32,1152]{2,1,0:T(8,128)S(1)}, f32[2,32,1152]{2,1,0:T(8,128)S(1)}, u32[]{:S(2)}, u32[]{:S(2)}) collective-permute-start(f32[2,32,1152]{2,1,0:T(8,128)S(1)} %bitcast.9), channel_id=1, source_target_pairs={{0,1},{1,0},{2,3},{3,2},{4,5},{5,4},{6,7},{7,6},{8,9},{9,8},{10,11... | collective-permute-start | bytes 884744 | tf_op jit(solution)/shard_map/ppermute | solution.py:263
  29.3 4.4 %collective-permute-start.7 = (s16[2,16,1152]{2,1,0:T(8,128)(2,1)S(1)}, s16[2,16,1152]{2,1,0:T(8,128)(2,1)S(1)}, u32[]{:S(2)}, u32[]{:S(2)}) collective-permute-start(s16[2,16,1152]{2,1,0:T(8,128)(2,1)S(1)} %get-tuple-element.17), channel_id=1, source_target_pairs={{0,2},{1,3},{2,0},{3,1},{4,6},{5,7},{6,4},{7,5},{8,10},{9,11},{10,... | collective-permute-start | bytes 221192 | tf_op jit(solution)/shard_map/ppermute | solution.py:263
  31.2 4.4 %collective-permute-start.10 = (s16[2,16,1152]{2,1,0:T(8,128)(2,1)S(1)}, s16[2,16,1152]{2,1,0:T(8,128)(2,1)S(1)}, u32[]{:S(2)}, u32[]{:S(2)}) collective-permute-start(s16[2,16,1152]{2,1,0:T(8,128)(2,1)S(1)} %get-tuple-element.23), channel_id=1, source_target_pairs={{0,2},{1,3},{2,0},{3,1},{4,6},{5,7},{6,4},{7,5},{8,10},{9,11},{10,... | collective-permute-start | bytes 221192 | tf_op jit(solution)/shard_map/ppermute | solution.py:263
  34.1 4.9 %collective-permute-start.8 = (s16[16,1152]{1,0:T(8,128)(2,1)S(1)}, s16[16,1152]{1,0:T(8,128)(2,1)S(1)}, u32[]{:S(2)}, u32[]{:S(2)}) collective-permute-start(s16[16,1152]{1,0:T(8,128)(2,1)S(1)} %get-tuple-element.19), channel_id=1, source_target_pairs={{0,4},{4,0},{8,12},{12,8},{1,5},{5,1},{9,13},{13,9},{2,6},{6,2},{1... | collective-permute-start | bytes 110600 | tf_op jit(solution)/shard_map/ppermute | solution.py:263
  36.0 5.7 %collective-permute-start.11 = (s16[16,1152]{1,0:T(8,128)(2,1)S(1)}, s16[16,1152]{1,0:T(8,128)(2,1)S(1)}, u32[]{:S(2)}, u32[]{:S(2)}) collective-permute-start(s16[16,1152]{1,0:T(8,128)(2,1)S(1)} %get-tuple-element.24), channel_id=1, source_target_pairs={{0,8},{4,12},{8,0},{12,4},{1,9},{5,13},{9,1},{13,5},{2,10},{6,14},... | collective-permute-start | bytes 110600 | tf_op jit(solution)/shard_map/ppermute | solution.py:263
  37.6 5.8 %collective-permute-start.12 = (s16[16,1152]{1,0:T(8,128)(2,1)S(1)}, s16[16,1152]{1,0:T(8,128)(2,1)S(1)}, u32[]{:S(2)}, u32[]{:S(2)}) collective-permute-start(s16[16,1152]{1,0:T(8,128)(2,1)S(1)} %get-tuple-element.25), channel_id=1, source_target_pairs={{0,12},{4,8},{8,4},{12,0},{1,13},{5,9},{9,5},{13,1},{2,14},{6,10},... | collective-permute-start | bytes 110600 | tf_op jit(solution)/shard_map/ppermute | solution.py:263

commit v4 on v3

--- a/solution.py
+++ b/solution.py
@@ -45,7 +45,7 @@
     k_pool[0] = k_first[...]
     v_pool[0] = v_first[...]
     for h in range(heads):
-        rows = [q_ref[:, h * DH : (h + 1) * DH] for q_ref in q_refs]
+        rows = [q_ref[:, h * DH : (h + 1) * DH] for q_ref in q_refs[::-1]]
         q_turned[h] = jnp.concatenate(rows, axis=0).T
     stats[...] = jnp.zeros_like(stats)
     ones = jnp.ones((8, PAGE), jnp.bfloat16)
@@ -140,7 +140,7 @@
         out_shape=outs,
         compiler_params=pltpu.CompilerParams(vmem_limit_bytes=VMEM_LIMIT),
         name="attend",
-    )(limits, *q_parts, keys, values, keys[:, :, :DH], values[:, :, :DH])
+    )(limits, *q_parts[::-1], keys, values, keys[:, :, :DH], values[:, :, :DH])
 
 
 def rounded(x):
@@ -198,7 +198,7 @@
         mine[h] * first[..., h : h + 1] + theirs[h] * second[..., h : h + 1] for h in range(heads)
     ]
     if last:
-        if len(out_refs) == 1:
+        if len(out_refs[0].shape) == 3:
             encode(outs, logs, out_refs[0])
         else:
             for block, out_ref in enumerate(out_refs):
@@ -222,12 +222,12 @@
     )(mine, theirs)
 
 
-def place_kernel(heads, axis, *refs):
+def place_kernel(heads, axis, names, *refs):
     part_refs, (out_ref, logs_ref) = refs[:-2], refs[-2:]
     here = lax.axis_index(axis) if len(part_refs) > 1 else 0
     pieces = []
     if len(part_refs) > 1:
-        for k, part_ref in enumerate(part_refs):
+        for k, part_ref in zip(names, part_refs):
             outs, logs = decode(heads, part_ref)
             at = lax.bitwise_xor(here, k)
             out_ref[:, pl.ds(pl.multiple_of(at * heads * DH, DH), heads * DH)] = jnp.concatenate(
@@ -247,9 +247,9 @@
     logs_ref[...] = jnp.concatenate(columns, axis=-1) * math.log(2.0)
 
 
-def place(parts, heads, axis, share):
+def place(parts, heads, axis, share, names):
     return pl.pallas_call(
-        functools.partial(place_kernel, heads, axis),
+        functools.partial(place_kernel, heads, axis, names),
         out_shape=[
             jax.ShapeDtypeStruct((share, HEADS * DH), jnp.float32),
             jax.ShapeDtypeStruct((share, HEADS), jnp.float32),
@@ -338,7 +338,9 @@
                 shapes = [jax.ShapeDtypeStruct((n_head, share, width), jnp.int16)]
                 (blocks,) = merge(keep, arrived[g], heads, shapes, True)
                 parts = [lax.all_to_all(blocks, "head", split_axis=0, concat_axis=0, tiled=True)]
-    return tuple(place(parts, heads, "head", share))
+    names = list(range(len(parts)))[::-1]
+    parts = [parts[k] for k in names]
+    return tuple(place(parts, heads, "head", share, names))
 
 
 def solution(mesh):

time: 44.6 us -> 42.7 us (0.957)
  waiting for transfers between devices: 11.9 us -> 7.99 us
  starting transfers between devices: 11.6 us -> 13.6 us
    ppermute x13, waiting for transfers between devices: 11.9 us -> 7.99 us  [across(): return lax.ppermute(value, axis, [(i, i ^ bit) for i in range(size)])]
    ppermute x13, starting transfers between devices: 11.6 us -> 13.6 us  [across(): return lax.ppermute(value, axis, [(i, i ^ bit) for i in range(size)])]
  transfers between devices with their start and end apart: 13 -> 13, of which waited for: 8 -> 7; matrix products, arithmetic and copies ran while one was open for 8% -> 8% of each run, Pallas kernels for 3% -> 3%
where the time goes in v4:
time: 42.7 us; the launch traced here: 42.4 us
  Pallas kernels  14.9 us (35%)
  starting transfers between devices  13.6 us (32%)
  waiting for transfers between devices  7.99 us (19%)
  local copies, waits for them, and re-layouts  3.68 us (9%)
  between operations  1.44 us (3%)
  other arithmetic  0.81 us (2%)
    ppermute x13, starting transfers between devices, across(): return lax.ppermute(value, axis, [(i, i ^ bit) for i in range(size)])  13.6 us
    pallas_call x1, Pallas kernels, attend(): pl.pallas_call(functools.partial(attend_kernel, len(q_parts), starts), in...  12.6 us
    ppermute x13, waiting for transfers between devices, across(): return lax.ppermute(value, axis, [(i, i ^ bit) for i in range(size)])  7.99 us
    pallas_call x4, Pallas kernels, merge(): pl.pallas_call(functools.partial(merge_kernel, heads, last), out_shape=ou...  1.4 us
    slice x1, local copies, waits for them, and re-layouts, attend(): values[:, :, :DH]  1.33 us
    slice x1, local copies, waits for them, and re-layouts, attend(): keys[:, :, :DH]  1.33 us
    dynamic_slice x1, local copies, waits for them, and re-layouts, pick(): lax.dynamic_slice(queries, ((cache_at ^ name) * share, at), (share, width))  0.95 us
    pallas_call x1, Pallas kernels, place(): pl.pallas_call(functools.partial(place_kernel, heads, axis, names), out_s...  0.94 us
  transfers between devices with their start and end apart: 13, of which 7 were waited for; matrix products, arithmetic and copies ran while one was open for 8% of the time, Pallas kernels for 3%

profile of v4, /device:TPU:0, one launch (start us, length us, event | category | flops | bytes accessed | tf_op | source)
XLA Modules:
  0.0 42.4 jit_solution(10668443052965215329)
XLA Ops:
  0.7 0.9 %fusion.2 = (bf16[16,1024]{1,0:T(8,128)(2,1)S(1)}, bf16[16,1024]{1,0:T(8,128)(2,1)S(1)}, bf16[16,1024]{1,0:T(8,128)(2,1)S(1)}, bf16[16,1024]{1,0:T(8,128)(2,1)S(...) fusion(bf16[64,4096]{1,0:T(8,128)(2,1)} %param.5, ...), kind=kLoop, calls=%fused_computation.10 | loop fusion | bytes 655392 | tf_op jit(solution)/shard_map/dynamic_slice | solution.py:291
  1.6 5.1 %collective-permute-start = (bf16[32,1024]{1,0:T(8,128)(2,1)S(1)}, bf16[32,1024]{1,0:T(8,128)(2,1)S(1)}, u32[]{:S(2)}, u32[]{:S(2)}) collective-permute-start(bf16[32,1024]{1,0:T(8,128)(2,1)S(1)} %pad_maximum_fusion), channel_id=1, source_target_pairs={{0,12},{4,8},{8,4},{12,0},{1,13},{5,9},{9,5},{13,1},{2,14},{6,10},... | collective-permute-start | bytes 196616 | tf_op jit(solution)/shard_map/ppermute | solution.py:263
  6.8 0.0 collective-permute-start.2
  6.8 0.6 %collective-permute-start.4 = (bf16[32,1024]{1,0:T(8,128)(2,1)S(1)}, bf16[32,1024]{1,0:T(8,128)(2,1)S(1)}, u32[]{:S(2)}, u32[]{:S(2)}) collective-permute-start(bf16[32,1024]{1,0:T(8,128)(2,1)S(1)} %pad_maximum_fusion.2), channel_id=1, source_target_pairs={{0,4},{4,0},{8,12},{12,8},{1,5},{5,1},{9,13},{13,9},{2,6},{6,2},{1... | collective-permute-start | bytes 196616 | tf_op jit(solution)/shard_map/ppermute | solution.py:263
  8.1 0.8 %fusion.1 = pred[32]{0:T(512)(128)(4,1)S(1)} fusion(s32[32]{0:T(128)} %bitcast.11, pred[32]{0:T(512)(128)(4,1)S(1)} %iota_compare_fusion.1), kind=kLoop, calls=%fused_computation.7 | loop fusion | flops 3040 | bytes 192 | tf_op jit(solution)/shard_map/reduce_or | solution.py:269
  8.9 1.3 %slice.6.refs_10_ = bf16[32,128,128]{2,1,0:T(8,128)(2,1)S(1)} slice(bf16[32,128,1024]{2,1,0:T(8,128)(2,1)} %refs_8_.1), slice={[0:32], [0:128], [0:128]} | slice | bytes 2097152 | tf_op jit(solution)/shard_map/slice | solution.py:143
  10.2 1.3 %slice.7.refs_11_ = bf16[32,128,128]{2,1,0:T(8,128)(2,1)S(1)} slice(bf16[32,128,1024]{2,1,0:T(8,128)(2,1)} %refs_9_.1), slice={[0:32], [0:128], [0:128]} | slice | bytes 2097152 | tf_op jit(solution)/shard_map/slice | solution.py:143
  11.5 0.0 collective-permute-done.refs_4_
  11.5 0.1 collective-permute-start.1
  11.6 0.7 %collective-permute-done.2.refs_5_ = bf16[32,1024]{1,0:T(8,128)(2,1)S(1)} collective-permute-done((bf16[32,1024]{1,0:T(8,128)(2,1)S(1)}, bf16[32,1024]{1,0:T(8,128)(2,1)S(1)}, u32[]{:S(2)}, u32[]{:S(2)}) %collective-permute-start.2) | collective-permute-done | bytes 65568 | tf_op jit(solution)/shard_map/ppermute | solution.py:263
  12.4 0.0 collective-permute-start.3
  12.4 0.0 collective-permute-done.4.refs_6_
  12.4 0.5 %collective-permute-start.5 = (bf16[32,1024]{1,0:T(8,128)(2,1)S(1)}, bf16[32,1024]{1,0:T(8,128)(2,1)S(1)}, u32[]{:S(2)}, u32[]{:S(2)}) collective-permute-start(bf16[32,1024]{1,0:T(8,128)(2,1)S(1)} %collective-permute-done.4.refs_6_), channel_id=1, source_target_pairs={{0,1},{1,0},{2,3},{3,2},{4,5},{5,4},{6,7},{7,6},{8,9},{9,8},{10,11... | collective-permute-start | bytes 196616 | tf_op jit(solution)/shard_map/ppermute | solution.py:263
  12.9 0.0 collective-permute-done.1.refs_0_
  12.9 0.7 %collective-permute-done.3.refs_1_ = bf16[32,1024]{1,0:T(8,128)(2,1)S(1)} collective-permute-done((bf16[32,1024]{1,0:T(8,128)(2,1)S(1)}, bf16[32,1024]{1,0:T(8,128)(2,1)S(1)}, u32[]{:S(2)}, u32[]{:S(2)}) %collective-permute-start.3) | collective-permute-done | bytes 65568 | tf_op jit(solution)/shard_map/ppermute | solution.py:263
  13.6 0.2 collective-permute-done.5.refs_2_
  13.8 0.1 broadcast_in_dim.18.limits_ref
  13.8 12.6 %attend.1 = (f32[64,1152]{1,0:T(8,128)S(1)}, f32[64,1152]{1,0:T(8,128)S(1)}, f32[64,1152]{1,0:T(8,128)S(1)}, f32[64,1152]{1,0:T(8,128)S(1)}) custom-call(f32[32,256]{1,0:T(8,128)S(1)} %broadcast_in_dim.18.limits_ref, bf16[32,1024]{1,0:T(8,128)(2,1)S(1)} %collective-permute-done.1.refs_0_, bf16[32,1024]{1,0:T(8,128)(2,1)S(1)} %collective-permute-done.3.refs_1_, ...), custom_call_target="tpu_custom_call" | custom-call | tf_op jit(solution)/shard_map/attend/pallas_call | solution.py:128
  26.4 0.4 collective-permute-start.6
  26.8 0.2 collective-permute-start.10
  27.0 1.1 %collective-permute-done.6.theirs_ref = f32[2,32,1152]{2,1,0:T(8,128)S(1)} collective-permute-done((f32[2,32,1152]{2,1,0:T(8,128)S(1)}, f32[2,32,1152]{2,1,0:T(8,128)S(1)}, u32[]{:S(2)}, u32[]{:S(2)}) %collective-permute-start.6) | collective-permute-done | bytes 294944 | tf_op jit(solution)/shard_map/ppermute | solution.py:263
  28.1 0.3 merge.4
  28.4 1.6 %collective-permute-start.7 = (s16[2,16,1152]{2,1,0:T(8,128)(2,1)S(1)}, s16[2,16,1152]{2,1,0:T(8,128)(2,1)S(1)}, u32[]{:S(2)}, u32[]{:S(2)}) collective-permute-start(s16[2,16,1152]{2,1,0:T(8,128)(2,1)S(1)} %get-tuple-element.17), channel_id=1, source_target_pairs={{0,2},{1,3},{2,0},{3,1},{4,6},{5,7},{6,4},{7,5},{8,10},{9,11},{10,... | collective-permute-start | bytes 221192 | tf_op jit(solution)/shard_map/ppermute | solution.py:263
  30.0 0.0 collective-permute-done.10.theirs_ref
  30.0 0.3 merge.6
  30.4 0.5 %collective-permute-start.11 = (s16[2,16,1152]{2,1,0:T(8,128)(2,1)S(1)}, s16[2,16,1152]{2,1,0:T(8,128)(2,1)S(1)}, u32[]{:S(2)}, u32[]{:S(2)}) collective-permute-start(s16[2,16,1152]{2,1,0:T(8,128)(2,1)S(1)} %get-tuple-element.23), channel_id=1, source_target_pairs={{0,2},{1,3},{2,0},{3,1},{4,6},{5,7},{6,4},{7,5},{8,10},{9,11},{10,... | collective-permute-start | bytes 221192 | tf_op jit(solution)/shard_map/ppermute | solution.py:263
  30.9 2.1 %collective-permute-done.7.theirs_ref = s16[2,16,1152]{2,1,0:T(8,128)(2,1)S(1)} collective-permute-done((s16[2,16,1152]{2,1,0:T(8,128)(2,1)S(1)}, s16[2,16,1152]{2,1,0:T(8,128)(2,1)S(1)}, u32[]{:S(2)}, u32[]{:S(2)}) %collective-permute-start.7) | collective-permute-done | bytes 73760 | tf_op jit(solution)/shard_map/ppermute | solution.py:263
  33.0 0.4 merge.5
  33.4 3.2 %collective-permute-start.8 = (s16[16,1152]{1,0:T(8,128)(2,1)S(1)}, s16[16,1152]{1,0:T(8,128)(2,1)S(1)}, u32[]{:S(2)}, u32[]{:S(2)}) collective-permute-start(s16[16,1152]{1,0:T(8,128)(2,1)S(1)} %get-tuple-element.18), channel_id=1, source_target_pairs={{0,12},{4,8},{8,4},{12,0},{1,13},{5,9},{9,5},{13,1},{2,14},{6,10},... | collective-permute-start | bytes 110600 | tf_op jit(solution)/shard_map/ppermute | solution.py:263
  36.6 0.0 collective-permute-start.9
  36.6 0.0 collective-permute-done.11.theirs_ref
  36.6 0.4 merge.7
  37.0 1.3 %collective-permute-start.12 = (s16[16,1152]{1,0:T(8,128)(2,1)S(1)}, s16[16,1152]{1,0:T(8,128)(2,1)S(1)}, u32[]{:S(2)}, u32[]{:S(2)}) collective-permute-start(s16[16,1152]{1,0:T(8,128)(2,1)S(1)} %get-tuple-element.24), channel_id=1, source_target_pairs={{0,4},{4,0},{8,12},{12,8},{1,5},{5,1},{9,13},{13,9},{2,6},{6,2},{1... | collective-permute-start | bytes 110600 | tf_op jit(solution)/shard_map/ppermute | solution.py:263
  38.3 1.0 %collective-permute-done.8.refs_0_ = s16[16,1152]{1,0:T(8,128)(2,1)S(1)} collective-permute-done((s16[16,1152]{1,0:T(8,128)(2,1)S(1)}, s16[16,1152]{1,0:T(8,128)(2,1)S(1)}, u32[]{:S(2)}, u32[]{:S(2)}) %collective-permute-start.8) | collective-permute-done | bytes 36896 | tf_op jit(solution)/shard_map/ppermute | solution.py:263
  39.2 2.2 %collective-permute-done.9.refs_1_ = s16[16,1152]{1,0:T(8,128)(2,1)S(1)} collective-permute-done((s16[16,1152]{1,0:T(8,128)(2,1)S(1)}, s16[16,1152]{1,0:T(8,128)(2,1)S(1)}, u32[]{:S(2)}, u32[]{:S(2)}) %collective-permute-start.9) | collective-permute-done | bytes 36896 | tf_op jit(solution)/shard_map/ppermute | solution.py:263
  41.5 0.0 collective-permute-done.12.refs_2_
  41.5 0.9 %place.1 = (f32[16,4096]{1,0:T(8,128)}, f32[16,32]{1,0:T(8,128)}) custom-call(s16[16,1152]{1,0:T(8,128)(2,1)S(1)} %collective-permute-done.8.refs_0_, s16[16,1152]{1,0:T(8,128)(2,1)S(1)} %collective-permute-done.9.refs_1_, s16[16,1152]{1,0:T(8,128)(2,1)S(1)} %collective-permute-done.12.refs_2_, s16[16,1152]{1,0:T(8,128)(2,1)S(1)} %get-tuple-element.25.refs_3_), custom_call_target="tpu_custom_call" | custom-call | tf_op jit(solution)/shard_map/place/pallas_call | solution.py:251
  (6 shorter events, 0.0 us)
Async XLA Ops:
  1.6 9.9 %collective-permute-start = (bf16[32,1024]{1,0:T(8,128)(2,1)S(1)}, bf16[32,1024]{1,0:T(8,128)(2,1)S(1)}, u32[]{:S(2)}, u32[]{:S(2)}) collective-permute-start(bf16[32,1024]{1,0:T(8,128)(2,1)S(1)} %pad_maximum_fusion), channel_id=1, source_target_pairs={{0,12},{4,8},{8,4},{12,0},{1,13},{5,9},{9,5},{13,1},{2,14},{6,10},... | collective-permute-start | bytes 196616 | tf_op jit(solution)/shard_map/ppermute | solution.py:263
  6.8 5.6 %collective-permute-start.2 = (bf16[32,1024]{1,0:T(8,128)(2,1)S(1)}, bf16[32,1024]{1,0:T(8,128)(2,1)S(1)}, u32[]{:S(2)}, u32[]{:S(2)}) collective-permute-start(bf16[32,1024]{1,0:T(8,128)(2,1)S(1)} %pad_maximum_fusion.1), channel_id=1, source_target_pairs={{0,8},{4,12},{8,0},{12,4},{1,9},{5,13},{9,1},{13,5},{2,10},{6,14},... | collective-permute-start | bytes 196616 | tf_op jit(solution)/shard_map/ppermute | solution.py:263
  6.8 5.6 %collective-permute-start.4 = (bf16[32,1024]{1,0:T(8,128)(2,1)S(1)}, bf16[32,1024]{1,0:T(8,128)(2,1)S(1)}, u32[]{:S(2)}, u32[]{:S(2)}) collective-permute-start(bf16[32,1024]{1,0:T(8,128)(2,1)S(1)} %pad_maximum_fusion.2), channel_id=1, source_target_pairs={{0,4},{4,0},{8,12},{12,8},{1,5},{5,1},{9,13},{13,9},{2,6},{6,2},{1... | collective-permute-start | bytes 196616 | tf_op jit(solution)/shard_map/ppermute | solution.py:263
  11.5 1.3 %collective-permute-start.1 = (bf16[32,1024]{1,0:T(8,128)(2,1)S(1)}, bf16[32,1024]{1,0:T(8,128)(2,1)S(1)}, u32[]{:S(2)}, u32[]{:S(2)}) collective-permute-start(bf16[32,1024]{1,0:T(8,128)(2,1)S(1)} %collective-permute-done.refs_4_), channel_id=1, source_target_pairs={{0,1},{1,0},{2,3},{3,2},{4,5},{5,4},{6,7},{7,6},{8,9},{9,8},{10,11... | collective-permute-start | bytes 196616 | tf_op jit(solution)/shard_map/ppermute | solution.py:263
  12.4 1.3 %collective-permute-start.3 = (bf16[32,1024]{1,0:T(8,128)(2,1)S(1)}, bf16[32,1024]{1,0:T(8,128)(2,1)S(1)}, u32[]{:S(2)}, u32[]{:S(2)}) collective-permute-start(bf16[32,1024]{1,0:T(8,128)(2,1)S(1)} %collective-permute-done.2.refs_5_), channel_id=1, source_target_pairs={{0,1},{1,0},{2,3},{3,2},{4,5},{5,4},{6,7},{7,6},{8,9},{9,8},{10,11... | collective-permute-start | bytes 196616 | tf_op jit(solution)/shard_map/ppermute | solution.py:263
  12.4 1.4 %collective-permute-start.5 = (bf16[32,1024]{1,0:T(8,128)(2,1)S(1)}, bf16[32,1024]{1,0:T(8,128)(2,1)S(1)}, u32[]{:S(2)}, u32[]{:S(2)}) collective-permute-start(bf16[32,1024]{1,0:T(8,128)(2,1)S(1)} %collective-permute-done.4.refs_6_), channel_id=1, source_target_pairs={{0,1},{1,0},{2,3},{3,2},{4,5},{5,4},{6,7},{7,6},{8,9},{9,8},{10,11... | collective-permute-start | bytes 196616 | tf_op jit(solution)/shard_map/ppermute | solution.py:263
  26.4 1.6 %collective-permute-start.6 = (f32[2,32,1152]{2,1,0:T(8,128)S(1)}, f32[2,32,1152]{2,1,0:T(8,128)S(1)}, u32[]{:S(2)}, u32[]{:S(2)}) collective-permute-start(f32[2,32,1152]{2,1,0:T(8,128)S(1)} %bitcast.10), channel_id=1, source_target_pairs={{0,1},{1,0},{2,3},{3,2},{4,5},{5,4},{6,7},{7,6},{8,9},{9,8},{10,11... | collective-permute-start | bytes 884744 | tf_op jit(solution)/shard_map/ppermute | solution.py:263
  26.8 3.2 %collective-permute-start.10 = (f32[2,32,1152]{2,1,0:T(8,128)S(1)}, f32[2,32,1152]{2,1,0:T(8,128)S(1)}, u32[]{:S(2)}, u32[]{:S(2)}) collective-permute-start(f32[2,32,1152]{2,1,0:T(8,128)S(1)} %bitcast.9), channel_id=1, source_target_pairs={{0,1},{1,0},{2,3},{3,2},{4,5},{5,4},{6,7},{7,6},{8,9},{9,8},{10,11... | collective-permute-start | bytes 884744 | tf_op jit(solution)/shard_map/ppermute | solution.py:263
  28.4 4.6 %collective-permute-start.7 = (s16[2,16,1152]{2,1,0:T(8,128)(2,1)S(1)}, s16[2,16,1152]{2,1,0:T(8,128)(2,1)S(1)}, u32[]{:S(2)}, u32[]{:S(2)}) collective-permute-start(s16[2,16,1152]{2,1,0:T(8,128)(2,1)S(1)} %get-tuple-element.17), channel_id=1, source_target_pairs={{0,2},{1,3},{2,0},{3,1},{4,6},{5,7},{6,4},{7,5},{8,10},{9,11},{10,... | collective-permute-start | bytes 221192 | tf_op jit(solution)/shard_map/ppermute | solution.py:263
  30.4 6.2 %collective-permute-start.11 = (s16[2,16,1152]{2,1,0:T(8,128)(2,1)S(1)}, s16[2,16,1152]{2,1,0:T(8,128)(2,1)S(1)}, u32[]{:S(2)}, u32[]{:S(2)}) collective-permute-start(s16[2,16,1152]{2,1,0:T(8,128)(2,1)S(1)} %get-tuple-element.23), channel_id=1, source_target_pairs={{0,2},{1,3},{2,0},{3,1},{4,6},{5,7},{6,4},{7,5},{8,10},{9,11},{10,... | collective-permute-start | bytes 221192 | tf_op jit(solution)/shard_map/ppermute | solution.py:263
  33.4 5.9 %collective-permute-start.8 = (s16[16,1152]{1,0:T(8,128)(2,1)S(1)}, s16[16,1152]{1,0:T(8,128)(2,1)S(1)}, u32[]{:S(2)}, u32[]{:S(2)}) collective-permute-start(s16[16,1152]{1,0:T(8,128)(2,1)S(1)} %get-tuple-element.18), channel_id=1, source_target_pairs={{0,12},{4,8},{8,4},{12,0},{1,13},{5,9},{9,5},{13,1},{2,14},{6,10},... | collective-permute-start | bytes 110600 | tf_op jit(solution)/shard_map/ppermute | solution.py:263
  36.6 4.9 %collective-permute-start.9 = (s16[16,1152]{1,0:T(8,128)(2,1)S(1)}, s16[16,1152]{1,0:T(8,128)(2,1)S(1)}, u32[]{:S(2)}, u32[]{:S(2)}) collective-permute-start(s16[16,1152]{1,0:T(8,128)(2,1)S(1)} %get-tuple-element.19), channel_id=1, source_target_pairs={{0,8},{4,12},{8,0},{12,4},{1,9},{5,13},{9,1},{13,5},{2,10},{6,14},... | collective-permute-start | bytes 110600 | tf_op jit(solution)/shard_map/ppermute | solution.py:263
  37.0 4.5 %collective-permute-start.12 = (s16[16,1152]{1,0:T(8,128)(2,1)S(1)}, s16[16,1152]{1,0:T(8,128)(2,1)S(1)}, u32[]{:S(2)}, u32[]{:S(2)}) collective-permute-start(s16[16,1152]{1,0:T(8,128)(2,1)S(1)} %get-tuple-element.24), channel_id=1, source_target_pairs={{0,4},{4,0},{8,12},{12,8},{1,5},{5,1},{9,13},{13,9},{2,6},{6,2},{1... | collective-permute-start | bytes 110600 | tf_op jit(solution)/shard_map/ppermute | solution.py:263

commit v5 on v4

--- a/solution.py
+++ b/solution.py
@@ -115,6 +115,30 @@
                 ]
 
 
+def first_kernel(k_hbm, v_hbm, k_ref, v_ref, sems):
+    copies = [
+        pltpu.make_async_copy(k_hbm.at[:, :, :DH], k_ref, sems.at[0]),
+        pltpu.make_async_copy(v_hbm.at[:, :, :DH], v_ref, sems.at[1]),
+    ]
+    for copy in copies:
+        copy.start()
+    for copy in copies:
+        copy.wait()
+
+
+def first_head(keys, values):
+    out = jax.ShapeDtypeStruct(keys.shape[:2] + (DH,), keys.dtype)
+    return pl.pallas_call(
+        first_kernel,
+        in_specs=[pl.BlockSpec(memory_space=pl.ANY)] * 2,
+        out_specs=[pl.BlockSpec(memory_space=pltpu.VMEM)] * 2,
+        scratch_shapes=[pltpu.SemaphoreType.DMA((2,))],
+        out_shape=[out, out],
+        compiler_params=pltpu.CompilerParams(vmem_limit_bytes=VMEM_LIMIT),
+        name="first_head",
+    )(keys, values)
+
+
 def attend(q_parts, keys, values, limits, starts):
     all_tok = sum(part.shape[0] for part in q_parts)
     pool = keys.shape[0]
@@ -140,7 +164,7 @@
         out_shape=outs,
         compiler_params=pltpu.CompilerParams(vmem_limit_bytes=VMEM_LIMIT),
         name="attend",
-    )(limits, *q_parts[::-1], keys, values, keys[:, :, :DH], values[:, :, :DH])
+    )(limits, *q_parts[::-1], keys, values, *first_head(keys, values))
 
 
 def rounded(x):

time: 42.7 us -> 42.2 us (0.988)
  local copies, waits for them, and re-layouts: 3.68 us -> 1.02 us
  Pallas kernels: 14.9 us -> 16.5 us
  waiting for transfers between devices: 7.99 us -> 8.6 us
    slice x2 -> x0, local copies, waits for them, and re-layouts: 2.66 us -> none  [the longest x1 1.33 us: attend(): values[:, :, :DH]]
    pallas_call x0 -> x1, Pallas kernels: none -> 1.62 us  [first_head(): pl.pallas_call(first_kernel, in_specs=[pl.BlockSpec(memory_space=pl.ANY)]...]
    ppermute x13, waiting for transfers between devices: 7.99 us -> 8.6 us  [across(): return lax.ppermute(value, axis, [(i, i ^ bit) for i in range(size)])]
  transfers between devices with their start and end apart: 13 -> 13, of which waited for: 7 -> 7; matrix products, arithmetic and copies ran while one was open for 8% -> 2% of each run, Pallas kernels for 3% -> 7%
where the time goes in v5:
time: 42.2 us; the launch traced here: 42 us
  Pallas kernels  16.5 us (39%)
  starting transfers between devices  13.6 us (32%)
  waiting for transfers between devices  8.6 us (20%)
  between operations  1.43 us (3%)
  local copies, waits for them, and re-layouts  1.02 us (2%)
  other arithmetic  0.81 us (2%)
    ppermute x13, starting transfers between devices, across(): return lax.ppermute(value, axis, [(i, i ^ bit) for i in range(size)])  13.6 us
    pallas_call x1, Pallas kernels, attend(): pl.pallas_call(functools.partial(attend_kernel, len(q_parts), starts), in...  12.6 us
    ppermute x13, waiting for transfers between devices, across(): return lax.ppermute(value, axis, [(i, i ^ bit) for i in range(size)])  8.6 us
    pallas_call x1, Pallas kernels, first_head(): pl.pallas_call(first_kernel, in_specs=[pl.BlockSpec(memory_space=pl.ANY)]...  1.62 us
    pallas_call x4, Pallas kernels, merge(): pl.pallas_call(functools.partial(merge_kernel, heads, last), out_shape=ou...  1.4 us
    dynamic_slice x1, local copies, waits for them, and re-layouts, pick(): lax.dynamic_slice(queries, ((cache_at ^ name) * share, at), (share, width))  0.95 us
    pallas_call x1, Pallas kernels, place(): pl.pallas_call(functools.partial(place_kernel, heads, axis, names), out_s...  0.94 us
  transfers between devices with their start and end apart: 13, of which 7 were waited for; matrix products, arithmetic and copies ran while one was open for 2% of the time, Pallas kernels for 7%

profile of v5, /device:TPU:0, one launch (start us, length us, event | category | flops | bytes accessed | tf_op | source)
XLA Modules:
  0.0 42.0 jit_solution(16416623819493125919)
XLA Ops:
  0.7 0.9 %fusion.2 = (bf16[16,1024]{1,0:T(8,128)(2,1)S(1)}, bf16[16,1024]{1,0:T(8,128)(2,1)S(1)}, bf16[16,1024]{1,0:T(8,128)(2,1)S(1)}, bf16[16,1024]{1,0:T(8,128)(2,1)S(...) fusion(bf16[64,4096]{1,0:T(8,128)(2,1)} %param.5, ...), kind=kLoop, calls=%fused_computation.10 | loop fusion | bytes 655392 | tf_op jit(solution)/shard_map/dynamic_slice | solution.py:315
  1.6 5.1 %collective-permute-start = (bf16[32,1024]{1,0:T(8,128)(2,1)S(1)}, bf16[32,1024]{1,0:T(8,128)(2,1)S(1)}, u32[]{:S(2)}, u32[]{:S(2)}) collective-permute-start(bf16[32,1024]{1,0:T(8,128)(2,1)S(1)} %pad_maximum_fusion), channel_id=1, source_target_pairs={{0,12},{4,8},{8,4},{12,0},{1,13},{5,9},{9,5},{13,1},{2,14},{6,10},... | collective-permute-start | bytes 196616 | tf_op jit(solution)/shard_map/ppermute | solution.py:287
  6.8 0.0 collective-permute-start.2
  6.8 0.6 %collective-permute-start.4 = (bf16[32,1024]{1,0:T(8,128)(2,1)S(1)}, bf16[32,1024]{1,0:T(8,128)(2,1)S(1)}, u32[]{:S(2)}, u32[]{:S(2)}) collective-permute-start(bf16[32,1024]{1,0:T(8,128)(2,1)S(1)} %pad_maximum_fusion.2), channel_id=1, source_target_pairs={{0,4},{4,0},{8,12},{12,8},{1,5},{5,1},{9,13},{13,9},{2,6},{6,2},{1... | collective-permute-start | bytes 196616 | tf_op jit(solution)/shard_map/ppermute | solution.py:287
  8.1 0.8 %fusion.1 = pred[32]{0:T(512)(128)(4,1)S(1)} fusion(s32[32]{0:T(128)} %bitcast.11, pred[32]{0:T(512)(128)(4,1)S(1)} %iota_compare_fusion.1), kind=kLoop, calls=%fused_computation.7 | loop fusion | flops 3040 | bytes 192 | tf_op jit(solution)/shard_map/reduce_or | solution.py:293
  8.9 1.6 %first_head.1 = (bf16[32,128,128]{2,1,0:T(8,128)(2,1)S(1)}, bf16[32,128,128]{2,1,0:T(8,128)(2,1)S(1)}) custom-call(bf16[32,128,1024]{2,1,0:T(8,128)(2,1)} %refs_8_.1, bf16[32,128,1024]{2,1,0:T(8,128)(2,1)} %refs_9_.1), custom_call_target="tpu_custom_call" | custom-call | tf_op jit(solution)/shard_map/first_head/pallas_call | solution.py:131
  10.5 0.0 collective-permute-done.refs_4_
  10.5 0.1 collective-permute-start.1
  10.6 1.8 %collective-permute-done.2.refs_5_ = bf16[32,1024]{1,0:T(8,128)(2,1)S(1)} collective-permute-done((bf16[32,1024]{1,0:T(8,128)(2,1)S(1)}, bf16[32,1024]{1,0:T(8,128)(2,1)S(1)}, u32[]{:S(2)}, u32[]{:S(2)}) %collective-permute-start.2) | collective-permute-done | bytes 65568 | tf_op jit(solution)/shard_map/ppermute | solution.py:287
  12.4 0.0 collective-permute-start.3
  12.4 0.0 collective-permute-done.4.refs_6_
  12.4 0.5 %collective-permute-start.5 = (bf16[32,1024]{1,0:T(8,128)(2,1)S(1)}, bf16[32,1024]{1,0:T(8,128)(2,1)S(1)}, u32[]{:S(2)}, u32[]{:S(2)}) collective-permute-start(bf16[32,1024]{1,0:T(8,128)(2,1)S(1)} %collective-permute-done.4.refs_6_), channel_id=1, source_target_pairs={{0,1},{1,0},{2,3},{3,2},{4,5},{5,4},{6,7},{7,6},{8,9},{9,8},{10,11... | collective-permute-start | bytes 196616 | tf_op jit(solution)/shard_map/ppermute | solution.py:287
  12.9 0.0 collective-permute-done.1.refs_0_
  12.9 0.7 %collective-permute-done.3.refs_1_ = bf16[32,1024]{1,0:T(8,128)(2,1)S(1)} collective-permute-done((bf16[32,1024]{1,0:T(8,128)(2,1)S(1)}, bf16[32,1024]{1,0:T(8,128)(2,1)S(1)}, u32[]{:S(2)}, u32[]{:S(2)}) %collective-permute-start.3) | collective-permute-done | bytes 65568 | tf_op jit(solution)/shard_map/ppermute | solution.py:287
  13.6 0.2 collective-permute-done.5.refs_2_
  13.8 0.1 broadcast_in_dim.18.limits_ref
  13.8 12.6 %attend.1 = (f32[64,1152]{1,0:T(8,128)S(1)}, f32[64,1152]{1,0:T(8,128)S(1)}, f32[64,1152]{1,0:T(8,128)S(1)}, f32[64,1152]{1,0:T(8,128)S(1)}) custom-call(f32[32,256]{1,0:T(8,128)S(1)} %broadcast_in_dim.18.limits_ref, bf16[32,1024]{1,0:T(8,128)(2,1)S(1)} %collective-permute-done.1.refs_0_, bf16[32,1024]{1,0:T(8,128)(2,1)S(1)} %collective-permute-done.3.refs_1_, ...), custom_call_target="tpu_custom_call" | custom-call | tf_op jit(solution)/shard_map/attend/pallas_call | solution.py:152
  26.4 0.4 collective-permute-start.6
  26.8 0.2 collective-permute-start.10
  27.0 1.1 %collective-permute-done.6.theirs_ref = f32[2,32,1152]{2,1,0:T(8,128)S(1)} collective-permute-done((f32[2,32,1152]{2,1,0:T(8,128)S(1)}, f32[2,32,1152]{2,1,0:T(8,128)S(1)}, u32[]{:S(2)}, u32[]{:S(2)}) %collective-permute-start.6) | collective-permute-done | bytes 294944 | tf_op jit(solution)/shard_map/ppermute | solution.py:287
  28.1 0.3 merge.4
  28.4 1.6 %collective-permute-start.7 = (s16[2,16,1152]{2,1,0:T(8,128)(2,1)S(1)}, s16[2,16,1152]{2,1,0:T(8,128)(2,1)S(1)}, u32[]{:S(2)}, u32[]{:S(2)}) collective-permute-start(s16[2,16,1152]{2,1,0:T(8,128)(2,1)S(1)} %get-tuple-element.21), channel_id=1, source_target_pairs={{0,2},{1,3},{2,0},{3,1},{4,6},{5,7},{6,4},{7,5},{8,10},{9,11},{10,... | collective-permute-start | bytes 221192 | tf_op jit(solution)/shard_map/ppermute | solution.py:287
  30.0 0.0 collective-permute-done.10.theirs_ref
  30.0 0.3 merge.6
  30.4 0.5 %collective-permute-start.11 = (s16[2,16,1152]{2,1,0:T(8,128)(2,1)S(1)}, s16[2,16,1152]{2,1,0:T(8,128)(2,1)S(1)}, u32[]{:S(2)}, u32[]{:S(2)}) collective-permute-start(s16[2,16,1152]{2,1,0:T(8,128)(2,1)S(1)} %get-tuple-element.27), channel_id=1, source_target_pairs={{0,2},{1,3},{2,0},{3,1},{4,6},{5,7},{6,4},{7,5},{8,10},{9,11},{10,... | collective-permute-start | bytes 221192 | tf_op jit(solution)/shard_map/ppermute | solution.py:287
  30.9 2.1 %collective-permute-done.7.theirs_ref = s16[2,16,1152]{2,1,0:T(8,128)(2,1)S(1)} collective-permute-done((s16[2,16,1152]{2,1,0:T(8,128)(2,1)S(1)}, s16[2,16,1152]{2,1,0:T(8,128)(2,1)S(1)}, u32[]{:S(2)}, u32[]{:S(2)}) %collective-permute-start.7) | collective-permute-done | bytes 73760 | tf_op jit(solution)/shard_map/ppermute | solution.py:287
  33.0 0.4 merge.5
  33.4 2.8 %collective-permute-start.8 = (s16[16,1152]{1,0:T(8,128)(2,1)S(1)}, s16[16,1152]{1,0:T(8,128)(2,1)S(1)}, u32[]{:S(2)}, u32[]{:S(2)}) collective-permute-start(s16[16,1152]{1,0:T(8,128)(2,1)S(1)} %get-tuple-element.22), channel_id=1, source_target_pairs={{0,12},{4,8},{8,4},{12,0},{1,13},{5,9},{9,5},{13,1},{2,14},{6,10},... | collective-permute-start | bytes 110600 | tf_op jit(solution)/shard_map/ppermute | solution.py:287
  36.2 0.0 collective-permute-start.9
  36.2 0.0 collective-permute-done.11.theirs_ref
  36.2 0.4 merge.7
  36.6 1.7 %collective-permute-start.12 = (s16[16,1152]{1,0:T(8,128)(2,1)S(1)}, s16[16,1152]{1,0:T(8,128)(2,1)S(1)}, u32[]{:S(2)}, u32[]{:S(2)}) collective-permute-start(s16[16,1152]{1,0:T(8,128)(2,1)S(1)} %get-tuple-element.28), channel_id=1, source_target_pairs={{0,4},{4,0},{8,12},{12,8},{1,5},{5,1},{9,13},{13,9},{2,6},{6,2},{1... | collective-permute-start | bytes 110600 | tf_op jit(solution)/shard_map/ppermute | solution.py:287
  38.3 1.0 %collective-permute-done.8.refs_0_ = s16[16,1152]{1,0:T(8,128)(2,1)S(1)} collective-permute-done((s16[16,1152]{1,0:T(8,128)(2,1)S(1)}, s16[16,1152]{1,0:T(8,128)(2,1)S(1)}, u32[]{:S(2)}, u32[]{:S(2)}) %collective-permute-start.8) | collective-permute-done | bytes 36896 | tf_op jit(solution)/shard_map/ppermute | solution.py:287
  39.3 1.7 %collective-permute-done.9.refs_1_ = s16[16,1152]{1,0:T(8,128)(2,1)S(1)} collective-permute-done((s16[16,1152]{1,0:T(8,128)(2,1)S(1)}, s16[16,1152]{1,0:T(8,128)(2,1)S(1)}, u32[]{:S(2)}, u32[]{:S(2)}) %collective-permute-start.9) | collective-permute-done | bytes 36896 | tf_op jit(solution)/shard_map/ppermute | solution.py:287
  41.0 0.0 collective-permute-done.12.refs_2_
  41.0 0.9 %place.1 = (f32[16,4096]{1,0:T(8,128)}, f32[16,32]{1,0:T(8,128)}) custom-call(s16[16,1152]{1,0:T(8,128)(2,1)S(1)} %collective-permute-done.8.refs_0_, s16[16,1152]{1,0:T(8,128)(2,1)S(1)} %collective-permute-done.9.refs_1_, s16[16,1152]{1,0:T(8,128)(2,1)S(1)} %collective-permute-done.12.refs_2_, s16[16,1152]{1,0:T(8,128)(2,1)S(1)} %get-tuple-element.29.refs_3_), custom_call_target="tpu_custom_call" | custom-call | tf_op jit(solution)/shard_map/place/pallas_call | solution.py:275
  (6 shorter events, 0.0 us)
Async XLA Ops:
  1.6 8.9 %collective-permute-start = (bf16[32,1024]{1,0:T(8,128)(2,1)S(1)}, bf16[32,1024]{1,0:T(8,128)(2,1)S(1)}, u32[]{:S(2)}, u32[]{:S(2)}) collective-permute-start(bf16[32,1024]{1,0:T(8,128)(2,1)S(1)} %pad_maximum_fusion), channel_id=1, source_target_pairs={{0,12},{4,8},{8,4},{12,0},{1,13},{5,9},{9,5},{13,1},{2,14},{6,10},... | collective-permute-start | bytes 196616 | tf_op jit(solution)/shard_map/ppermute | solution.py:287
  6.8 5.6 %collective-permute-start.2 = (bf16[32,1024]{1,0:T(8,128)(2,1)S(1)}, bf16[32,1024]{1,0:T(8,128)(2,1)S(1)}, u32[]{:S(2)}, u32[]{:S(2)}) collective-permute-start(bf16[32,1024]{1,0:T(8,128)(2,1)S(1)} %pad_maximum_fusion.1), channel_id=1, source_target_pairs={{0,8},{4,12},{8,0},{12,4},{1,9},{5,13},{9,1},{13,5},{2,10},{6,14},... | collective-permute-start | bytes 196616 | tf_op jit(solution)/shard_map/ppermute | solution.py:287
  6.8 5.6 %collective-permute-start.4 = (bf16[32,1024]{1,0:T(8,128)(2,1)S(1)}, bf16[32,1024]{1,0:T(8,128)(2,1)S(1)}, u32[]{:S(2)}, u32[]{:S(2)}) collective-permute-start(bf16[32,1024]{1,0:T(8,128)(2,1)S(1)} %pad_maximum_fusion.2), channel_id=1, source_target_pairs={{0,4},{4,0},{8,12},{12,8},{1,5},{5,1},{9,13},{13,9},{2,6},{6,2},{1... | collective-permute-start | bytes 196616 | tf_op jit(solution)/shard_map/ppermute | solution.py:287
  10.5 2.4 %collective-permute-start.1 = (bf16[32,1024]{1,0:T(8,128)(2,1)S(1)}, bf16[32,1024]{1,0:T(8,128)(2,1)S(1)}, u32[]{:S(2)}, u32[]{:S(2)}) collective-permute-start(bf16[32,1024]{1,0:T(8,128)(2,1)S(1)} %collective-permute-done.refs_4_), channel_id=1, source_target_pairs={{0,1},{1,0},{2,3},{3,2},{4,5},{5,4},{6,7},{7,6},{8,9},{9,8},{10,11... | collective-permute-start | bytes 196616 | tf_op jit(solution)/shard_map/ppermute | solution.py:287
  12.4 1.3 %collective-permute-start.3 = (bf16[32,1024]{1,0:T(8,128)(2,1)S(1)}, bf16[32,1024]{1,0:T(8,128)(2,1)S(1)}, u32[]{:S(2)}, u32[]{:S(2)}) collective-permute-start(bf16[32,1024]{1,0:T(8,128)(2,1)S(1)} %collective-permute-done.2.refs_5_), channel_id=1, source_target_pairs={{0,1},{1,0},{2,3},{3,2},{4,5},{5,4},{6,7},{7,6},{8,9},{9,8},{10,11... | collective-permute-start | bytes 196616 | tf_op jit(solution)/shard_map/ppermute | solution.py:287
  12.4 1.4 %collective-permute-start.5 = (bf16[32,1024]{1,0:T(8,128)(2,1)S(1)}, bf16[32,1024]{1,0:T(8,128)(2,1)S(1)}, u32[]{:S(2)}, u32[]{:S(2)}) collective-permute-start(bf16[32,1024]{1,0:T(8,128)(2,1)S(1)} %collective-permute-done.4.refs_6_), channel_id=1, source_target_pairs={{0,1},{1,0},{2,3},{3,2},{4,5},{5,4},{6,7},{7,6},{8,9},{9,8},{10,11... | collective-permute-start | bytes 196616 | tf_op jit(solution)/shard_map/ppermute | solution.py:287
  26.4 1.6 %collective-permute-start.6 = (f32[2,32,1152]{2,1,0:T(8,128)S(1)}, f32[2,32,1152]{2,1,0:T(8,128)S(1)}, u32[]{:S(2)}, u32[]{:S(2)}) collective-permute-start(f32[2,32,1152]{2,1,0:T(8,128)S(1)} %bitcast.10), channel_id=1, source_target_pairs={{0,1},{1,0},{2,3},{3,2},{4,5},{5,4},{6,7},{7,6},{8,9},{9,8},{10,11... | collective-permute-start | bytes 884744 | tf_op jit(solution)/shard_map/ppermute | solution.py:287
  26.8 3.2 %collective-permute-start.10 = (f32[2,32,1152]{2,1,0:T(8,128)S(1)}, f32[2,32,1152]{2,1,0:T(8,128)S(1)}, u32[]{:S(2)}, u32[]{:S(2)}) collective-permute-start(f32[2,32,1152]{2,1,0:T(8,128)S(1)} %bitcast.9), channel_id=1, source_target_pairs={{0,1},{1,0},{2,3},{3,2},{4,5},{5,4},{6,7},{7,6},{8,9},{9,8},{10,11... | collective-permute-start | bytes 884744 | tf_op jit(solution)/shard_map/ppermute | solution.py:287
  28.4 4.6 %collective-permute-start.7 = (s16[2,16,1152]{2,1,0:T(8,128)(2,1)S(1)}, s16[2,16,1152]{2,1,0:T(8,128)(2,1)S(1)}, u32[]{:S(2)}, u32[]{:S(2)}) collective-permute-start(s16[2,16,1152]{2,1,0:T(8,128)(2,1)S(1)} %get-tuple-element.21), channel_id=1, source_target_pairs={{0,2},{1,3},{2,0},{3,1},{4,6},{5,7},{6,4},{7,5},{8,10},{9,11},{10,... | collective-permute-start | bytes 221192 | tf_op jit(solution)/shard_map/ppermute | solution.py:287
  30.4 5.8 %collective-permute-start.11 = (s16[2,16,1152]{2,1,0:T(8,128)(2,1)S(1)}, s16[2,16,1152]{2,1,0:T(8,128)(2,1)S(1)}, u32[]{:S(2)}, u32[]{:S(2)}) collective-permute-start(s16[2,16,1152]{2,1,0:T(8,128)(2,1)S(1)} %get-tuple-element.27), channel_id=1, source_target_pairs={{0,2},{1,3},{2,0},{3,1},{4,6},{5,7},{6,4},{7,5},{8,10},{9,11},{10,... | collective-permute-start | bytes 221192 | tf_op jit(solution)/shard_map/ppermute | solution.py:287
  33.4 5.9 %collective-permute-start.8 = (s16[16,1152]{1,0:T(8,128)(2,1)S(1)}, s16[16,1152]{1,0:T(8,128)(2,1)S(1)}, u32[]{:S(2)}, u32[]{:S(2)}) collective-permute-start(s16[16,1152]{1,0:T(8,128)(2,1)S(1)} %get-tuple-element.22), channel_id=1, source_target_pairs={{0,12},{4,8},{8,4},{12,0},{1,13},{5,9},{9,5},{13,1},{2,14},{6,10},... | collective-permute-start | bytes 110600 | tf_op jit(solution)/shard_map/ppermute | solution.py:287
  36.2 4.9 %collective-permute-start.9 = (s16[16,1152]{1,0:T(8,128)(2,1)S(1)}, s16[16,1152]{1,0:T(8,128)(2,1)S(1)}, u32[]{:S(2)}, u32[]{:S(2)}) collective-permute-start(s16[16,1152]{1,0:T(8,128)(2,1)S(1)} %get-tuple-element.23), channel_id=1, source_target_pairs={{0,8},{4,12},{8,0},{12,4},{1,9},{5,13},{9,1},{13,5},{2,10},{6,14},... | collective-permute-start | bytes 110600 | tf_op jit(solution)/shard_map/ppermute | solution.py:287
  36.6 4.5 %collective-permute-start.12 = (s16[16,1152]{1,0:T(8,128)(2,1)S(1)}, s16[16,1152]{1,0:T(8,128)(2,1)S(1)}, u32[]{:S(2)}, u32[]{:S(2)}) collective-permute-start(s16[16,1152]{1,0:T(8,128)(2,1)S(1)} %get-tuple-element.28), channel_id=1, source_target_pairs={{0,4},{4,0},{8,12},{12,8},{1,5},{5,1},{9,13},{13,9},{2,6},{6,2},{1... | collective-permute-start | bytes 110600 | tf_op jit(solution)/shard_map/ppermute | solution.py:287

commit v6 on v5

--- a/solution.py
+++ b/solution.py
@@ -44,9 +44,12 @@
             copy.start()
     k_pool[0] = k_first[...]
     v_pool[0] = v_first[...]
-    for h in range(heads):
-        rows = [q_ref[:, h * DH : (h + 1) * DH] for q_ref in q_refs[::-1]]
-        q_turned[h] = jnp.concatenate(rows, axis=0).T
+    def turn(h):
+        lanes = pl.ds(pl.multiple_of(h * DH, DH), DH)
+        q_turned[h] = jnp.concatenate([q_ref[:, lanes] for q_ref in q_refs[::-1]], axis=0).T
+
+    for h in range(1 if tiles == 1 else heads):
+        turn(h)
     stats[...] = jnp.zeros_like(stats)
     ones = jnp.ones((8, PAGE), jnp.bfloat16)
 
@@ -68,6 +71,8 @@
         start = pl.multiple_of(t * tile, tile)
         columns = pl.ds(start, tile)
         q_tile = q_turned[h, :, columns]
+        if tiles == 1:
+            turn(jnp.minimum(h + 1, heads - 1))
         scores, tops = [], []
         for i in range(0, pool, GROUP):
             block = k_pool[h, i : i + GROUP].reshape(GROUP * PAGE, DH)
@@ -88,8 +93,10 @@
             fresh = jnp.exp2((used[i] - best) * to_log2)
             total = total + fresh * page_out[DH : DH + 1]
             accum = accum + fresh * page_out[:DH]
-        out = (accum / total).T
+        out = accum / total
         stats[pl.ds(h, 1), columns] = best * to_log2 + jnp.log2(total)
+        stats[pl.ds(heads + h, 1), columns] = jnp.max(jnp.abs(out), axis=0, keepdims=True)
+        out = out.T
         lanes = pl.ds(pl.multiple_of(h * DH, DH), DH)
         for first, out_ref in zip(starts, out_refs):
             length = out_ref.shape[0]
@@ -171,24 +178,13 @@
     return jnp.where(x < 0, x - 0.5, x + 0.5).astype(jnp.int32)
 
 
-def encode(outs, logs, out_ref):
-    heads = len(outs)
-    where = (slice(None),) * (len(out_ref.shape) - 1)
-    powers = []
-    for h, out in enumerate(outs):
-        largest = jnp.max(jnp.abs(out), axis=-1, keepdims=True)
-        power = jnp.ceil(jnp.log2(jnp.maximum(largest, 2.0**-100)))
-        powers.append(power)
-        out_ref[where + (slice(h * DH, (h + 1) * DH),)] = rounded(
-            out * (jnp.exp2(-power) * 32767.0)
-        ).astype(jnp.int16)
+def write_stats(logs, powers, out_ref, heads):
     fixed = rounded(logs * 2.0**19)
     high = lax.shift_right_arithmetic(fixed, 16)
     low = lax.bitwise_and(fixed, 65535) - 32768
     pad = jnp.zeros(logs.shape[:-1] + (LANES - 3 * heads,), jnp.int32)
-    stat = jnp.concatenate(
-        [high[..., :heads], low[..., :heads]] + [p.astype(jnp.int32) for p in powers] + [pad], axis=-1
-    )
+    stat = jnp.concatenate([high, low, powers.astype(jnp.int32), pad], axis=-1)
+    where = (slice(None),) * (len(out_ref.shape) - 1)
     out_ref[where + (slice(heads * DH, heads * DH + LANES),)] = stat.astype(jnp.int16)
 
 
@@ -205,36 +201,64 @@
     return outs, logs
 
 
-def plain(heads, ref):
-    where = (slice(None),) * (len(ref.shape) - 1)
-    outs = [ref[where + (slice(h * DH, (h + 1) * DH),)] for h in range(heads)]
-    return outs, ref[where + (slice(heads * DH, heads * DH + heads),)]
-
-
 def merge_kernel(heads, last, mine_ref, theirs_ref, *out_refs):
-    mine, mine_logs = plain(heads, mine_ref)
-    theirs, their_logs = (decode if theirs_ref.dtype == jnp.int16 else plain)(heads, theirs_ref)
+    def lanes(h):
+        return slice(h * DH, (h + 1) * DH)
+
+    first_stat = heads * DH
+    mine_logs = mine_ref[:, :, first_stat : first_stat + heads]
+    mine_bound = mine_ref[:, :, first_stat + heads : first_stat + 2 * heads]
+    coded = theirs_ref.dtype == jnp.int16
+    if coded:
+        stat = theirs_ref[:, :, first_stat:].astype(jnp.int32)
+        fixed = lax.shift_left(stat[..., :heads], 16) + (stat[..., heads : 2 * heads] + 32768)
+        their_logs = fixed.astype(jnp.float32) * 2.0**-19
+        their_bound = jnp.exp2(stat[..., 2 * heads : 3 * heads].astype(jnp.float32))
+    else:
+        their_logs = theirs_ref[:, :, first_stat : first_stat + heads]
+        their_bound = theirs_ref[:, :, first_stat + heads : first_stat + 2 * heads]
     top = jnp.maximum(mine_logs, their_logs)
     first, second = jnp.exp2(mine_logs - top), jnp.exp2(their_logs - top)
     both = first + second
     first, second, logs = first / both, second / both, top + jnp.log2(both)
-    outs = [
-        mine[h] * first[..., h : h + 1] + theirs[h] * second[..., h : h + 1] for h in range(heads)
-    ]
+    bound = first * mine_bound + second * their_bound
+    powers = jnp.ceil(jnp.log2(jnp.maximum(bound, 2.0**-100)) + 0.001)
+    scale = jnp.exp2(-powers) * 32767.0
+    if coded:
+        second = second * their_bound * (1.0 / 32767.0)
+    first_coded, second_coded = first * scale, second * scale
+
+    def joined(h, a, b, rows):
+        theirs = theirs_ref[:, rows, lanes(h)]
+        if coded:
+            theirs = theirs.astype(jnp.int32).astype(jnp.float32)
+        return mine_ref[:, rows, lanes(h)] * a[:, rows, h : h + 1] + theirs * b[:, rows, h : h + 1]
+
     if last:
+        everything = slice(0, mine_ref.shape[1])
+        for h in range(heads):
+            out = rounded(joined(h, first_coded, second_coded, everything)).astype(jnp.int16)
+            if len(out_refs[0].shape) == 3:
+                out_refs[0][:, :, lanes(h)] = out
+            else:
+                for block, out_ref in enumerate(out_refs):
+                    out_ref[:, lanes(h)] = out[block]
         if len(out_refs[0].shape) == 3:
-            encode(outs, logs, out_refs[0])
+            write_stats(logs, powers, out_refs[0], heads)
         else:
             for block, out_ref in enumerate(out_refs):
-                encode([out[block] for out in outs], logs[block], out_ref)
+                write_stats(logs[block], powers[block], out_ref, heads)
     else:
         keep_ref, send_ref = out_refs
         half = keep_ref.shape[1]
+        low, high = slice(0, half), slice(half, 2 * half)
         for h in range(heads):
-            keep_ref[:, :, h * DH : (h + 1) * DH] = outs[h][:, :half]
-        pad = jnp.zeros(logs.shape[:-1] + (LANES - heads,), jnp.float32)
-        keep_ref[:, :, heads * DH :] = jnp.concatenate([logs, pad], axis=-1)[:, :half]
-        encode([out[:, half:] for out in outs], logs[:, half:], send_ref)
+            keep_ref[:, :, lanes(h)] = joined(h, first, second, low)
+            out = rounded(joined(h, first_coded, second_coded, high))
+            send_ref[:, :, lanes(h)] = out.astype(jnp.int16)
+        pad = jnp.zeros(logs.shape[:-1] + (LANES - 2 * heads,), jnp.float32)
+        keep_ref[:, :, first_stat:] = jnp.concatenate([logs, bound, pad], axis=-1)[:, low]
+        write_stats(logs[:, high], powers[:, high], send_ref, heads)
 
 
 def merge(mine, theirs, heads, out_shapes, last):

time: 42.2 us -> 42 us (level)
  no operation moved by 1% of the time
where the time goes in v6:
time: 42 us; the launch traced here: 41.7 us
  Pallas kernels  16.1 us (38%)
  starting transfers between devices  13.6 us (32%)
  waiting for transfers between devices  8.75 us (21%)
  between operations  1.43 us (3%)
  local copies, waits for them, and re-layouts  1.02 us (2%)
  other arithmetic  0.81 us (2%)
    ppermute x13, starting transfers between devices, across(): return lax.ppermute(value, axis, [(i, i ^ bit) for i in range(size)])  13.6 us
    pallas_call x1, Pallas kernels, attend(): pl.pallas_call(functools.partial(attend_kernel, len(q_parts), starts), in...  12.4 us
    ppermute x13, waiting for transfers between devices, across(): return lax.ppermute(value, axis, [(i, i ^ bit) for i in range(size)])  8.75 us
    pallas_call x1, Pallas kernels, first_head(): pl.pallas_call(first_kernel, in_specs=[pl.BlockSpec(memory_space=pl.ANY)]...  1.62 us
    pallas_call x4, Pallas kernels, merge(): pl.pallas_call(functools.partial(merge_kernel, heads, last), out_shape=ou...  1.11 us
    dynamic_slice x1, local copies, waits for them, and re-layouts, pick(): lax.dynamic_slice(queries, ((cache_at ^ name) * share, at), (share, width))  0.95 us
    pallas_call x1, Pallas kernels, place(): pl.pallas_call(functools.partial(place_kernel, heads, axis, names), out_s...  0.94 us
  transfers between devices with their start and end apart: 13, of which 7 were waited for; matrix products, arithmetic and copies ran while one was open for 2% of the time, Pallas kernels for 7%

profile of v6, /device:TPU:0, one launch (start us, length us, event | category | flops | bytes accessed | tf_op | source)
XLA Modules:
  0.0 41.7 jit_solution(14984878799660112050)
XLA Ops:
  0.7 0.9 %fusion.2 = (bf16[16,1024]{1,0:T(8,128)(2,1)S(1)}, bf16[16,1024]{1,0:T(8,128)(2,1)S(1)}, bf16[16,1024]{1,0:T(8,128)(2,1)S(1)}, bf16[16,1024]{1,0:T(8,128)(2,1)S(...) fusion(bf16[64,4096]{1,0:T(8,128)(2,1)} %param.5, ...), kind=kLoop, calls=%fused_computation.10 | loop fusion | bytes 655392 | tf_op jit(solution)/shard_map/dynamic_slice | solution.py:339
  1.6 5.1 %collective-permute-start = (bf16[32,1024]{1,0:T(8,128)(2,1)S(1)}, bf16[32,1024]{1,0:T(8,128)(2,1)S(1)}, u32[]{:S(2)}, u32[]{:S(2)}) collective-permute-start(bf16[32,1024]{1,0:T(8,128)(2,1)S(1)} %pad_maximum_fusion), channel_id=1, source_target_pairs={{0,12},{4,8},{8,4},{12,0},{1,13},{5,9},{9,5},{13,1},{2,14},{6,10},... | collective-permute-start | bytes 196616 | tf_op jit(solution)/shard_map/ppermute | solution.py:311
  6.8 0.0 collective-permute-start.2
  6.8 0.6 %collective-permute-start.4 = (bf16[32,1024]{1,0:T(8,128)(2,1)S(1)}, bf16[32,1024]{1,0:T(8,128)(2,1)S(1)}, u32[]{:S(2)}, u32[]{:S(2)}) collective-permute-start(bf16[32,1024]{1,0:T(8,128)(2,1)S(1)} %pad_maximum_fusion.2), channel_id=1, source_target_pairs={{0,4},{4,0},{8,12},{12,8},{1,5},{5,1},{9,13},{13,9},{2,6},{6,2},{1... | collective-permute-start | bytes 196616 | tf_op jit(solution)/shard_map/ppermute | solution.py:311
  8.1 0.8 %fusion.1 = pred[32]{0:T(512)(128)(4,1)S(1)} fusion(s32[32]{0:T(128)} %bitcast.11, pred[32]{0:T(512)(128)(4,1)S(1)} %iota_compare_fusion.1), kind=kLoop, calls=%fused_computation.7 | loop fusion | flops 3040 | bytes 192 | tf_op jit(solution)/shard_map/reduce_or | solution.py:317
  8.9 1.6 %first_head.1 = (bf16[32,128,128]{2,1,0:T(8,128)(2,1)S(1)}, bf16[32,128,128]{2,1,0:T(8,128)(2,1)S(1)}) custom-call(bf16[32,128,1024]{2,1,0:T(8,128)(2,1)} %refs_8_.1, bf16[32,128,1024]{2,1,0:T(8,128)(2,1)} %refs_9_.1), custom_call_target="tpu_custom_call" | custom-call | tf_op jit(solution)/shard_map/first_head/pallas_call | solution.py:138
  10.5 0.0 collective-permute-done.refs_4_
  10.5 0.1 collective-permute-start.1
  10.6 1.8 %collective-permute-done.2.refs_5_ = bf16[32,1024]{1,0:T(8,128)(2,1)S(1)} collective-permute-done((bf16[32,1024]{1,0:T(8,128)(2,1)S(1)}, bf16[32,1024]{1,0:T(8,128)(2,1)S(1)}, u32[]{:S(2)}, u32[]{:S(2)}) %collective-permute-start.2) | collective-permute-done | bytes 65568 | tf_op jit(solution)/shard_map/ppermute | solution.py:311
  12.4 0.0 collective-permute-start.3
  12.4 0.0 collective-permute-done.4.refs_6_
  12.4 0.5 %collective-permute-start.5 = (bf16[32,1024]{1,0:T(8,128)(2,1)S(1)}, bf16[32,1024]{1,0:T(8,128)(2,1)S(1)}, u32[]{:S(2)}, u32[]{:S(2)}) collective-permute-start(bf16[32,1024]{1,0:T(8,128)(2,1)S(1)} %collective-permute-done.4.refs_6_), channel_id=1, source_target_pairs={{0,1},{1,0},{2,3},{3,2},{4,5},{5,4},{6,7},{7,6},{8,9},{9,8},{10,11... | collective-permute-start | bytes 196616 | tf_op jit(solution)/shard_map/ppermute | solution.py:311
  12.9 0.0 collective-permute-done.1.refs_0_
  12.9 0.7 %collective-permute-done.3.refs_1_ = bf16[32,1024]{1,0:T(8,128)(2,1)S(1)} collective-permute-done((bf16[32,1024]{1,0:T(8,128)(2,1)S(1)}, bf16[32,1024]{1,0:T(8,128)(2,1)S(1)}, u32[]{:S(2)}, u32[]{:S(2)}) %collective-permute-start.3) | collective-permute-done | bytes 65568 | tf_op jit(solution)/shard_map/ppermute | solution.py:311
  13.6 0.2 collective-permute-done.5.refs_2_
  13.8 0.1 broadcast_in_dim.18.limits_ref
  13.8 12.4 %attend.1 = (f32[64,1152]{1,0:T(8,128)S(1)}, f32[64,1152]{1,0:T(8,128)S(1)}, f32[64,1152]{1,0:T(8,128)S(1)}, f32[64,1152]{1,0:T(8,128)S(1)}) custom-call(f32[32,256]{1,0:T(8,128)S(1)} %broadcast_in_dim.18.limits_ref, bf16[32,1024]{1,0:T(8,128)(2,1)S(1)} %collective-permute-done.1.refs_0_, bf16[32,1024]{1,0:T(8,128)(2,1)S(1)} %collective-permute-done.3.refs_1_, ...), custom_call_target="tpu_custom_call" | custom-call | tf_op jit(solution)/shard_map/attend/pallas_call | solution.py:159
  26.3 0.4 %collective-permute-start.6 = (f32[2,32,1152]{2,1,0:T(8,128)S(1)}, f32[2,32,1152]{2,1,0:T(8,128)S(1)}, u32[]{:S(2)}, u32[]{:S(2)}) collective-permute-start(f32[2,32,1152]{2,1,0:T(8,128)S(1)} %bitcast.10), channel_id=1, source_target_pairs={{0,1},{1,0},{2,3},{3,2},{4,5},{5,4},{6,7},{7,6},{8,9},{9,8},{10,11... | collective-permute-start | bytes 884744 | tf_op jit(solution)/shard_map/ppermute | solution.py:311
  26.7 0.2 collective-permute-start.10
  26.9 1.1 %collective-permute-done.6.theirs_ref = f32[2,32,1152]{2,1,0:T(8,128)S(1)} collective-permute-done((f32[2,32,1152]{2,1,0:T(8,128)S(1)}, f32[2,32,1152]{2,1,0:T(8,128)S(1)}, u32[]{:S(2)}, u32[]{:S(2)}) %collective-permute-start.6) | collective-permute-done | bytes 294944 | tf_op jit(solution)/shard_map/ppermute | solution.py:311
  27.9 0.3 merge.4
  28.2 1.6 %collective-permute-start.7 = (s16[2,16,1152]{2,1,0:T(8,128)(2,1)S(1)}, s16[2,16,1152]{2,1,0:T(8,128)(2,1)S(1)}, u32[]{:S(2)}, u32[]{:S(2)}) collective-permute-start(s16[2,16,1152]{2,1,0:T(8,128)(2,1)S(1)} %get-tuple-element.21), channel_id=1, source_target_pairs={{0,2},{1,3},{2,0},{3,1},{4,6},{5,7},{6,4},{7,5},{8,10},{9,11},{10,... | collective-permute-start | bytes 221192 | tf_op jit(solution)/shard_map/ppermute | solution.py:311
  29.9 0.0 collective-permute-done.10.theirs_ref
  29.9 0.3 merge.6
  30.2 0.5 %collective-permute-start.11 = (s16[2,16,1152]{2,1,0:T(8,128)(2,1)S(1)}, s16[2,16,1152]{2,1,0:T(8,128)(2,1)S(1)}, u32[]{:S(2)}, u32[]{:S(2)}) collective-permute-start(s16[2,16,1152]{2,1,0:T(8,128)(2,1)S(1)} %get-tuple-element.27), channel_id=1, source_target_pairs={{0,2},{1,3},{2,0},{3,1},{4,6},{5,7},{6,4},{7,5},{8,10},{9,11},{10,... | collective-permute-start | bytes 221192 | tf_op jit(solution)/shard_map/ppermute | solution.py:311
  30.7 2.1 %collective-permute-done.7.theirs_ref = s16[2,16,1152]{2,1,0:T(8,128)(2,1)S(1)} collective-permute-done((s16[2,16,1152]{2,1,0:T(8,128)(2,1)S(1)}, s16[2,16,1152]{2,1,0:T(8,128)(2,1)S(1)}, u32[]{:S(2)}, u32[]{:S(2)}) %collective-permute-start.7) | collective-permute-done | bytes 73760 | tf_op jit(solution)/shard_map/ppermute | solution.py:311
  32.8 0.3 merge.5
  33.1 2.8 %collective-permute-start.8 = (s16[16,1152]{1,0:T(8,128)(2,1)S(1)}, s16[16,1152]{1,0:T(8,128)(2,1)S(1)}, u32[]{:S(2)}, u32[]{:S(2)}) collective-permute-start(s16[16,1152]{1,0:T(8,128)(2,1)S(1)} %get-tuple-element.22), channel_id=1, source_target_pairs={{0,12},{4,8},{8,4},{12,0},{1,13},{5,9},{9,5},{13,1},{2,14},{6,10},... | collective-permute-start | bytes 110600 | tf_op jit(solution)/shard_map/ppermute | solution.py:311
  35.9 0.0 collective-permute-start.9
  35.9 0.0 collective-permute-done.11.theirs_ref
  35.9 0.3 merge.7
  36.2 1.7 %collective-permute-start.12 = (s16[16,1152]{1,0:T(8,128)(2,1)S(1)}, s16[16,1152]{1,0:T(8,128)(2,1)S(1)}, u32[]{:S(2)}, u32[]{:S(2)}) collective-permute-start(s16[16,1152]{1,0:T(8,128)(2,1)S(1)} %get-tuple-element.28), channel_id=1, source_target_pairs={{0,4},{4,0},{8,12},{12,8},{1,5},{5,1},{9,13},{13,9},{2,6},{6,2},{1... | collective-permute-start | bytes 110600 | tf_op jit(solution)/shard_map/ppermute | solution.py:311
  37.9 1.1 %collective-permute-done.8.refs_0_ = s16[16,1152]{1,0:T(8,128)(2,1)S(1)} collective-permute-done((s16[16,1152]{1,0:T(8,128)(2,1)S(1)}, s16[16,1152]{1,0:T(8,128)(2,1)S(1)}, u32[]{:S(2)}, u32[]{:S(2)}) %collective-permute-start.8) | collective-permute-done | bytes 36896 | tf_op jit(solution)/shard_map/ppermute | solution.py:311
  39.0 1.8 %collective-permute-done.9.refs_1_ = s16[16,1152]{1,0:T(8,128)(2,1)S(1)} collective-permute-done((s16[16,1152]{1,0:T(8,128)(2,1)S(1)}, s16[16,1152]{1,0:T(8,128)(2,1)S(1)}, u32[]{:S(2)}, u32[]{:S(2)}) %collective-permute-start.9) | collective-permute-done | bytes 36896 | tf_op jit(solution)/shard_map/ppermute | solution.py:311
  40.8 0.0 collective-permute-done.12.refs_2_
  40.8 0.9 %place.1 = (f32[16,4096]{1,0:T(8,128)}, f32[16,32]{1,0:T(8,128)}) custom-call(s16[16,1152]{1,0:T(8,128)(2,1)S(1)} %collective-permute-done.8.refs_0_, s16[16,1152]{1,0:T(8,128)(2,1)S(1)} %collective-permute-done.9.refs_1_, s16[16,1152]{1,0:T(8,128)(2,1)S(1)} %collective-permute-done.12.refs_2_, s16[16,1152]{1,0:T(8,128)(2,1)S(1)} %get-tuple-element.29.refs_3_), custom_call_target="tpu_custom_call" | custom-call | tf_op jit(solution)/shard_map/place/pallas_call | solution.py:299
  (6 shorter events, 0.0 us)
Async XLA Ops:
  1.6 8.9 %collective-permute-start = (bf16[32,1024]{1,0:T(8,128)(2,1)S(1)}, bf16[32,1024]{1,0:T(8,128)(2,1)S(1)}, u32[]{:S(2)}, u32[]{:S(2)}) collective-permute-start(bf16[32,1024]{1,0:T(8,128)(2,1)S(1)} %pad_maximum_fusion), channel_id=1, source_target_pairs={{0,12},{4,8},{8,4},{12,0},{1,13},{5,9},{9,5},{13,1},{2,14},{6,10},... | collective-permute-start | bytes 196616 | tf_op jit(solution)/shard_map/ppermute | solution.py:311
  6.8 5.6 %collective-permute-start.2 = (bf16[32,1024]{1,0:T(8,128)(2,1)S(1)}, bf16[32,1024]{1,0:T(8,128)(2,1)S(1)}, u32[]{:S(2)}, u32[]{:S(2)}) collective-permute-start(bf16[32,1024]{1,0:T(8,128)(2,1)S(1)} %pad_maximum_fusion.1), channel_id=1, source_target_pairs={{0,8},{4,12},{8,0},{12,4},{1,9},{5,13},{9,1},{13,5},{2,10},{6,14},... | collective-permute-start | bytes 196616 | tf_op jit(solution)/shard_map/ppermute | solution.py:311
  6.8 5.6 %collective-permute-start.4 = (bf16[32,1024]{1,0:T(8,128)(2,1)S(1)}, bf16[32,1024]{1,0:T(8,128)(2,1)S(1)}, u32[]{:S(2)}, u32[]{:S(2)}) collective-permute-start(bf16[32,1024]{1,0:T(8,128)(2,1)S(1)} %pad_maximum_fusion.2), channel_id=1, source_target_pairs={{0,4},{4,0},{8,12},{12,8},{1,5},{5,1},{9,13},{13,9},{2,6},{6,2},{1... | collective-permute-start | bytes 196616 | tf_op jit(solution)/shard_map/ppermute | solution.py:311
  10.5 2.4 %collective-permute-start.1 = (bf16[32,1024]{1,0:T(8,128)(2,1)S(1)}, bf16[32,1024]{1,0:T(8,128)(2,1)S(1)}, u32[]{:S(2)}, u32[]{:S(2)}) collective-permute-start(bf16[32,1024]{1,0:T(8,128)(2,1)S(1)} %collective-permute-done.refs_4_), channel_id=1, source_target_pairs={{0,1},{1,0},{2,3},{3,2},{4,5},{5,4},{6,7},{7,6},{8,9},{9,8},{10,11... | collective-permute-start | bytes 196616 | tf_op jit(solution)/shard_map/ppermute | solution.py:311
  12.4 1.3 %collective-permute-start.3 = (bf16[32,1024]{1,0:T(8,128)(2,1)S(1)}, bf16[32,1024]{1,0:T(8,128)(2,1)S(1)}, u32[]{:S(2)}, u32[]{:S(2)}) collective-permute-start(bf16[32,1024]{1,0:T(8,128)(2,1)S(1)} %collective-permute-done.2.refs_5_), channel_id=1, source_target_pairs={{0,1},{1,0},{2,3},{3,2},{4,5},{5,4},{6,7},{7,6},{8,9},{9,8},{10,11... | collective-permute-start | bytes 196616 | tf_op jit(solution)/shard_map/ppermute | solution.py:311
  12.4 1.4 %collective-permute-start.5 = (bf16[32,1024]{1,0:T(8,128)(2,1)S(1)}, bf16[32,1024]{1,0:T(8,128)(2,1)S(1)}, u32[]{:S(2)}, u32[]{:S(2)}) collective-permute-start(bf16[32,1024]{1,0:T(8,128)(2,1)S(1)} %collective-permute-done.4.refs_6_), channel_id=1, source_target_pairs={{0,1},{1,0},{2,3},{3,2},{4,5},{5,4},{6,7},{7,6},{8,9},{9,8},{10,11... | collective-permute-start | bytes 196616 | tf_op jit(solution)/shard_map/ppermute | solution.py:311
  26.3 1.6 %collective-permute-start.6 = (f32[2,32,1152]{2,1,0:T(8,128)S(1)}, f32[2,32,1152]{2,1,0:T(8,128)S(1)}, u32[]{:S(2)}, u32[]{:S(2)}) collective-permute-start(f32[2,32,1152]{2,1,0:T(8,128)S(1)} %bitcast.10), channel_id=1, source_target_pairs={{0,1},{1,0},{2,3},{3,2},{4,5},{5,4},{6,7},{7,6},{8,9},{9,8},{10,11... | collective-permute-start | bytes 884744 | tf_op jit(solution)/shard_map/ppermute | solution.py:311
  26.7 3.2 %collective-permute-start.10 = (f32[2,32,1152]{2,1,0:T(8,128)S(1)}, f32[2,32,1152]{2,1,0:T(8,128)S(1)}, u32[]{:S(2)}, u32[]{:S(2)}) collective-permute-start(f32[2,32,1152]{2,1,0:T(8,128)S(1)} %bitcast.9), channel_id=1, source_target_pairs={{0,1},{1,0},{2,3},{3,2},{4,5},{5,4},{6,7},{7,6},{8,9},{9,8},{10,11... | collective-permute-start | bytes 884744 | tf_op jit(solution)/shard_map/ppermute | solution.py:311
  28.2 4.6 %collective-permute-start.7 = (s16[2,16,1152]{2,1,0:T(8,128)(2,1)S(1)}, s16[2,16,1152]{2,1,0:T(8,128)(2,1)S(1)}, u32[]{:S(2)}, u32[]{:S(2)}) collective-permute-start(s16[2,16,1152]{2,1,0:T(8,128)(2,1)S(1)} %get-tuple-element.21), channel_id=1, source_target_pairs={{0,2},{1,3},{2,0},{3,1},{4,6},{5,7},{6,4},{7,5},{8,10},{9,11},{10,... | collective-permute-start | bytes 221192 | tf_op jit(solution)/shard_map/ppermute | solution.py:311
  30.2 5.8 %collective-permute-start.11 = (s16[2,16,1152]{2,1,0:T(8,128)(2,1)S(1)}, s16[2,16,1152]{2,1,0:T(8,128)(2,1)S(1)}, u32[]{:S(2)}, u32[]{:S(2)}) collective-permute-start(s16[2,16,1152]{2,1,0:T(8,128)(2,1)S(1)} %get-tuple-element.27), channel_id=1, source_target_pairs={{0,2},{1,3},{2,0},{3,1},{4,6},{5,7},{6,4},{7,5},{8,10},{9,11},{10,... | collective-permute-start | bytes 221192 | tf_op jit(solution)/shard_map/ppermute | solution.py:311
  33.1 5.8 %collective-permute-start.8 = (s16[16,1152]{1,0:T(8,128)(2,1)S(1)}, s16[16,1152]{1,0:T(8,128)(2,1)S(1)}, u32[]{:S(2)}, u32[]{:S(2)}) collective-permute-start(s16[16,1152]{1,0:T(8,128)(2,1)S(1)} %get-tuple-element.22), channel_id=1, source_target_pairs={{0,12},{4,8},{8,4},{12,0},{1,13},{5,9},{9,5},{13,1},{2,14},{6,10},... | collective-permute-start | bytes 110600 | tf_op jit(solution)/shard_map/ppermute | solution.py:311
  35.9 4.9 %collective-permute-start.9 = (s16[16,1152]{1,0:T(8,128)(2,1)S(1)}, s16[16,1152]{1,0:T(8,128)(2,1)S(1)}, u32[]{:S(2)}, u32[]{:S(2)}) collective-permute-start(s16[16,1152]{1,0:T(8,128)(2,1)S(1)} %get-tuple-element.23), channel_id=1, source_target_pairs={{0,8},{4,12},{8,0},{12,4},{1,9},{5,13},{9,1},{13,5},{2,10},{6,14},... | collective-permute-start | bytes 110600 | tf_op jit(solution)/shard_map/ppermute | solution.py:311
  36.2 4.6 %collective-permute-start.12 = (s16[16,1152]{1,0:T(8,128)(2,1)S(1)}, s16[16,1152]{1,0:T(8,128)(2,1)S(1)}, u32[]{:S(2)}, u32[]{:S(2)}) collective-permute-start(s16[16,1152]{1,0:T(8,128)(2,1)S(1)} %get-tuple-element.28), channel_id=1, source_target_pairs={{0,4},{4,0},{8,12},{12,8},{1,5},{5,1},{9,13},{13,9},{2,6},{6,2},{1... | collective-permute-start | bytes 110600 | tf_op jit(solution)/shard_map/ppermute | solution.py:311

commit v7 on v6

--- a/solution.py
+++ b/solution.py
@@ -93,7 +93,7 @@
             fresh = jnp.exp2((used[i] - best) * to_log2)
             total = total + fresh * page_out[DH : DH + 1]
             accum = accum + fresh * page_out[:DH]
-        out = accum / total
+        out = accum * (1.0 / total)
         stats[pl.ds(h, 1), columns] = best * to_log2 + jnp.log2(total)
         stats[pl.ds(heads + h, 1), columns] = jnp.max(jnp.abs(out), axis=0, keepdims=True)
         out = out.T
@@ -229,9 +229,10 @@
     first_coded, second_coded = first * scale, second * scale
 
     def joined(h, a, b, rows):
-        theirs = theirs_ref[:, rows, lanes(h)]
         if coded:
-            theirs = theirs.astype(jnp.int32).astype(jnp.float32)
+            theirs = theirs_ref[:, :, lanes(h)].astype(jnp.int32).astype(jnp.float32)[:, rows]
+        else:
+            theirs = theirs_ref[:, rows, lanes(h)]
         return mine_ref[:, rows, lanes(h)] * a[:, rows, h : h + 1] + theirs * b[:, rows, h : h + 1]
 
     if last:

time: 42 us -> 41.9 us (level)
  no operation moved by 1% of the time
where the time goes in v7:
time: 41.9 us; the launch traced here: 41.7 us
  Pallas kernels  16.1 us (38%)
  starting transfers between devices  13.6 us (32%)
  waiting for transfers between devices  8.74 us (21%)
  between operations  1.43 us (3%)
  local copies, waits for them, and re-layouts  1.02 us (2%)
  other arithmetic  0.81 us (2%)
    ppermute x13, starting transfers between devices, across(): return lax.ppermute(value, axis, [(i, i ^ bit) for i in range(size)])  13.6 us
    pallas_call x1, Pallas kernels, attend(): pl.pallas_call(functools.partial(attend_kernel, len(q_parts), starts), in...  12.4 us
    ppermute x13, waiting for transfers between devices, across(): return lax.ppermute(value, axis, [(i, i ^ bit) for i in range(size)])  8.74 us
    pallas_call x1, Pallas kernels, first_head(): pl.pallas_call(first_kernel, in_specs=[pl.BlockSpec(memory_space=pl.ANY)]...  1.62 us
    pallas_call x4, Pallas kernels, merge(): pl.pallas_call(functools.partial(merge_kernel, heads, last), out_shape=ou...  1.11 us
    dynamic_slice x1, local copies, waits for them, and re-layouts, pick(): lax.dynamic_slice(queries, ((cache_at ^ name) * share, at), (share, width))  0.95 us
    pallas_call x1, Pallas kernels, place(): pl.pallas_call(functools.partial(place_kernel, heads, axis, names), out_s...  0.94 us
  transfers between devices with their start and end apart: 13, of which 7 were waited for; matrix products, arithmetic and copies ran while one was open for 2% of the time, Pallas kernels for 7%

profile of v7, /device:TPU:0, one launch (start us, length us, event | category | flops | bytes accessed | tf_op | source)
XLA Modules:
  0.0 41.7 jit_solution(7780165006641072475)
XLA Ops:
  0.7 0.9 %fusion.2 = (bf16[16,1024]{1,0:T(8,128)(2,1)S(1)}, bf16[16,1024]{1,0:T(8,128)(2,1)S(1)}, bf16[16,1024]{1,0:T(8,128)(2,1)S(1)}, bf16[16,1024]{1,0:T(8,128)(2,1)S(...) fusion(bf16[64,4096]{1,0:T(8,128)(2,1)} %param.5, ...), kind=kLoop, calls=%fused_computation.10 | loop fusion | bytes 655392 | tf_op jit(solution)/shard_map/dynamic_slice | solution.py:340
  1.6 5.1 %collective-permute-start = (bf16[32,1024]{1,0:T(8,128)(2,1)S(1)}, bf16[32,1024]{1,0:T(8,128)(2,1)S(1)}, u32[]{:S(2)}, u32[]{:S(2)}) collective-permute-start(bf16[32,1024]{1,0:T(8,128)(2,1)S(1)} %pad_maximum_fusion), channel_id=1, source_target_pairs={{0,12},{4,8},{8,4},{12,0},{1,13},{5,9},{9,5},{13,1},{2,14},{6,10},... | collective-permute-start | bytes 196616 | tf_op jit(solution)/shard_map/ppermute | solution.py:312
  6.8 0.0 collective-permute-start.2
  6.8 0.6 %collective-permute-start.4 = (bf16[32,1024]{1,0:T(8,128)(2,1)S(1)}, bf16[32,1024]{1,0:T(8,128)(2,1)S(1)}, u32[]{:S(2)}, u32[]{:S(2)}) collective-permute-start(bf16[32,1024]{1,0:T(8,128)(2,1)S(1)} %pad_maximum_fusion.2), channel_id=1, source_target_pairs={{0,4},{4,0},{8,12},{12,8},{1,5},{5,1},{9,13},{13,9},{2,6},{6,2},{1... | collective-permute-start | bytes 196616 | tf_op jit(solution)/shard_map/ppermute | solution.py:312
  8.1 0.8 %fusion.1 = pred[32]{0:T(512)(128)(4,1)S(1)} fusion(s32[32]{0:T(128)} %bitcast.11, pred[32]{0:T(512)(128)(4,1)S(1)} %iota_compare_fusion.1), kind=kLoop, calls=%fused_computation.7 | loop fusion | flops 3040 | bytes 192 | tf_op jit(solution)/shard_map/reduce_or | solution.py:318
  8.9 1.6 %first_head.1 = (bf16[32,128,128]{2,1,0:T(8,128)(2,1)S(1)}, bf16[32,128,128]{2,1,0:T(8,128)(2,1)S(1)}) custom-call(bf16[32,128,1024]{2,1,0:T(8,128)(2,1)} %refs_8_.1, bf16[32,128,1024]{2,1,0:T(8,128)(2,1)} %refs_9_.1), custom_call_target="tpu_custom_call" | custom-call | tf_op jit(solution)/shard_map/first_head/pallas_call | solution.py:138
  10.5 0.0 collective-permute-done.refs_4_
  10.5 0.1 collective-permute-start.1
  10.6 1.8 %collective-permute-done.2.refs_5_ = bf16[32,1024]{1,0:T(8,128)(2,1)S(1)} collective-permute-done((bf16[32,1024]{1,0:T(8,128)(2,1)S(1)}, bf16[32,1024]{1,0:T(8,128)(2,1)S(1)}, u32[]{:S(2)}, u32[]{:S(2)}) %collective-permute-start.2) | collective-permute-done | bytes 65568 | tf_op jit(solution)/shard_map/ppermute | solution.py:312
  12.4 0.0 collective-permute-start.3
  12.4 0.0 collective-permute-done.4.refs_6_
  12.4 0.5 %collective-permute-start.5 = (bf16[32,1024]{1,0:T(8,128)(2,1)S(1)}, bf16[32,1024]{1,0:T(8,128)(2,1)S(1)}, u32[]{:S(2)}, u32[]{:S(2)}) collective-permute-start(bf16[32,1024]{1,0:T(8,128)(2,1)S(1)} %collective-permute-done.4.refs_6_), channel_id=1, source_target_pairs={{0,1},{1,0},{2,3},{3,2},{4,5},{5,4},{6,7},{7,6},{8,9},{9,8},{10,11... | collective-permute-start | bytes 196616 | tf_op jit(solution)/shard_map/ppermute | solution.py:312
  12.9 0.0 collective-permute-done.1.refs_0_
  12.9 0.7 %collective-permute-done.3.refs_1_ = bf16[32,1024]{1,0:T(8,128)(2,1)S(1)} collective-permute-done((bf16[32,1024]{1,0:T(8,128)(2,1)S(1)}, bf16[32,1024]{1,0:T(8,128)(2,1)S(1)}, u32[]{:S(2)}, u32[]{:S(2)}) %collective-permute-start.3) | collective-permute-done | bytes 65568 | tf_op jit(solution)/shard_map/ppermute | solution.py:312
  13.6 0.2 collective-permute-done.5.refs_2_
  13.8 0.1 broadcast_in_dim.18.limits_ref
  13.8 12.4 %attend.1 = (f32[64,1152]{1,0:T(8,128)S(1)}, f32[64,1152]{1,0:T(8,128)S(1)}, f32[64,1152]{1,0:T(8,128)S(1)}, f32[64,1152]{1,0:T(8,128)S(1)}) custom-call(f32[32,256]{1,0:T(8,128)S(1)} %broadcast_in_dim.18.limits_ref, bf16[32,1024]{1,0:T(8,128)(2,1)S(1)} %collective-permute-done.1.refs_0_, bf16[32,1024]{1,0:T(8,128)(2,1)S(1)} %collective-permute-done.3.refs_1_, ...), custom_call_target="tpu_custom_call" | custom-call | tf_op jit(solution)/shard_map/attend/pallas_call | solution.py:159
  26.3 0.4 %collective-permute-start.6 = (f32[2,32,1152]{2,1,0:T(8,128)S(1)}, f32[2,32,1152]{2,1,0:T(8,128)S(1)}, u32[]{:S(2)}, u32[]{:S(2)}) collective-permute-start(f32[2,32,1152]{2,1,0:T(8,128)S(1)} %bitcast.10), channel_id=1, source_target_pairs={{0,1},{1,0},{2,3},{3,2},{4,5},{5,4},{6,7},{7,6},{8,9},{9,8},{10,11... | collective-permute-start | bytes 884744 | tf_op jit(solution)/shard_map/ppermute | solution.py:312
  26.7 0.2 collective-permute-start.10
  26.9 1.1 %collective-permute-done.6.theirs_ref = f32[2,32,1152]{2,1,0:T(8,128)S(1)} collective-permute-done((f32[2,32,1152]{2,1,0:T(8,128)S(1)}, f32[2,32,1152]{2,1,0:T(8,128)S(1)}, u32[]{:S(2)}, u32[]{:S(2)}) %collective-permute-start.6) | collective-permute-done | bytes 294944 | tf_op jit(solution)/shard_map/ppermute | solution.py:312
  27.9 0.3 merge.4
  28.2 1.6 %collective-permute-start.7 = (s16[2,16,1152]{2,1,0:T(8,128)(2,1)S(1)}, s16[2,16,1152]{2,1,0:T(8,128)(2,1)S(1)}, u32[]{:S(2)}, u32[]{:S(2)}) collective-permute-start(s16[2,16,1152]{2,1,0:T(8,128)(2,1)S(1)} %get-tuple-element.21), channel_id=1, source_target_pairs={{0,2},{1,3},{2,0},{3,1},{4,6},{5,7},{6,4},{7,5},{8,10},{9,11},{10,... | collective-permute-start | bytes 221192 | tf_op jit(solution)/shard_map/ppermute | solution.py:312
  29.9 0.0 collective-permute-done.10.theirs_ref
  29.9 0.3 merge.6
  30.2 0.5 %collective-permute-start.11 = (s16[2,16,1152]{2,1,0:T(8,128)(2,1)S(1)}, s16[2,16,1152]{2,1,0:T(8,128)(2,1)S(1)}, u32[]{:S(2)}, u32[]{:S(2)}) collective-permute-start(s16[2,16,1152]{2,1,0:T(8,128)(2,1)S(1)} %get-tuple-element.27), channel_id=1, source_target_pairs={{0,2},{1,3},{2,0},{3,1},{4,6},{5,7},{6,4},{7,5},{8,10},{9,11},{10,... | collective-permute-start | bytes 221192 | tf_op jit(solution)/shard_map/ppermute | solution.py:312
  30.7 2.1 %collective-permute-done.7.theirs_ref = s16[2,16,1152]{2,1,0:T(8,128)(2,1)S(1)} collective-permute-done((s16[2,16,1152]{2,1,0:T(8,128)(2,1)S(1)}, s16[2,16,1152]{2,1,0:T(8,128)(2,1)S(1)}, u32[]{:S(2)}, u32[]{:S(2)}) %collective-permute-start.7) | collective-permute-done | bytes 73760 | tf_op jit(solution)/shard_map/ppermute | solution.py:312
  32.8 0.3 merge.5
  33.1 2.8 %collective-permute-start.8 = (s16[16,1152]{1,0:T(8,128)(2,1)S(1)}, s16[16,1152]{1,0:T(8,128)(2,1)S(1)}, u32[]{:S(2)}, u32[]{:S(2)}) collective-permute-start(s16[16,1152]{1,0:T(8,128)(2,1)S(1)} %get-tuple-element.22), channel_id=1, source_target_pairs={{0,12},{4,8},{8,4},{12,0},{1,13},{5,9},{9,5},{13,1},{2,14},{6,10},... | collective-permute-start | bytes 110600 | tf_op jit(solution)/shard_map/ppermute | solution.py:312
  35.9 0.0 collective-permute-start.9
  35.9 0.0 collective-permute-done.11.theirs_ref
  35.9 0.3 merge.7
  36.2 1.7 %collective-permute-start.12 = (s16[16,1152]{1,0:T(8,128)(2,1)S(1)}, s16[16,1152]{1,0:T(8,128)(2,1)S(1)}, u32[]{:S(2)}, u32[]{:S(2)}) collective-permute-start(s16[16,1152]{1,0:T(8,128)(2,1)S(1)} %get-tuple-element.28), channel_id=1, source_target_pairs={{0,4},{4,0},{8,12},{12,8},{1,5},{5,1},{9,13},{13,9},{2,6},{6,2},{1... | collective-permute-start | bytes 110600 | tf_op jit(solution)/shard_map/ppermute | solution.py:312
  37.9 1.1 %collective-permute-done.8.refs_0_ = s16[16,1152]{1,0:T(8,128)(2,1)S(1)} collective-permute-done((s16[16,1152]{1,0:T(8,128)(2,1)S(1)}, s16[16,1152]{1,0:T(8,128)(2,1)S(1)}, u32[]{:S(2)}, u32[]{:S(2)}) %collective-permute-start.8) | collective-permute-done | bytes 36896 | tf_op jit(solution)/shard_map/ppermute | solution.py:312
  38.9 1.8 %collective-permute-done.9.refs_1_ = s16[16,1152]{1,0:T(8,128)(2,1)S(1)} collective-permute-done((s16[16,1152]{1,0:T(8,128)(2,1)S(1)}, s16[16,1152]{1,0:T(8,128)(2,1)S(1)}, u32[]{:S(2)}, u32[]{:S(2)}) %collective-permute-start.9) | collective-permute-done | bytes 36896 | tf_op jit(solution)/shard_map/ppermute | solution.py:312
  40.7 0.0 collective-permute-done.12.refs_2_
  40.7 0.9 %place.1 = (f32[16,4096]{1,0:T(8,128)}, f32[16,32]{1,0:T(8,128)}) custom-call(s16[16,1152]{1,0:T(8,128)(2,1)S(1)} %collective-permute-done.8.refs_0_, s16[16,1152]{1,0:T(8,128)(2,1)S(1)} %collective-permute-done.9.refs_1_, s16[16,1152]{1,0:T(8,128)(2,1)S(1)} %collective-permute-done.12.refs_2_, s16[16,1152]{1,0:T(8,128)(2,1)S(1)} %get-tuple-element.29.refs_3_), custom_call_target="tpu_custom_call" | custom-call | tf_op jit(solution)/shard_map/place/pallas_call | solution.py:300
  (6 shorter events, 0.0 us)
Async XLA Ops:
  1.6 8.9 %collective-permute-start = (bf16[32,1024]{1,0:T(8,128)(2,1)S(1)}, bf16[32,1024]{1,0:T(8,128)(2,1)S(1)}, u32[]{:S(2)}, u32[]{:S(2)}) collective-permute-start(bf16[32,1024]{1,0:T(8,128)(2,1)S(1)} %pad_maximum_fusion), channel_id=1, source_target_pairs={{0,12},{4,8},{8,4},{12,0},{1,13},{5,9},{9,5},{13,1},{2,14},{6,10},... | collective-permute-start | bytes 196616 | tf_op jit(solution)/shard_map/ppermute | solution.py:312
  6.8 5.6 %collective-permute-start.2 = (bf16[32,1024]{1,0:T(8,128)(2,1)S(1)}, bf16[32,1024]{1,0:T(8,128)(2,1)S(1)}, u32[]{:S(2)}, u32[]{:S(2)}) collective-permute-start(bf16[32,1024]{1,0:T(8,128)(2,1)S(1)} %pad_maximum_fusion.1), channel_id=1, source_target_pairs={{0,8},{4,12},{8,0},{12,4},{1,9},{5,13},{9,1},{13,5},{2,10},{6,14},... | collective-permute-start | bytes 196616 | tf_op jit(solution)/shard_map/ppermute | solution.py:312
  6.8 5.6 %collective-permute-start.4 = (bf16[32,1024]{1,0:T(8,128)(2,1)S(1)}, bf16[32,1024]{1,0:T(8,128)(2,1)S(1)}, u32[]{:S(2)}, u32[]{:S(2)}) collective-permute-start(bf16[32,1024]{1,0:T(8,128)(2,1)S(1)} %pad_maximum_fusion.2), channel_id=1, source_target_pairs={{0,4},{4,0},{8,12},{12,8},{1,5},{5,1},{9,13},{13,9},{2,6},{6,2},{1... | collective-permute-start | bytes 196616 | tf_op jit(solution)/shard_map/ppermute | solution.py:312
  10.5 2.4 %collective-permute-start.1 = (bf16[32,1024]{1,0:T(8,128)(2,1)S(1)}, bf16[32,1024]{1,0:T(8,128)(2,1)S(1)}, u32[]{:S(2)}, u32[]{:S(2)}) collective-permute-start(bf16[32,1024]{1,0:T(8,128)(2,1)S(1)} %collective-permute-done.refs_4_), channel_id=1, source_target_pairs={{0,1},{1,0},{2,3},{3,2},{4,5},{5,4},{6,7},{7,6},{8,9},{9,8},{10,11... | collective-permute-start | bytes 196616 | tf_op jit(solution)/shard_map/ppermute | solution.py:312
  12.4 1.3 %collective-permute-start.3 = (bf16[32,1024]{1,0:T(8,128)(2,1)S(1)}, bf16[32,1024]{1,0:T(8,128)(2,1)S(1)}, u32[]{:S(2)}, u32[]{:S(2)}) collective-permute-start(bf16[32,1024]{1,0:T(8,128)(2,1)S(1)} %collective-permute-done.2.refs_5_), channel_id=1, source_target_pairs={{0,1},{1,0},{2,3},{3,2},{4,5},{5,4},{6,7},{7,6},{8,9},{9,8},{10,11... | collective-permute-start | bytes 196616 | tf_op jit(solution)/shard_map/ppermute | solution.py:312
  12.4 1.4 %collective-permute-start.5 = (bf16[32,1024]{1,0:T(8,128)(2,1)S(1)}, bf16[32,1024]{1,0:T(8,128)(2,1)S(1)}, u32[]{:S(2)}, u32[]{:S(2)}) collective-permute-start(bf16[32,1024]{1,0:T(8,128)(2,1)S(1)} %collective-permute-done.4.refs_6_), channel_id=1, source_target_pairs={{0,1},{1,0},{2,3},{3,2},{4,5},{5,4},{6,7},{7,6},{8,9},{9,8},{10,11... | collective-permute-start | bytes 196616 | tf_op jit(solution)/shard_map/ppermute | solution.py:312
  26.3 1.6 %collective-permute-start.6 = (f32[2,32,1152]{2,1,0:T(8,128)S(1)}, f32[2,32,1152]{2,1,0:T(8,128)S(1)}, u32[]{:S(2)}, u32[]{:S(2)}) collective-permute-start(f32[2,32,1152]{2,1,0:T(8,128)S(1)} %bitcast.10), channel_id=1, source_target_pairs={{0,1},{1,0},{2,3},{3,2},{4,5},{5,4},{6,7},{7,6},{8,9},{9,8},{10,11... | collective-permute-start | bytes 884744 | tf_op jit(solution)/shard_map/ppermute | solution.py:312
  26.7 3.2 %collective-permute-start.10 = (f32[2,32,1152]{2,1,0:T(8,128)S(1)}, f32[2,32,1152]{2,1,0:T(8,128)S(1)}, u32[]{:S(2)}, u32[]{:S(2)}) collective-permute-start(f32[2,32,1152]{2,1,0:T(8,128)S(1)} %bitcast.9), channel_id=1, source_target_pairs={{0,1},{1,0},{2,3},{3,2},{4,5},{5,4},{6,7},{7,6},{8,9},{9,8},{10,11... | collective-permute-start | bytes 884744 | tf_op jit(solution)/shard_map/ppermute | solution.py:312
  28.2 4.6 %collective-permute-start.7 = (s16[2,16,1152]{2,1,0:T(8,128)(2,1)S(1)}, s16[2,16,1152]{2,1,0:T(8,128)(2,1)S(1)}, u32[]{:S(2)}, u32[]{:S(2)}) collective-permute-start(s16[2,16,1152]{2,1,0:T(8,128)(2,1)S(1)} %get-tuple-element.21), channel_id=1, source_target_pairs={{0,2},{1,3},{2,0},{3,1},{4,6},{5,7},{6,4},{7,5},{8,10},{9,11},{10,... | collective-permute-start | bytes 221192 | tf_op jit(solution)/shard_map/ppermute | solution.py:312
  30.2 5.7 %collective-permute-start.11 = (s16[2,16,1152]{2,1,0:T(8,128)(2,1)S(1)}, s16[2,16,1152]{2,1,0:T(8,128)(2,1)S(1)}, u32[]{:S(2)}, u32[]{:S(2)}) collective-permute-start(s16[2,16,1152]{2,1,0:T(8,128)(2,1)S(1)} %get-tuple-element.27), channel_id=1, source_target_pairs={{0,2},{1,3},{2,0},{3,1},{4,6},{5,7},{6,4},{7,5},{8,10},{9,11},{10,... | collective-permute-start | bytes 221192 | tf_op jit(solution)/shard_map/ppermute | solution.py:312
  33.1 5.8 %collective-permute-start.8 = (s16[16,1152]{1,0:T(8,128)(2,1)S(1)}, s16[16,1152]{1,0:T(8,128)(2,1)S(1)}, u32[]{:S(2)}, u32[]{:S(2)}) collective-permute-start(s16[16,1152]{1,0:T(8,128)(2,1)S(1)} %get-tuple-element.22), channel_id=1, source_target_pairs={{0,12},{4,8},{8,4},{12,0},{1,13},{5,9},{9,5},{13,1},{2,14},{6,10},... | collective-permute-start | bytes 110600 | tf_op jit(solution)/shard_map/ppermute | solution.py:312
  35.9 4.9 %collective-permute-start.9 = (s16[16,1152]{1,0:T(8,128)(2,1)S(1)}, s16[16,1152]{1,0:T(8,128)(2,1)S(1)}, u32[]{:S(2)}, u32[]{:S(2)}) collective-permute-start(s16[16,1152]{1,0:T(8,128)(2,1)S(1)} %get-tuple-element.23), channel_id=1, source_target_pairs={{0,8},{4,12},{8,0},{12,4},{1,9},{5,13},{9,1},{13,5},{2,10},{6,14},... | collective-permute-start | bytes 110600 | tf_op jit(solution)/shard_map/ppermute | solution.py:312
  36.2 4.6 %collective-permute-start.12 = (s16[16,1152]{1,0:T(8,128)(2,1)S(1)}, s16[16,1152]{1,0:T(8,128)(2,1)S(1)}, u32[]{:S(2)}, u32[]{:S(2)}) collective-permute-start(s16[16,1152]{1,0:T(8,128)(2,1)S(1)} %get-tuple-element.28), channel_id=1, source_target_pairs={{0,4},{4,0},{8,12},{12,8},{1,5},{5,1},{9,13},{13,9},{2,6},{6,2},{1... | collective-permute-start | bytes 110600 | tf_op jit(solution)/shard_map/ppermute | solution.py:312

commit v8 on v7

--- a/solution.py
+++ b/solution.py
@@ -13,7 +13,7 @@
 PAGE = 128
 LANES = 128
 TOK_TILE = 256
-GROUP = 4
+GROUP = 16
 MOST_PERMUTES = 8
 VMEM_LIMIT = 50 * 2**20
 

time: 41.9 us -> 41.9 us (level)
  no operation moved by 1% of the time
where the time goes in v8:
time: 41.9 us; the launch traced here: 41.6 us
  Pallas kernels  16 us (38%)
  starting transfers between devices  13.6 us (32%)
  waiting for transfers between devices  8.73 us (21%)
  between operations  1.43 us (3%)
  local copies, waits for them, and re-layouts  1.02 us (2%)
  other arithmetic  0.81 us (2%)
    ppermute x13, starting transfers between devices, across(): return lax.ppermute(value, axis, [(i, i ^ bit) for i in range(size)])  13.6 us
    pallas_call x1, Pallas kernels, attend(): pl.pallas_call(functools.partial(attend_kernel, len(q_parts), starts), in...  12.4 us
    ppermute x13, waiting for transfers between devices, across(): return lax.ppermute(value, axis, [(i, i ^ bit) for i in range(size)])  8.73 us
    pallas_call x1, Pallas kernels, first_head(): pl.pallas_call(first_kernel, in_specs=[pl.BlockSpec(memory_space=pl.ANY)]...  1.62 us
    pallas_call x4, Pallas kernels, merge(): pl.pallas_call(functools.partial(merge_kernel, heads, last), out_shape=ou...  1.11 us
    dynamic_slice x1, local copies, waits for them, and re-layouts, pick(): lax.dynamic_slice(queries, ((cache_at ^ name) * share, at), (share, width))  0.95 us
    pallas_call x1, Pallas kernels, place(): pl.pallas_call(functools.partial(place_kernel, heads, axis, names), out_s...  0.94 us
  transfers between devices with their start and end apart: 13, of which 7 were waited for; matrix products, arithmetic and copies ran while one was open for 2% of the time, Pallas kernels for 7%

profile of v8, /device:TPU:0, one launch (start us, length us, event | category | flops | bytes accessed | tf_op | source)
XLA Modules:
  0.0 41.6 jit_solution(12954870740072563404)
XLA Ops:
  0.7 0.9 %fusion.2 = (bf16[16,1024]{1,0:T(8,128)(2,1)S(1)}, bf16[16,1024]{1,0:T(8,128)(2,1)S(1)}, bf16[16,1024]{1,0:T(8,128)(2,1)S(1)}, bf16[16,1024]{1,0:T(8,128)(2,1)S(...) fusion(bf16[64,4096]{1,0:T(8,128)(2,1)} %param.5, ...), kind=kLoop, calls=%fused_computation.10 | loop fusion | bytes 655392 | tf_op jit(solution)/shard_map/dynamic_slice | solution.py:340
  1.6 5.1 %collective-permute-start = (bf16[32,1024]{1,0:T(8,128)(2,1)S(1)}, bf16[32,1024]{1,0:T(8,128)(2,1)S(1)}, u32[]{:S(2)}, u32[]{:S(2)}) collective-permute-start(bf16[32,1024]{1,0:T(8,128)(2,1)S(1)} %pad_maximum_fusion), channel_id=1, source_target_pairs={{0,12},{4,8},{8,4},{12,0},{1,13},{5,9},{9,5},{13,1},{2,14},{6,10},... | collective-permute-start | bytes 196616 | tf_op jit(solution)/shard_map/ppermute | solution.py:312
  6.8 0.0 collective-permute-start.2
  6.8 0.6 %collective-permute-start.4 = (bf16[32,1024]{1,0:T(8,128)(2,1)S(1)}, bf16[32,1024]{1,0:T(8,128)(2,1)S(1)}, u32[]{:S(2)}, u32[]{:S(2)}) collective-permute-start(bf16[32,1024]{1,0:T(8,128)(2,1)S(1)} %pad_maximum_fusion.2), channel_id=1, source_target_pairs={{0,4},{4,0},{8,12},{12,8},{1,5},{5,1},{9,13},{13,9},{2,6},{6,2},{1... | collective-permute-start | bytes 196616 | tf_op jit(solution)/shard_map/ppermute | solution.py:312
  8.1 0.8 %fusion.1 = pred[32]{0:T(512)(128)(4,1)S(1)} fusion(s32[32]{0:T(128)} %bitcast.11, pred[32]{0:T(512)(128)(4,1)S(1)} %iota_compare_fusion.1), kind=kLoop, calls=%fused_computation.7 | loop fusion | flops 3040 | bytes 192 | tf_op jit(solution)/shard_map/reduce_or | solution.py:318
  8.9 1.6 %first_head.1 = (bf16[32,128,128]{2,1,0:T(8,128)(2,1)S(1)}, bf16[32,128,128]{2,1,0:T(8,128)(2,1)S(1)}) custom-call(bf16[32,128,1024]{2,1,0:T(8,128)(2,1)} %refs_8_.1, bf16[32,128,1024]{2,1,0:T(8,128)(2,1)} %refs_9_.1), custom_call_target="tpu_custom_call" | custom-call | tf_op jit(solution)/shard_map/first_head/pallas_call | solution.py:138
  10.5 0.0 collective-permute-done.refs_4_
  10.5 0.1 collective-permute-start.1
  10.6 1.8 %collective-permute-done.2.refs_5_ = bf16[32,1024]{1,0:T(8,128)(2,1)S(1)} collective-permute-done((bf16[32,1024]{1,0:T(8,128)(2,1)S(1)}, bf16[32,1024]{1,0:T(8,128)(2,1)S(1)}, u32[]{:S(2)}, u32[]{:S(2)}) %collective-permute-start.2) | collective-permute-done | bytes 65568 | tf_op jit(solution)/shard_map/ppermute | solution.py:312
  12.4 0.0 collective-permute-start.3
  12.4 0.0 collective-permute-done.4.refs_6_
  12.4 0.5 %collective-permute-start.5 = (bf16[32,1024]{1,0:T(8,128)(2,1)S(1)}, bf16[32,1024]{1,0:T(8,128)(2,1)S(1)}, u32[]{:S(2)}, u32[]{:S(2)}) collective-permute-start(bf16[32,1024]{1,0:T(8,128)(2,1)S(1)} %collective-permute-done.4.refs_6_), channel_id=1, source_target_pairs={{0,1},{1,0},{2,3},{3,2},{4,5},{5,4},{6,7},{7,6},{8,9},{9,8},{10,11... | collective-permute-start | bytes 196616 | tf_op jit(solution)/shard_map/ppermute | solution.py:312
  12.9 0.0 collective-permute-done.1.refs_0_
  12.9 0.7 %collective-permute-done.3.refs_1_ = bf16[32,1024]{1,0:T(8,128)(2,1)S(1)} collective-permute-done((bf16[32,1024]{1,0:T(8,128)(2,1)S(1)}, bf16[32,1024]{1,0:T(8,128)(2,1)S(1)}, u32[]{:S(2)}, u32[]{:S(2)}) %collective-permute-start.3) | collective-permute-done | bytes 65568 | tf_op jit(solution)/shard_map/ppermute | solution.py:312
  13.6 0.2 collective-permute-done.5.refs_2_
  13.8 0.1 broadcast_in_dim.18.limits_ref
  13.8 12.4 %attend.1 = (f32[64,1152]{1,0:T(8,128)S(1)}, f32[64,1152]{1,0:T(8,128)S(1)}, f32[64,1152]{1,0:T(8,128)S(1)}, f32[64,1152]{1,0:T(8,128)S(1)}) custom-call(f32[32,256]{1,0:T(8,128)S(1)} %broadcast_in_dim.18.limits_ref, bf16[32,1024]{1,0:T(8,128)(2,1)S(1)} %collective-permute-done.1.refs_0_, bf16[32,1024]{1,0:T(8,128)(2,1)S(1)} %collective-permute-done.3.refs_1_, ...), custom_call_target="tpu_custom_call" | custom-call | tf_op jit(solution)/shard_map/attend/pallas_call | solution.py:159
  26.2 0.4 collective-permute-start.6
  26.6 0.2 collective-permute-start.10
  26.8 1.1 %collective-permute-done.6.theirs_ref = f32[2,32,1152]{2,1,0:T(8,128)S(1)} collective-permute-done((f32[2,32,1152]{2,1,0:T(8,128)S(1)}, f32[2,32,1152]{2,1,0:T(8,128)S(1)}, u32[]{:S(2)}, u32[]{:S(2)}) %collective-permute-start.6) | collective-permute-done | bytes 294944 | tf_op jit(solution)/shard_map/ppermute | solution.py:312
  27.9 0.3 merge.4
  28.2 1.7 %collective-permute-start.7 = (s16[2,16,1152]{2,1,0:T(8,128)(2,1)S(1)}, s16[2,16,1152]{2,1,0:T(8,128)(2,1)S(1)}, u32[]{:S(2)}, u32[]{:S(2)}) collective-permute-start(s16[2,16,1152]{2,1,0:T(8,128)(2,1)S(1)} %get-tuple-element.21), channel_id=1, source_target_pairs={{0,2},{1,3},{2,0},{3,1},{4,6},{5,7},{6,4},{7,5},{8,10},{9,11},{10,... | collective-permute-start | bytes 221192 | tf_op jit(solution)/shard_map/ppermute | solution.py:312
  29.8 0.0 collective-permute-done.10.theirs_ref
  29.8 0.3 merge.6
  30.1 0.5 %collective-permute-start.11 = (s16[2,16,1152]{2,1,0:T(8,128)(2,1)S(1)}, s16[2,16,1152]{2,1,0:T(8,128)(2,1)S(1)}, u32[]{:S(2)}, u32[]{:S(2)}) collective-permute-start(s16[2,16,1152]{2,1,0:T(8,128)(2,1)S(1)} %get-tuple-element.27), channel_id=1, source_target_pairs={{0,2},{1,3},{2,0},{3,1},{4,6},{5,7},{6,4},{7,5},{8,10},{9,11},{10,... | collective-permute-start | bytes 221192 | tf_op jit(solution)/shard_map/ppermute | solution.py:312
  30.6 2.1 %collective-permute-done.7.theirs_ref = s16[2,16,1152]{2,1,0:T(8,128)(2,1)S(1)} collective-permute-done((s16[2,16,1152]{2,1,0:T(8,128)(2,1)S(1)}, s16[2,16,1152]{2,1,0:T(8,128)(2,1)S(1)}, u32[]{:S(2)}, u32[]{:S(2)}) %collective-permute-start.7) | collective-permute-done | bytes 73760 | tf_op jit(solution)/shard_map/ppermute | solution.py:312
  32.7 0.3 merge.5
  33.0 2.8 %collective-permute-start.8 = (s16[16,1152]{1,0:T(8,128)(2,1)S(1)}, s16[16,1152]{1,0:T(8,128)(2,1)S(1)}, u32[]{:S(2)}, u32[]{:S(2)}) collective-permute-start(s16[16,1152]{1,0:T(8,128)(2,1)S(1)} %get-tuple-element.22), channel_id=1, source_target_pairs={{0,12},{4,8},{8,4},{12,0},{1,13},{5,9},{9,5},{13,1},{2,14},{6,10},... | collective-permute-start | bytes 110600 | tf_op jit(solution)/shard_map/ppermute | solution.py:312
  35.8 0.0 collective-permute-start.9
  35.8 0.0 collective-permute-done.11.theirs_ref
  35.8 0.3 merge.7
  36.1 1.7 %collective-permute-start.12 = (s16[16,1152]{1,0:T(8,128)(2,1)S(1)}, s16[16,1152]{1,0:T(8,128)(2,1)S(1)}, u32[]{:S(2)}, u32[]{:S(2)}) collective-permute-start(s16[16,1152]{1,0:T(8,128)(2,1)S(1)} %get-tuple-element.28), channel_id=1, source_target_pairs={{0,4},{4,0},{8,12},{12,8},{1,5},{5,1},{9,13},{13,9},{2,6},{6,2},{1... | collective-permute-start | bytes 110600 | tf_op jit(solution)/shard_map/ppermute | solution.py:312
  37.8 1.1 %collective-permute-done.8.refs_0_ = s16[16,1152]{1,0:T(8,128)(2,1)S(1)} collective-permute-done((s16[16,1152]{1,0:T(8,128)(2,1)S(1)}, s16[16,1152]{1,0:T(8,128)(2,1)S(1)}, u32[]{:S(2)}, u32[]{:S(2)}) %collective-permute-start.8) | collective-permute-done | bytes 36896 | tf_op jit(solution)/shard_map/ppermute | solution.py:312
  38.9 1.8 %collective-permute-done.9.refs_1_ = s16[16,1152]{1,0:T(8,128)(2,1)S(1)} collective-permute-done((s16[16,1152]{1,0:T(8,128)(2,1)S(1)}, s16[16,1152]{1,0:T(8,128)(2,1)S(1)}, u32[]{:S(2)}, u32[]{:S(2)}) %collective-permute-start.9) | collective-permute-done | bytes 36896 | tf_op jit(solution)/shard_map/ppermute | solution.py:312
  40.7 0.0 collective-permute-done.12.refs_2_
  40.7 0.9 %place.1 = (f32[16,4096]{1,0:T(8,128)}, f32[16,32]{1,0:T(8,128)}) custom-call(s16[16,1152]{1,0:T(8,128)(2,1)S(1)} %collective-permute-done.8.refs_0_, s16[16,1152]{1,0:T(8,128)(2,1)S(1)} %collective-permute-done.9.refs_1_, s16[16,1152]{1,0:T(8,128)(2,1)S(1)} %collective-permute-done.12.refs_2_, s16[16,1152]{1,0:T(8,128)(2,1)S(1)} %get-tuple-element.29.refs_3_), custom_call_target="tpu_custom_call" | custom-call | tf_op jit(solution)/shard_map/place/pallas_call | solution.py:300
  (6 shorter events, 0.0 us)
Async XLA Ops:
  1.6 8.9 %collective-permute-start = (bf16[32,1024]{1,0:T(8,128)(2,1)S(1)}, bf16[32,1024]{1,0:T(8,128)(2,1)S(1)}, u32[]{:S(2)}, u32[]{:S(2)}) collective-permute-start(bf16[32,1024]{1,0:T(8,128)(2,1)S(1)} %pad_maximum_fusion), channel_id=1, source_target_pairs={{0,12},{4,8},{8,4},{12,0},{1,13},{5,9},{9,5},{13,1},{2,14},{6,10},... | collective-permute-start | bytes 196616 | tf_op jit(solution)/shard_map/ppermute | solution.py:312
  6.8 5.6 %collective-permute-start.2 = (bf16[32,1024]{1,0:T(8,128)(2,1)S(1)}, bf16[32,1024]{1,0:T(8,128)(2,1)S(1)}, u32[]{:S(2)}, u32[]{:S(2)}) collective-permute-start(bf16[32,1024]{1,0:T(8,128)(2,1)S(1)} %pad_maximum_fusion.1), channel_id=1, source_target_pairs={{0,8},{4,12},{8,0},{12,4},{1,9},{5,13},{9,1},{13,5},{2,10},{6,14},... | collective-permute-start | bytes 196616 | tf_op jit(solution)/shard_map/ppermute | solution.py:312
  6.8 5.6 %collective-permute-start.4 = (bf16[32,1024]{1,0:T(8,128)(2,1)S(1)}, bf16[32,1024]{1,0:T(8,128)(2,1)S(1)}, u32[]{:S(2)}, u32[]{:S(2)}) collective-permute-start(bf16[32,1024]{1,0:T(8,128)(2,1)S(1)} %pad_maximum_fusion.2), channel_id=1, source_target_pairs={{0,4},{4,0},{8,12},{12,8},{1,5},{5,1},{9,13},{13,9},{2,6},{6,2},{1... | collective-permute-start | bytes 196616 | tf_op jit(solution)/shard_map/ppermute | solution.py:312
  10.5 2.4 %collective-permute-start.1 = (bf16[32,1024]{1,0:T(8,128)(2,1)S(1)}, bf16[32,1024]{1,0:T(8,128)(2,1)S(1)}, u32[]{:S(2)}, u32[]{:S(2)}) collective-permute-start(bf16[32,1024]{1,0:T(8,128)(2,1)S(1)} %collective-permute-done.refs_4_), channel_id=1, source_target_pairs={{0,1},{1,0},{2,3},{3,2},{4,5},{5,4},{6,7},{7,6},{8,9},{9,8},{10,11... | collective-permute-start | bytes 196616 | tf_op jit(solution)/shard_map/ppermute | solution.py:312
  12.4 1.3 %collective-permute-start.3 = (bf16[32,1024]{1,0:T(8,128)(2,1)S(1)}, bf16[32,1024]{1,0:T(8,128)(2,1)S(1)}, u32[]{:S(2)}, u32[]{:S(2)}) collective-permute-start(bf16[32,1024]{1,0:T(8,128)(2,1)S(1)} %collective-permute-done.2.refs_5_), channel_id=1, source_target_pairs={{0,1},{1,0},{2,3},{3,2},{4,5},{5,4},{6,7},{7,6},{8,9},{9,8},{10,11... | collective-permute-start | bytes 196616 | tf_op jit(solution)/shard_map/ppermute | solution.py:312
  12.4 1.4 %collective-permute-start.5 = (bf16[32,1024]{1,0:T(8,128)(2,1)S(1)}, bf16[32,1024]{1,0:T(8,128)(2,1)S(1)}, u32[]{:S(2)}, u32[]{:S(2)}) collective-permute-start(bf16[32,1024]{1,0:T(8,128)(2,1)S(1)} %collective-permute-done.4.refs_6_), channel_id=1, source_target_pairs={{0,1},{1,0},{2,3},{3,2},{4,5},{5,4},{6,7},{7,6},{8,9},{9,8},{10,11... | collective-permute-start | bytes 196616 | tf_op jit(solution)/shard_map/ppermute | solution.py:312
  26.2 1.6 %collective-permute-start.6 = (f32[2,32,1152]{2,1,0:T(8,128)S(1)}, f32[2,32,1152]{2,1,0:T(8,128)S(1)}, u32[]{:S(2)}, u32[]{:S(2)}) collective-permute-start(f32[2,32,1152]{2,1,0:T(8,128)S(1)} %bitcast.10), channel_id=1, source_target_pairs={{0,1},{1,0},{2,3},{3,2},{4,5},{5,4},{6,7},{7,6},{8,9},{9,8},{10,11... | collective-permute-start | bytes 884744 | tf_op jit(solution)/shard_map/ppermute | solution.py:312
  26.6 3.2 %collective-permute-start.10 = (f32[2,32,1152]{2,1,0:T(8,128)S(1)}, f32[2,32,1152]{2,1,0:T(8,128)S(1)}, u32[]{:S(2)}, u32[]{:S(2)}) collective-permute-start(f32[2,32,1152]{2,1,0:T(8,128)S(1)} %bitcast.9), channel_id=1, source_target_pairs={{0,1},{1,0},{2,3},{3,2},{4,5},{5,4},{6,7},{7,6},{8,9},{9,8},{10,11... | collective-permute-start | bytes 884744 | tf_op jit(solution)/shard_map/ppermute | solution.py:312
  28.2 4.6 %collective-permute-start.7 = (s16[2,16,1152]{2,1,0:T(8,128)(2,1)S(1)}, s16[2,16,1152]{2,1,0:T(8,128)(2,1)S(1)}, u32[]{:S(2)}, u32[]{:S(2)}) collective-permute-start(s16[2,16,1152]{2,1,0:T(8,128)(2,1)S(1)} %get-tuple-element.21), channel_id=1, source_target_pairs={{0,2},{1,3},{2,0},{3,1},{4,6},{5,7},{6,4},{7,5},{8,10},{9,11},{10,... | collective-permute-start | bytes 221192 | tf_op jit(solution)/shard_map/ppermute | solution.py:312
  30.1 5.7 %collective-permute-start.11 = (s16[2,16,1152]{2,1,0:T(8,128)(2,1)S(1)}, s16[2,16,1152]{2,1,0:T(8,128)(2,1)S(1)}, u32[]{:S(2)}, u32[]{:S(2)}) collective-permute-start(s16[2,16,1152]{2,1,0:T(8,128)(2,1)S(1)} %get-tuple-element.27), channel_id=1, source_target_pairs={{0,2},{1,3},{2,0},{3,1},{4,6},{5,7},{6,4},{7,5},{8,10},{9,11},{10,... | collective-permute-start | bytes 221192 | tf_op jit(solution)/shard_map/ppermute | solution.py:312
  33.0 5.8 %collective-permute-start.8 = (s16[16,1152]{1,0:T(8,128)(2,1)S(1)}, s16[16,1152]{1,0:T(8,128)(2,1)S(1)}, u32[]{:S(2)}, u32[]{:S(2)}) collective-permute-start(s16[16,1152]{1,0:T(8,128)(2,1)S(1)} %get-tuple-element.22), channel_id=1, source_target_pairs={{0,12},{4,8},{8,4},{12,0},{1,13},{5,9},{9,5},{13,1},{2,14},{6,10},... | collective-permute-start | bytes 110600 | tf_op jit(solution)/shard_map/ppermute | solution.py:312
  35.8 4.9 %collective-permute-start.9 = (s16[16,1152]{1,0:T(8,128)(2,1)S(1)}, s16[16,1152]{1,0:T(8,128)(2,1)S(1)}, u32[]{:S(2)}, u32[]{:S(2)}) collective-permute-start(s16[16,1152]{1,0:T(8,128)(2,1)S(1)} %get-tuple-element.23), channel_id=1, source_target_pairs={{0,8},{4,12},{8,0},{12,4},{1,9},{5,13},{9,1},{13,5},{2,10},{6,14},... | collective-permute-start | bytes 110600 | tf_op jit(solution)/shard_map/ppermute | solution.py:312
  36.1 4.6 %collective-permute-start.12 = (s16[16,1152]{1,0:T(8,128)(2,1)S(1)}, s16[16,1152]{1,0:T(8,128)(2,1)S(1)}, u32[]{:S(2)}, u32[]{:S(2)}) collective-permute-start(s16[16,1152]{1,0:T(8,128)(2,1)S(1)} %get-tuple-element.28), channel_id=1, source_target_pairs={{0,4},{4,0},{8,12},{12,8},{1,5},{5,1},{9,13},{13,9},{2,6},{6,2},{1... | collective-permute-start | bytes 110600 | tf_op jit(solution)/shard_map/ppermute | solution.py:312
